TPU v7x, 256 devices: a whole 4x4x8 slice. The times are simulated.
256 devices in a mesh: dp: 8 (over x_lo, y), fsdp: 32 (over x_hi, z, core).
Axes of the slice: x: 4 (x_hi: 2, x_lo: 2; x = x_hi * 2 + x_lo), y: 4, z: 8, core: 2. Of those that a mesh axis runs over, the one named last changes fastest.
Arguments:
- layer_input: bfloat16 [65536, 8192], P(('dp', 'fsdp')), may hold values from -6 to 6
- value_grad: bfloat16 [65536, 1024], P(('dp', 'fsdp')), may hold values from -6 to 6
- base_weight_t: bfloat16 [1024, 8192], P('fsdp'), may hold values from -0.1875 to 0.1875
- adapter_down: bfloat16 [8192, 64], replicated, may hold values from -0.0625 to 0.0625
- adapter_up: bfloat16 [64, 1024], replicated, may hold values from -0.75 to 0.75
Outputs:
- input_gradient: bfloat16 [65536, 8192], P(('dp', 'fsdp'))
- down_grad: float32 [8192, 64], replicated
- up_grad: float32 [64, 1024], replicated
All inputs are finite; a program needn't handle non-finite values.
Results may differ from a plain program's by a relative error of at most 0.0034.
Values may be sent and summed in bfloat16 or wider, within the bound.
No kernel may reach another device: no remote copies, remote signals or barrier semaphores. Data moves between devices by JAX's collectives and lax.ppermute only.
A program may use at most 128 MiB of HBM per device.

v0:
```python
import math

import jax
import jax.numpy as jnp
from jax import lax
from jax.sharding import PartitionSpec as P

adapter_scale = 2.0


def local(layer_input, value_grad, base_weight_t, adapter_down, adapter_up):
    token_total_rows = layer_input.shape[0] * lax.axis_size("dp") * lax.axis_size("fsdp")
    adapter_factor = adapter_scale / math.sqrt(token_total_rows)
    projected = jnp.dot(layer_input, adapter_down, preferred_element_type=jnp.float32).astype(
        jnp.bfloat16
    )
    pulled = jnp.dot(value_grad, adapter_up.T, preferred_element_type=jnp.float32).astype(
        jnp.bfloat16
    )
    part_up = adapter_factor * jnp.dot(projected.T, value_grad, preferred_element_type=jnp.float32)
    part_down = adapter_factor * jnp.dot(layer_input.T, pulled, preferred_element_type=jnp.float32)
    down_grad, up_grad = lax.psum((part_down, part_up), ("dp", "fsdp"))
    adapter_extra = jnp.dot(pulled, adapter_down.T, preferred_element_type=jnp.float32)
    whole_weight = lax.all_gather(base_weight_t, "fsdp", axis=0, tiled=True)
    frozen_weight = jnp.dot(value_grad, whole_weight, preferred_element_type=jnp.float32)
    input_gradient = (frozen_weight + adapter_scale * adapter_extra).astype(jnp.bfloat16)
    return (input_gradient, down_grad, up_grad)


def solution(mesh):
    return jax.shard_map(
        local,
        mesh=mesh,
        in_specs=(P(("dp", "fsdp"), None), P(("dp", "fsdp"), None), P("fsdp", None), P(), P()),
        out_specs=(P(("dp", "fsdp"), None), P(), P()),
        check_vma=False,
    )
```

profile of v0, /device:TPU:1, one launch (start us, length us, event | category | flops | bytes accessed | tf_op | source)
XLA Modules:
  0.0 345.1 jit_solution(16468796343925419166)
XLA Ops:
  8.0 0.0 copy-start
  8.0 0.0 copy-start.1
  8.0 0.0 all-gather.2.cloned.1.call-start
  8.1 0.7 all-gather.2.cloned.1.call-update
  8.8 0.0 all-reduce.3.cloned.1.call-start
  8.8 1.3 convolution_convert_fusion.1
  10.2 4.4 %fusion.2 = f32[8192,64]{0,1:T(8,128)} fusion(bf16[256,64]{0,1:T(8,128)(2,1)S(1)} %convolution_convert_fusion.1, bf16[256,8192]{1,0:T(8,128)(2,1)} %param.5), kind=kOutput, calls=%fused_computation.4 | convolution fusion | flops 268959744 | bytes 6324224 | tf_op jit(solution)/shard_map/dot_general | solution.py:21
  14.5 0.0 copy-done
  14.5 0.0 copy-done.1
  14.5 4.5 %convolution_multiply_fusion.2 = f32[64,1024]{1,0:T(8,128)} fusion(bf16[256,1024]{1,0:T(8,128)(2,1)S(1)} %copy-done.1, bf16[256,8192]{1,0:T(8,128)(2,1)} %param.5, bf16[8192,64]{0,1:T(8,128)(2,1)S(1)} %copy-done), kind=kOutput, calls=%fused_computation.5 | convolution fusion | flops 302071808 | bytes 6029312 | tf_op jit(solution)/shard_map/dot_general | solution.py:20
  19.0 0.0 all-reduce.3.cloned.1.call-update
  19.0 135.4 %all-gather.2.cloned.1.call-done = bf16[1024,8192]{1,0:T(8,128)(2,1)} async-done(((bf16[32,8192]{1,0:T(8,128)(2,1)}), bf16[1024,8192]{1,0:T(8,128)(2,1)}) %all-gather.2.cloned.1.call-update) | async-done | bytes 16777232 | tf_op jit(solution)/shard_map/all_gather | solution.py:24
  154.4 8.2 %fusion.3 = f32[256,8192]{1,0:T(8,128)S(1)} fusion(bf16[256,1024]{1,0:T(8,128)(2,1)S(1)} %copy-done.1, bf16[1024,8192]{1,0:T(8,128)(2,1)} %all-gather.2.cloned.1.call-done), kind=kOutput, calls=%fused_computation.8 | convolution fusion | flops 4294967296 | bytes 25690112 | tf_op jit(solution)/shard_map/dot_general | solution.py:25
  162.6 3.3 fusion.1
  165.9 167.9 %all-reduce.3.cloned.1.call-done = (f32[8192,64]{0,1:T(8,128)}, f32[64,1024]{1,0:T(8,128)}) async-done(((f32[8192,64]{0,1:T(8,128)}, f32[64,1024]{1,0:T(8,128)}), (f32[8192,64]{0,1:T(8,128)}, f32[64,1024]{1,0:T(8,128)})) %all-reduce.3.cloned.1.call-update) | async-done | bytes 2359312 | tf_op jit(solution)/shard_map/psum | solution.py:22
  333.8 0.0 copy-start.2
  333.8 3.1 copy.10
  336.9 0.0 copy-done.2
  336.9 0.7 copy.11
Async XLA Ops:
  8.0 6.5 %copy-start = (bf16[8192,64]{0,1:T(8,128)(2,1)S(1)}, bf16[8192,64]{0,1:T(8,128)(2,1)}, u32[]{:S(2)}) copy-start(bf16[8192,64]{0,1:T(8,128)(2,1)} %param.8) | copy-start | bytes 3145732
  8.0 6.5 %copy-start.1 = (bf16[256,1024]{1,0:T(8,128)(2,1)S(1)}, bf16[256,1024]{1,0:T(8,128)(2,1)}, u32[]{:S(2)}) copy-start(bf16[256,1024]{1,0:T(8,128)(2,1)} %param.6) | copy-start | bytes 1572868
  8.0 146.4 %all-gather.2.cloned.1.call-start = ((), (), s32[]{:S(2)}) async-start(), calls=%async_computation | async-start | bytes 17301504 | tf_op jit(solution)/shard_map/all_gather | solution.py:24
  8.8 325.1 %all-reduce.3.cloned.1.call-start = ((), (), s32[]{:S(2)}) async-start(), calls=%async_computation.1 | async-start | bytes 4718592 | tf_op jit(solution)/shard_map/psum | solution.py:22
  333.8 3.1 copy-start.2
Sparse Core Ops, SparseCore 0:
  11.6 142.7 all-gather.1
Sparse Core Ops, SparseCore 1:
  19.1 314.7 all-reduce.2
where the time goes:
time: 346 us; the launch traced here: 345 us
  waiting for transfers between devices  304 us (88%)
  matrix products  21.6 us (6%)
  between operations  15.5 us (4%)
  local copies, waits for them, and re-layouts  3.82 us (1%)
    psum x1, waiting for transfers between devices, local(): down_grad, up_grad = lax.psum((part_down, part_up), ('dp', 'fsdp'))  168 us
    all_gather x1, waiting for transfers between devices, local(): whole_weight = lax.all_gather(base_weight_t, 'fsdp', axis=0, tiled=True)  135 us
    dot_general x1, matrix products, local(): jnp.dot(value_grad, whole_weight, preferred_element_type=jnp.float32)  8.17 us
  transfers between devices with their start and end apart: 2, of which 2 were waited for; matrix products, arithmetic and copies ran while one was open for 6% of the time, Pallas kernels for 0%

commit v1 on v0

v1 whole, which is shorter than its diff:
```python
import functools
import math

import jax
import jax.numpy as jnp
from jax import lax
from jax.experimental import pallas as pl
from jax.experimental.pallas import tpu as pltpu
from jax.sharding import Mesh
from jax.sharding import PartitionSpec as P

adapter_scale = 2.0
AXES = ("x_lo", "y", "x_hi", "z", "core")
SIZES = (2, 4, 2, 8, 2)
HALF = 4096
ZCOLS = 2560
YQ = 384
f32, bf16 = jnp.float32, jnp.bfloat16


def shift(x, axis, k):
    n = SIZES[AXES.index(axis)]
    return lax.ppermute(x, axis, [(i, (i + k) % n) for i in range(n)])


def flip(x, axis, k):
    n = SIZES[AXES.index(axis)]
    return lax.ppermute(x, axis, [(i, i ^ k) for i in range(n)])


def shift_x(x, k):
    place = lambda at: (at % 2) * 2 + at // 2
    return lax.ppermute(x, ("x_lo", "x_hi"), [(place(i), place((i + k) % 4)) for i in range(4)])


def cross_x(x):
    return lax.ppermute(x, ("x_lo", "x_hi"), [(0, 3), (3, 0), (1, 2), (2, 1)])


def product_kernel(x_ref, w_ref, p_ref, d_ref, own_ref, other_ref):
    total = jnp.dot(x_ref[...], w_ref[...], preferred_element_type=f32)
    total += lax.dot_general(
        p_ref[...], d_ref[...], (((1,), (1,)), ((), ())), preferred_element_type=f32
    )
    total = total.astype(bf16)
    rows = own_ref.shape[0]
    own_ref[...] = total[:rows]
    other_ref[...] = total[rows:]


def product(x, w, p, d, step):
    tokens, depth = x.shape
    n = d.shape[0]
    if w.ndim == 2:
        w_spec = pl.BlockSpec((depth, step), lambda i: (0, i))
    else:
        w_spec = pl.BlockSpec((None, depth, step), lambda i: (i, 0, 0))
    out = jax.ShapeDtypeStruct((tokens // 2, n), bf16)
    out_spec = pl.BlockSpec((tokens // 2, step), lambda i: (0, i))
    return pl.pallas_call(
        product_kernel,
        grid=(n // step,),
        in_specs=[
            pl.BlockSpec((tokens, depth), lambda i: (0, 0)),
            w_spec,
            pl.BlockSpec((tokens, p.shape[1]), lambda i: (0, 0)),
            pl.BlockSpec((step, d.shape[1]), lambda i: (i, 0)),
        ],
        out_specs=[out_spec, out_spec],
        out_shape=[out, out],
        compiler_params=pltpu.CompilerParams(vmem_limit_bytes=32 * 2**20),
        cost_estimate=pl.CostEstimate(
            flops=2 * tokens * depth * n, bytes_accessed=2 * depth * n + 2 * tokens * n, transcendentals=0
        ),
    )(x, w, p, d)


def adapter_kernel(li_ref, down_ref, vg_ref, pulled_ref, down_part_ref, up_part_ref, proj, *, factor):
    i = pl.program_id(0)

    @pl.when(i == 0)
    def _():
        proj[...] = jnp.zeros_like(proj)

    li = li_ref[...]
    proj[...] += jnp.dot(li, down_ref[...], preferred_element_type=f32)
    down_part_ref[...] = factor * lax.dot_general(
        pulled_ref[...], li, (((0,), (0,)), ((), ())), preferred_element_type=f32
    )

    @pl.when(i == pl.num_programs(0) - 1)
    def _():
        up_part_ref[...] = factor * lax.dot_general(
            proj[...].astype(bf16), vg_ref[...], (((0,), (0,)), ((), ())), preferred_element_type=f32
        )


def adapter_parts(li, down, vg, pulled, factor, step=1024):
    tokens, width = li.shape
    rank = down.shape[1]
    features = vg.shape[1]
    return pl.pallas_call(
        functools.partial(adapter_kernel, factor=factor),
        grid=(width // step,),
        in_specs=[
            pl.BlockSpec((tokens, step), lambda i: (0, i)),
            pl.BlockSpec((step, rank), lambda i: (i, 0)),
            pl.BlockSpec((tokens, features), lambda i: (0, 0)),
            pl.BlockSpec((tokens, rank), lambda i: (0, 0)),
        ],
        out_specs=[
            pl.BlockSpec((rank, step), lambda i: (0, i)),
            pl.BlockSpec((rank, features), lambda i: (0, 0)),
        ],
        out_shape=[
            jax.ShapeDtypeStruct((rank, width), f32),
            jax.ShapeDtypeStruct((rank, features), f32),
        ],
        scratch_shapes=[pltpu.VMEM((tokens, rank), f32)],
        compiler_params=pltpu.CompilerParams(vmem_limit_bytes=32 * 2**20),
        cost_estimate=pl.CostEstimate(
            flops=4 * tokens * width * rank, bytes_accessed=2 * tokens * width + 4 * rank * width, transcendentals=0
        ),
    )(li, down, vg, pulled)


def pair(first_is_mine, mine, other):
    return jnp.where(first_is_mine, jnp.stack([mine, other]), jnp.stack([other, mine]))


def local(layer_input, value_grad, base_weight_t, adapter_down, adapter_up):
    core, y, z = lax.axis_index("core"), lax.axis_index("y"), lax.axis_index("z")
    x_hi = lax.axis_index("x_hi")
    x = 2 * x_hi + lax.axis_index("x_lo")
    tokens = value_grad.shape[0]
    factor = adapter_scale / math.sqrt(tokens * math.prod(SIZES))
    rank, features = adapter_up.shape

    mine = lax.dynamic_slice_in_dim(base_weight_t, core * HALF, HALF, 1)
    give = lax.dynamic_slice_in_dim(base_weight_t, (1 - core) * HALF, HALF, 1)
    chip_rows = pair(core == 0, mine, flip(give, "core", 1)).reshape(-1, HALF)

    quarter = lax.dynamic_slice_in_dim(chip_rows, ZCOLS + YQ * y, YQ, 1)
    line = lax.all_gather(quarter, "z", axis=0, tiled=True)
    both = pair(x_hi == 0, line, cross_x(line)).reshape(-1, YQ)
    weight_y = lax.all_gather(both, "y", axis=0, tiled=False)

    strip = chip_rows[:, :ZCOLS]
    strips = pair(x_hi == 0, strip, cross_x(strip)).reshape(-1, ZCOLS)
    weight_z = lax.all_gather(strips, "z", axis=0, tiled=True)

    pulled = lax.dot_general(
        value_grad, adapter_up, (((1,), (1,)), ((), ())), preferred_element_type=f32
    ).astype(bf16)
    down_part, up_part = adapter_parts(layer_input, adapter_down, value_grad, pulled, factor)

    half_up = features // 2
    halves = jnp.stack(
        [
            jnp.concatenate([down_part[:, :HALF], up_part[:, :half_up]], 1),
            jnp.concatenate([down_part[:, HALF:], up_part[:, half_up:]], 1),
        ]
    )
    keep = lax.dynamic_index_in_dim(halves, core, 0, False)
    total = keep + flip(lax.dynamic_index_in_dim(halves, 1 - core, 0, False), "core", 1)
    piece = total.shape[1] // 4
    part = lambda k: lax.dynamic_slice_in_dim(total, ((y + k) % 4) * piece, piece, 1)
    total_y = part(0) + shift(part(1), "y", 1) + shift(part(2), "y", 2) + shift(part(3), "y", 3)
    rows = rank // 4
    part_x = lambda k: lax.dynamic_slice_in_dim(total_y, ((x + k) % 4) * rows, rows, 0)
    total_x = part_x(0) + shift_x(part_x(1), 1) + shift_x(part_x(2), 2) + shift_x(part_x(3), 3)
    for k in (1, 2, 4):
        total_x = total_x + flip(total_x, "z", k)
    got = [total_x] + [shift_x(total_x, k) for k in (1, 2, 3)]
    line_x = jnp.zeros((rank, piece), f32)
    for k in range(4):
        line_x = lax.dynamic_update_slice_in_dim(line_x, got[k], ((x - k) % 4) * rows, 0)
    got = [line_x] + [shift(line_x, "y", k) for k in (1, 2, 3)]
    half = jnp.zeros((rank, piece * 4), f32)
    for k in range(4):
        half = lax.dynamic_update_slice_in_dim(half, got[k], ((y - k) % 4) * piece, 1)
    whole = pair(core == 0, half, flip(half, "core", 1))
    down_grad = jnp.concatenate([whole[0, :, :HALF], whole[1, :, :HALF]], 1).T
    up_grad = jnp.concatenate([whole[0, :, HALF:], whole[1, :, HALF:]], 1)

    grads = jnp.concatenate([value_grad, flip(value_grad, "core", 1)], 0)
    pulled_both = lax.dot_general(
        grads, adapter_up, (((1,), (1,)), ((), ())), preferred_element_type=f32
    ).astype(bf16)
    pulled_both = (adapter_scale * pulled_both).astype(bf16)
    down_half = lax.dynamic_slice_in_dim(adapter_down, core * HALF, HALF, 0)
    grads_z = grads.reshape(2 * tokens, 2, 8, -1).transpose(0, 2, 1, 3).reshape(2 * tokens, -1)
    own_z, other_z = product(grads_z, weight_z, pulled_both, down_half[:ZCOLS], 512)
    own_y, other_y = product(grads, weight_y, pulled_both, down_half[ZCOLS:], YQ)
    got_z, got_y = flip(other_z, "core", 1), flip(other_y, "core", 1)
    first = [jnp.where(core == 0, a, b) for a, b in ((own_z, got_z), (own_y, got_y))]
    second = [jnp.where(core == 0, b, a) for a, b in ((own_z, got_z), (own_y, got_y))]
    input_gradient = jnp.concatenate(first + second, 1)
    return (input_gradient, down_grad, up_grad)


def solution(mesh):
    fine = Mesh(mesh.devices.reshape(SIZES), AXES)
    return jax.shard_map(
        local,
        mesh=fine,
        in_specs=(P(AXES, None), P(AXES, None), P(("x_hi", "z", "core"), None), P(), P()),
        out_specs=(P(AXES, None), P(), P()),
        check_vma=False,
    )
```

time: 346 us -> 199 us (0.58)
  waiting for transfers between devices: 304 us -> 57.3 us
  starting transfers between devices: 0.08 us -> 50.7 us
  blocking collectives: 0 us -> 21 us
  local copies, waits for them, and re-layouts: 3.82 us -> 23.6 us
  matrix products: 21.6 us -> 1.93 us
  other arithmetic: 0 us -> 15.5 us
  Pallas kernels: 0 us -> 13.6 us
    psum x1 -> x0, waiting for transfers between devices: 168 us -> none  [local(): down_grad, up_grad = lax.psum((part_down, part_up), ('dp', 'fsdp'))]
    all_gather x1 -> x2, waiting for transfers between devices: 135 us -> 0.01 us  [the longest x1 0.01 us: local(): weight_y = lax.all_gather(both, 'y', axis=0, tiled=False)]
    ppermute x0 -> x23, waiting for transfers between devices: none -> 57.3 us  [the longest x6 25.2 us: shift(): return lax.ppermute(x, axis, [(i, (i + k) % n) for i in range(n)])]
    ppermute x0 -> x23, starting transfers between devices: none -> 50.6 us  [the longest x9 26.5 us: flip(): return lax.ppermute(x, axis, [(i, i ^ k) for i in range(n)])]
    all_gather x0 -> x1, blocking collectives: none -> 21 us  [local(): line = lax.all_gather(quarter, 'z', axis=0, tiled=True)]
    dot_general x5 -> x2, matrix products: 21.6 us -> 1.93 us  [the longest x1 1.65 us: local(): lax.dot_general(grads, adapter_up, (((1,), (1,)), ((), ())), preferred_el...]
    pallas_call x0 -> x3, Pallas kernels: none -> 13.6 us  [the longest x2 10.1 us: product(): pl.pallas_call(product_kernel, grid=(n // step,), in_specs=[pl.BlockSpec(...]
    unnamed x8 -> x24, local copies, waits for them, and re-layouts: 3.82 us -> 11 us
  transfers between devices with their start and end apart: 2 -> 25, of which waited for: 2 -> 18; matrix products, arithmetic and copies ran while one was open for 6% -> 14% of each run, Pallas kernels for 0% -> 7%
where the time goes in v1:
time: 199 us; the launch traced here: 198 us
  waiting for transfers between devices  57.3 us (29%)
  starting transfers between devices  50.7 us (25%)
  local copies, waits for them, and re-layouts  23.6 us (12%)
  blocking collectives  21 us (11%)
  other arithmetic  15.5 us (8%)
  between operations  14.4 us (7%)
  Pallas kernels  13.6 us (7%)
    ppermute x9, starting transfers between devices, flip(): return lax.ppermute(x, axis, [(i, i ^ k) for i in range(n)])  26.5 us
    ppermute x6, waiting for transfers between devices, shift(): return lax.ppermute(x, axis, [(i, (i + k) % n) for i in range(n)])  25.2 us
    all_gather x1, blocking collectives, local(): line = lax.all_gather(quarter, 'z', axis=0, tiled=True)  21 us
    ppermute x2, waiting for transfers between devices, cross_x(): return lax.ppermute(x, ('x_lo', 'x_hi'), [(0, 3), (3, 0), (1, 2), (2, 1)])  13.5 us
    ppermute x9, waiting for transfers between devices, flip(): return lax.ppermute(x, axis, [(i, i ^ k) for i in range(n)])  12.2 us
    ppermute x6, starting transfers between devices, shift(): return lax.ppermute(x, axis, [(i, (i + k) % n) for i in range(n)])  11 us
    unnamed x24, local copies, waits for them, and re-layouts  11 us
    pallas_call x2, Pallas kernels, product(): pl.pallas_call(product_kernel, grid=(n // step,), in_specs=[pl.BlockSpec(...  10.1 us
  transfers between devices with their start and end apart: 25, of which 18 were waited for; matrix products, arithmetic and copies ran while one was open for 14% of the time, Pallas kernels for 7%

profile of v1, /device:TPU:1, one launch (start us, length us, event | category | flops | bytes accessed | tf_op | source)
XLA Modules:
  0.0 198.1 jit_solution(2021901136508216595)
XLA Ops:
  7.2 1.1 dynamic-slice_bitcast_fusion
  8.3 3.3 %collective-permute-start.1 = (bf16[32,4096]{1,0:T(8,128)(2,1)S(1)}, bf16[32,4096]{1,0:T(8,128)(2,1)S(1)}, u32[]{:S(2)}, u32[]{:S(2)}) collective-permute-start(bf16[32,4096]{1,0:T(8,128)(2,1)S(1)} %get-tuple-element.33), channel_id=1, source_target_pairs={{0,1},{1,0},{2,3},{3,2},{4,5},{5,4},{6,7},{7,6},{8,9},{9,8},{10,11... | collective-permute-start | bytes 786440 | tf_op jit(solution)/shard_map/ppermute | solution.py:28
  11.6 1.2 collective-permute-done.1
  12.9 21.0 %all_gather.10 = bf16[512,384]{1,0:T(8,128)(2,1)S(1)} all-gather(bf16[64,384]{1,0:T(8,128)(2,1)S(1)} %constant_dynamic-slice_fusion.7), channel_id=1, replica_groups=mesh['x_lo'=2,'y'=4,'x_hi'=2,'z'=8,'core'=2] {'z'}, dimensions={0}, use_global_device_ids=true | all-gather | bytes 442368 | tf_op jit(solution)/shard_map/all_gather | solution.py:144
  33.9 2.5 %collective-permute-start.4 = (bf16[512,384]{1,0:T(8,128)(2,1)S(1)}, bf16[512,384]{1,0:T(8,128)(2,1)S(1)}, u32[]{:S(2)}, u32[]{:S(2)}) collective-permute-start(bf16[512,384]{1,0:T(8,128)(2,1)S(1)} %all_gather.10), channel_id=1, source_target_pairs={{0,144},{144,0},{16,128},{128,16},{1,145},{145,1},{17,129},{129,17... | collective-permute-start | bytes 1179656 | tf_op jit(solution)/shard_map/ppermute | solution.py:37
  36.4 5.4 %collective-permute-done.4 = bf16[512,384]{1,0:T(8,128)(2,1)S(1)} collective-permute-done((bf16[512,384]{1,0:T(8,128)(2,1)S(1)}, bf16[512,384]{1,0:T(8,128)(2,1)S(1)}, u32[]{:S(2)}, u32[]{:S(2)}) %collective-permute-start.4) | collective-permute-done | bytes 393248 | tf_op jit(solution)/shard_map/ppermute | solution.py:37
  41.8 1.0 maximum_select_fusion.1
  42.9 2.1 %copy.30.down_ref = bf16[8192,64]{1,0:T(8,128)(2,1)S(1)} copy(bf16[8192,64]{0,1:T(8,128)(2,1)} %param.8) | data formatting | bytes 2097152 | tf_op args[3]
  45.4 2.2 %copy-done.2 = bf16[256,8192]{1,0:T(8,128)(2,1)S(1)} copy-done((bf16[256,8192]{1,0:T(8,128)(2,1)S(1)}, bf16[256,8192]{1,0:T(8,128)(2,1)}, u32[]{:S(2)}) %copy-start.2) | copy-done | bytes 4194328
  47.6 3.5 %shard_map.78 = (f32[64,8192]{1,0:T(8,128)S(1)}, f32[64,1024]{1,0:T(8,128)S(1)}) custom-call(bf16[256,8192]{1,0:T(8,128)(2,1)S(1)} %copy-done.2, bf16[8192,64]{1,0:T(8,128)(2,1)S(1)} %copy.30.down_ref, bf16[256,1024]{1,0:T(8,128)(2,1)S(1)} %copy-done.1, bf16[256,64]{1,0:T(8,128)(2,1)S(1)} %copy.33.pulled_ref), custom_call_target="tpu_custom_call" | custom-call | flops 536870912 | bytes 6291456 | tf_op jit(solution)/shard_map/pallas_call | solution.py:102
  51.5 1.3 fusion.1
  53.3 7.4 %collective-permute-start.6 = (f32[64,4608]{1,0:T(8,128)}, f32[64,4608]{1,0:T(8,128)}, u32[]{:S(2)}, u32[]{:S(2)}) collective-permute-start(f32[64,4608]{1,0:T(8,128)} %fusion.1), channel_id=1, source_target_pairs={{0,1},{1,0},{2,3},{3,2},{4,5},{5,4},{6,7},{7,6},{8,9},{9,8},{10,11... | collective-permute-start | bytes 3538952 | tf_op jit(solution)/shard_map/ppermute | solution.py:28
  60.7 2.6 %collective-permute-start.2 = (bf16[64,2560]{1,0:T(8,128)(2,1)S(1)}, bf16[64,2560]{1,0:T(8,128)(2,1)S(1)}, u32[]{:S(2)}, u32[]{:S(2)}) collective-permute-start(bf16[64,2560]{1,0:T(8,128)(2,1)S(1)} %get-tuple-element.31), channel_id=1, source_target_pairs={{0,144},{144,0},{16,128},{128,16},{1,145},{145,1},{17,129},{129,17... | collective-permute-start | bytes 983048 | tf_op jit(solution)/shard_map/ppermute | solution.py:37
  63.3 8.2 %collective-permute-done.2 = bf16[64,2560]{1,0:T(8,128)(2,1)S(1)} collective-permute-done((bf16[64,2560]{1,0:T(8,128)(2,1)S(1)}, bf16[64,2560]{1,0:T(8,128)(2,1)S(1)}, u32[]{:S(2)}, u32[]{:S(2)}) %collective-permute-start.2) | collective-permute-done | bytes 327712 | tf_op jit(solution)/shard_map/ppermute | solution.py:37
  71.5 1.0 maximum_select_fusion.2
  72.5 1.9 fusion.4
  74.4 1.0 copy-done.8
  75.4 0.8 constant_dynamic-slice_fusion.6
  76.2 2.7 %collective-permute-start.9 = (f32[64,1152]{1,0:T(8,128)}, f32[64,1152]{1,0:T(8,128)}, u32[]{:S(2)}, u32[]{:S(2)}) collective-permute-start(f32[64,1152]{1,0:T(8,128)} %get-tuple-element.28), channel_id=1, source_target_pairs={{0,96},{32,0},{64,32},{96,64},{1,97},{33,1},{65,33},{97,65},{2,98}... | collective-permute-start | bytes 884744 | tf_op jit(solution)/shard_map/ppermute | solution.py:23
  79.1 0.7 collective-permute-start.7
  79.8 11.9 %collective-permute-done.9 = f32[64,1152]{1,0:T(8,128)} collective-permute-done((f32[64,1152]{1,0:T(8,128)}, f32[64,1152]{1,0:T(8,128)}, u32[]{:S(2)}, u32[]{:S(2)}) %collective-permute-start.9) | collective-permute-done | bytes 294944 | tf_op jit(solution)/shard_map/ppermute | solution.py:23
  91.7 3.6 %collective-permute-done.8 = f32[64,1152]{1,0:T(8,128)} collective-permute-done((f32[64,1152]{1,0:T(8,128)S(1)}, f32[64,1152]{1,0:T(8,128)}, u32[]{:S(2)}, u32[]{:S(2)}) %collective-permute-start.8) | collective-permute-done | bytes 294944 | tf_op jit(solution)/shard_map/ppermute | solution.py:23
  95.3 6.3 %collective-permute-done.7 = f32[64,1152]{1,0:T(8,128)} collective-permute-done((f32[64,1152]{1,0:T(8,128)S(1)}, f32[64,1152]{1,0:T(8,128)}, u32[]{:S(2)}, u32[]{:S(2)}) %collective-permute-start.7) | collective-permute-done | bytes 294944 | tf_op jit(solution)/shard_map/ppermute | solution.py:23
  101.7 1.3 add_add_fusion
  103.0 2.6 %collective-permute-start.12 = (f32[16,1152]{1,0:T(8,128)S(1)}, f32[16,1152]{1,0:T(8,128)S(1)}, u32[]{:S(2)}, u32[]{:S(2)}) collective-permute-start(f32[16,1152]{1,0:T(8,128)S(1)} %get-tuple-element.35), channel_id=1, source_target_pairs={{0,144},{128,0},{16,128},{144,16},{1,145},{129,1},{17,129},{145,17... | collective-permute-start | bytes 221192 | tf_op jit(solution)/shard_map/ppermute | solution.py:33
  105.6 0.7 collective-permute-start.10
  106.2 1.2 collective-permute-done.12
  107.4 2.9 %collective-permute-done.11 = f32[16,1152]{1,0:T(8,128)S(1)} collective-permute-done((f32[16,1152]{1,0:T(8,128)S(1)}, f32[16,1152]{1,0:T(8,128)S(1)}, u32[]{:S(2)}, u32[]{:S(2)}) %collective-permute-start.11) | collective-permute-done | bytes 73760 | tf_op jit(solution)/shard_map/ppermute | solution.py:33
  110.8 1.1 collective-permute-start.13
  111.8 2.2 %collective-permute-done.13 = f32[16,1152]{1,0:T(8,128)S(1)} collective-permute-done((f32[16,1152]{1,0:T(8,128)S(1)}, f32[16,1152]{1,0:T(8,128)S(1)}, u32[]{:S(2)}, u32[]{:S(2)}) %collective-permute-start.13) | collective-permute-done | bytes 73760 | tf_op jit(solution)/shard_map/ppermute | solution.py:28
  114.1 1.5 collective-permute-start.14
  115.6 2.7 %collective-permute-done.14 = f32[16,1152]{1,0:T(8,128)S(1)} collective-permute-done((f32[16,1152]{1,0:T(8,128)S(1)}, f32[16,1152]{1,0:T(8,128)S(1)}, u32[]{:S(2)}, u32[]{:S(2)}) %collective-permute-start.14) | collective-permute-done | bytes 73760 | tf_op jit(solution)/shard_map/ppermute | solution.py:28
  118.3 4.6 %collective-permute-start.15 = (f32[16,1152]{1,0:T(8,128)S(1)}, f32[16,1152]{1,0:T(8,128)S(1)}, u32[]{:S(2)}, u32[]{:S(2)}) collective-permute-start(f32[16,1152]{1,0:T(8,128)S(1)} %add.202), channel_id=1, source_target_pairs={{0,8},{2,10},{4,12},{6,14},{8,0},{10,2},{12,4},{14,6},{1,9},{3,11}... | collective-permute-start | bytes 221192 | tf_op jit(solution)/shard_map/ppermute | solution.py:28
  122.9 4.5 %collective-permute-done.15 = f32[16,1152]{1,0:T(8,128)S(1)} collective-permute-done((f32[16,1152]{1,0:T(8,128)S(1)}, f32[16,1152]{1,0:T(8,128)S(1)}, u32[]{:S(2)}, u32[]{:S(2)}) %collective-permute-start.15) | collective-permute-done | bytes 73760 | tf_op jit(solution)/shard_map/ppermute | solution.py:28
  127.6 2.9 %collective-permute-start.17 = (f32[16,1152]{1,0:T(8,128)S(1)}, f32[16,1152]{1,0:T(8,128)S(1)}, u32[]{:S(2)}, u32[]{:S(2)}) collective-permute-start(f32[16,1152]{1,0:T(8,128)S(1)} %get-tuple-element.16), channel_id=1, source_target_pairs={{0,16},{128,144},{16,0},{144,128},{1,17},{129,145},{17,1},{145,129... | collective-permute-start | bytes 221192 | tf_op jit(solution)/shard_map/ppermute | solution.py:33
  130.5 1.7 collective-permute-start.18
  132.4 0.6 collective-permute-done.17
  133.0 1.1 collective-permute-done.18
  134.1 4.8 %collective-permute-start.19 = (f32[64,1152]{1,0:T(8,128)S(1)}, f32[64,1152]{1,0:T(8,128)S(1)}, u32[]{:S(2)}, u32[]{:S(2)}) collective-permute-start(f32[64,1152]{1,0:T(8,128)S(1)} %constant_dynamic-update-slice_fusion.4), channel_id=1, source_target_pairs={{0,32},{32,64},{64,96},{96,0},{1,33},{33,65},{65,97},{97,1},{2,34}... | collective-permute-start | bytes 884744 | tf_op jit(solution)/shard_map/ppermute | solution.py:23
  139.0 1.2 collective-permute-start.20
  140.1 1.4 collective-permute-start.21
  141.5 1.1 broadcast_in_dim.6
  142.6 0.7 constant_dynamic-update-slice_fusion.3
  143.5 0.7 constant_dynamic-update-slice_fusion.2
  144.2 3.2 %collective-permute-done.20 = f32[64,1152]{1,0:T(8,128)S(1)} collective-permute-done((f32[64,1152]{1,0:T(8,128)S(1)}, f32[64,1152]{1,0:T(8,128)S(1)}, u32[]{:S(2)}, u32[]{:S(2)}) %collective-permute-start.20) | collective-permute-done | bytes 294944 | tf_op jit(solution)/shard_map/ppermute | solution.py:23
  147.4 0.7 constant_dynamic-update-slice_fusion.1
  148.2 0.7 constant_dynamic-update-slice_fusion
  148.9 8.1 %collective-permute-start.22 = (f32[64,4608]{1,0:T(8,128)}, f32[64,4608]{1,0:T(8,128)}, u32[]{:S(2)}, u32[]{:S(2)}) collective-permute-start(f32[64,4608]{1,0:T(8,128)} %constant_dynamic-update-slice_fusion), channel_id=1, source_target_pairs={{0,1},{1,0},{2,3},{3,2},{4,5},{5,4},{6,7},{7,6},{8,9},{9,8},{10,11... | collective-permute-start | bytes 3538952 | tf_op jit(solution)/shard_map/ppermute | solution.py:28
  157.0 0.8 constant_dynamic-slice_fusion.8.d_ref
  157.8 0.8 constant_dynamic-update-slice_fusion.9
  158.6 1.6 collective-permute-done
  160.2 1.9 constant_dynamic-update-slice_fusion.8.x_ref
  162.1 1.5 copy.27
  164.2 1.6 fusion.5.p_ref
  165.9 2.7 %maximum_select_fusion = f32[2,64,4608]{2,1,0:T(8,128)S(1)} fusion(f32[1,64,4608]{2,1,0:T(8,128)} %bitcast.17, f32[1,64,4608]{2,1,0:T(8,128)} %bitcast.16, pred[]{:T(512)S(6)} %eq.29), kind=kLoop, calls=%fused_computation.5 | loop fusion | flops 1769472 | bytes 4718593 | tf_op jit(solution)/shard_map/jit(_where)/select_n | solution.py:128
  168.6 0.7 pad_maximum_fusion.1
  169.4 1.5 slice_bitcast_fusion.1
  170.8 1.9 copy-done.5
  172.7 5.3 %shard_map.77 = (bf16[256,1536]{1,0:T(8,128)(2,1)S(1)}, bf16[256,1536]{1,0:T(8,128)(2,1)}) custom-call(bf16[512,1024]{1,0:T(8,128)(2,1)} %constant_dynamic-update-slice_fusion.8.x_ref, bf16[4,1024,384]{2,1,0:T(8,128)(2,1)S(1)} %copy-done.5, bf16[512,64]{1,0:T(8,128)(2,1)S(1)} %fusion.5.p_ref, bf16[1536,64]{1,0:T(8,128)(2,1)S(1)} %copy-done.3), custom_call_target="tpu_custom_call" | custom-call | flops 1610612736 | bytes 4718592 | tf_op jit(solution)/shard_map/pallas_call | solution.py:60
  178.2 2.5 %copy-done.4 = bf16[1024,2560]{1,0:T(8,128)(2,1)S(1)} copy-done((bf16[1024,2560]{1,0:T(8,128)(2,1)S(1)}, bf16[1024,2560]{1,0:T(8,128)(2,1)}, u32[]{:S(2)}) %copy-start.4) | copy-done | bytes 5242904
  180.7 4.8 %shard_map.76 = (bf16[256,2560]{1,0:T(8,128)(2,1)S(1)}, bf16[256,2560]{1,0:T(8,128)(2,1)S(1)}) custom-call(bf16[512,1024]{1,0:T(8,128)(2,1)S(1)} %copy.31.x_ref, bf16[1024,2560]{1,0:T(8,128)(2,1)S(1)} %copy-done.4, bf16[512,64]{1,0:T(8,128)(2,1)S(1)} %fusion.5.p_ref, bf16[2560,64]{1,0:T(8,128)(2,1)S(1)} %constant_dynamic-slice_fusion.d_ref), custom_call_target="tpu_custom_call" | custom-call | flops 2684354560 | bytes 7864320 | tf_op jit(solution)/shard_map/pallas_call | solution.py:60
  185.9 1.5 maximum_bitcast_fusion
  187.4 1.2 broadcast_select_fusion.3
  189.0 2.3 %pad_maximum_fusion = bf16[256,8192]{1,0:T(8,128)(2,1)} fusion(bf16[256,1536]{1,0:T(8,128)(2,1)S(1)} %get-tuple-element.26, bf16[256,2560]{1,0:T(8,128)(2,1)S(1)} %get-tuple-element.18, bf16[256,1536]{1,0:T(8,128)(2,1)S(1)} %get-tuple-element.25, bf16[256,2560]{1,0:T(8,128)(2,1)S(1)} %get-tuple-element.17), kind=kLoop, calls=%fused_computation | loop fusion | flops 16777216 | bytes 8388608 | tf_op jit(solution)/shard_map/concatenate | solution.py:198
  (60 shorter events, 4.1 us)
Async XLA Ops:
  7.2 37.8 %copy-start = (bf16[64,1024]{1,0:T(8,128)(2,1)S(1)}, bf16[64,1024]{1,0:T(8,128)(2,1)}, u32[]{:S(2)}) copy-start(bf16[64,1024]{1,0:T(8,128)(2,1)} %param.9) | copy-start | bytes 393220
  7.2 163.6 %all-gather.5.cloned.1.call-start = ((), (), s32[]{:S(2)}) async-start(), calls=%async_computation.1 | async-start | bytes 3932160 | tf_op jit(solution)/shard_map/all_gather | solution.py:146
  8.3 4.5 %collective-permute-start.1 = (bf16[32,4096]{1,0:T(8,128)(2,1)S(1)}, bf16[32,4096]{1,0:T(8,128)(2,1)S(1)}, u32[]{:S(2)}, u32[]{:S(2)}) collective-permute-start(bf16[32,4096]{1,0:T(8,128)(2,1)S(1)} %get-tuple-element.33), channel_id=1, source_target_pairs={{0,1},{1,0},{2,3},{3,2},{4,5},{5,4},{6,7},{7,6},{8,9},{9,8},{10,11... | collective-permute-start | bytes 786440 | tf_op jit(solution)/shard_map/ppermute | solution.py:28
  33.9 7.8 %collective-permute-start.4 = (bf16[512,384]{1,0:T(8,128)(2,1)S(1)}, bf16[512,384]{1,0:T(8,128)(2,1)S(1)}, u32[]{:S(2)}, u32[]{:S(2)}) collective-permute-start(bf16[512,384]{1,0:T(8,128)(2,1)S(1)} %all_gather.10), channel_id=1, source_target_pairs={{0,144},{144,0},{16,128},{128,16},{1,145},{145,1},{17,129},{129,17... | collective-permute-start | bytes 1179656 | tf_op jit(solution)/shard_map/ppermute | solution.py:37
  42.8 135.4 %all-gather.3.cloned.1.call-start = ((), (), s32[]{:S(2)}) async-start(), calls=%async_computation | async-start | bytes 5898240 | tf_op jit(solution)/shard_map/all_gather | solution.py:150
  42.9 2.1 %copy-start.1 = (bf16[256,1024]{1,0:T(8,128)(2,1)S(1)}, bf16[256,1024]{1,0:T(8,128)(2,1)}, u32[]{:S(2)}) copy-start(bf16[256,1024]{1,0:T(8,128)(2,1)} %vg_ref.1) | copy-start | bytes 1572868
  45.4 2.2 %copy-start.2 = (bf16[256,8192]{1,0:T(8,128)(2,1)S(1)}, bf16[256,8192]{1,0:T(8,128)(2,1)}, u32[]{:S(2)}) copy-start(bf16[256,8192]{1,0:T(8,128)(2,1)} %li_ref.1) | copy-start | bytes 12582916
  51.5 1.4 copy-start.6
  51.5 1.8 copy-start.7
  53.3 19.2 %collective-permute-start.6 = (f32[64,4608]{1,0:T(8,128)}, f32[64,4608]{1,0:T(8,128)}, u32[]{:S(2)}, u32[]{:S(2)}) collective-permute-start(f32[64,4608]{1,0:T(8,128)} %fusion.1), channel_id=1, source_target_pairs={{0,1},{1,0},{2,3},{3,2},{4,5},{5,4},{6,7},{7,6},{8,9},{9,8},{10,11... | collective-permute-start | bytes 3538952 | tf_op jit(solution)/shard_map/ppermute | solution.py:28
  60.7 10.7 %collective-permute-start.2 = (bf16[64,2560]{1,0:T(8,128)(2,1)S(1)}, bf16[64,2560]{1,0:T(8,128)(2,1)S(1)}, u32[]{:S(2)}, u32[]{:S(2)}) collective-permute-start(bf16[64,2560]{1,0:T(8,128)(2,1)S(1)} %get-tuple-element.31), channel_id=1, source_target_pairs={{0,144},{144,0},{16,128},{128,16},{1,145},{145,1},{17,129},{129,17... | collective-permute-start | bytes 983048 | tf_op jit(solution)/shard_map/ppermute | solution.py:37
  74.4 1.0 copy-start.8
  76.2 15.6 %collective-permute-start.9 = (f32[64,1152]{1,0:T(8,128)}, f32[64,1152]{1,0:T(8,128)}, u32[]{:S(2)}, u32[]{:S(2)}) collective-permute-start(f32[64,1152]{1,0:T(8,128)} %get-tuple-element.28), channel_id=1, source_target_pairs={{0,96},{32,0},{64,32},{96,64},{1,97},{33,1},{65,33},{97,65},{2,98}... | collective-permute-start | bytes 884744 | tf_op jit(solution)/shard_map/ppermute | solution.py:23
  78.9 16.5 %collective-permute-start.8 = (f32[64,1152]{1,0:T(8,128)S(1)}, f32[64,1152]{1,0:T(8,128)}, u32[]{:S(2)}, u32[]{:S(2)}) collective-permute-start(f32[64,1152]{1,0:T(8,128)S(1)} %get-tuple-element.29), channel_id=1, source_target_pairs={{0,64},{32,96},{64,0},{96,32},{1,65},{33,97},{65,1},{97,33},{2,66}... | collective-permute-start | bytes 884744 | tf_op jit(solution)/shard_map/ppermute | solution.py:23
  79.1 22.6 %collective-permute-start.7 = (f32[64,1152]{1,0:T(8,128)S(1)}, f32[64,1152]{1,0:T(8,128)}, u32[]{:S(2)}, u32[]{:S(2)}) collective-permute-start(f32[64,1152]{1,0:T(8,128)S(1)} %get-tuple-element.27), channel_id=1, source_target_pairs={{0,32},{32,64},{64,96},{96,0},{1,33},{33,65},{65,97},{97,1},{2,34}... | collective-permute-start | bytes 884744 | tf_op jit(solution)/shard_map/ppermute | solution.py:23
  103.0 4.4 %collective-permute-start.12 = (f32[16,1152]{1,0:T(8,128)S(1)}, f32[16,1152]{1,0:T(8,128)S(1)}, u32[]{:S(2)}, u32[]{:S(2)}) collective-permute-start(f32[16,1152]{1,0:T(8,128)S(1)} %get-tuple-element.35), channel_id=1, source_target_pairs={{0,144},{128,0},{16,128},{144,16},{1,145},{129,1},{17,129},{145,17... | collective-permute-start | bytes 221192 | tf_op jit(solution)/shard_map/ppermute | solution.py:33
  105.6 4.8 %collective-permute-start.11 = (f32[16,1152]{1,0:T(8,128)S(1)}, f32[16,1152]{1,0:T(8,128)S(1)}, u32[]{:S(2)}, u32[]{:S(2)}) collective-permute-start(f32[16,1152]{1,0:T(8,128)S(1)} %get-tuple-element.36), channel_id=1, source_target_pairs={{0,16},{128,144},{16,0},{144,128},{1,17},{129,145},{17,1},{145,129... | collective-permute-start | bytes 221192 | tf_op jit(solution)/shard_map/ppermute | solution.py:33
  105.6 5.2 %collective-permute-start.10 = (f32[16,1152]{1,0:T(8,128)S(1)}, f32[16,1152]{1,0:T(8,128)S(1)}, u32[]{:S(2)}, u32[]{:S(2)}) collective-permute-start(f32[16,1152]{1,0:T(8,128)S(1)} %get-tuple-element.34), channel_id=1, source_target_pairs={{0,128},{128,16},{16,144},{144,0},{1,129},{129,17},{17,145},{145,1... | collective-permute-start | bytes 221192 | tf_op jit(solution)/shard_map/ppermute | solution.py:33
  110.8 3.3 %collective-permute-start.13 = (f32[16,1152]{1,0:T(8,128)S(1)}, f32[16,1152]{1,0:T(8,128)S(1)}, u32[]{:S(2)}, u32[]{:S(2)}) collective-permute-start(f32[16,1152]{1,0:T(8,128)S(1)} %add_add_fusion.1), channel_id=1, source_target_pairs={{0,2},{2,0},{4,6},{6,4},{8,10},{10,8},{12,14},{14,12},{1,3},{3,1},... | collective-permute-start | bytes 221192 | tf_op jit(solution)/shard_map/ppermute | solution.py:28
  114.1 4.2 %collective-permute-start.14 = (f32[16,1152]{1,0:T(8,128)S(1)}, f32[16,1152]{1,0:T(8,128)S(1)}, u32[]{:S(2)}, u32[]{:S(2)}) collective-permute-start(f32[16,1152]{1,0:T(8,128)S(1)} %add.201), channel_id=1, source_target_pairs={{0,4},{2,6},{4,0},{6,2},{8,12},{10,14},{12,8},{14,10},{1,5},{3,7},... | collective-permute-start | bytes 221192 | tf_op jit(solution)/shard_map/ppermute | solution.py:28
  118.3 9.1 %collective-permute-start.15 = (f32[16,1152]{1,0:T(8,128)S(1)}, f32[16,1152]{1,0:T(8,128)S(1)}, u32[]{:S(2)}, u32[]{:S(2)}) collective-permute-start(f32[16,1152]{1,0:T(8,128)S(1)} %add.202), channel_id=1, source_target_pairs={{0,8},{2,10},{4,12},{6,14},{8,0},{10,2},{12,4},{14,6},{1,9},{3,11}... | collective-permute-start | bytes 221192 | tf_op jit(solution)/shard_map/ppermute | solution.py:28
  127.5 4.9 %collective-permute-start.16 = (f32[16,1152]{1,0:T(8,128)S(1)}, f32[16,1152]{1,0:T(8,128)S(1)}, u32[]{:S(2)}, u32[]{:S(2)}) collective-permute-start(f32[16,1152]{1,0:T(8,128)S(1)} %get-tuple-element.16), channel_id=1, source_target_pairs={{0,128},{128,16},{16,144},{144,0},{1,129},{129,17},{17,145},{145,1... | collective-permute-start | bytes 221192 | tf_op jit(solution)/shard_map/ppermute | solution.py:33
  127.6 5.4 %collective-permute-start.17 = (f32[16,1152]{1,0:T(8,128)S(1)}, f32[16,1152]{1,0:T(8,128)S(1)}, u32[]{:S(2)}, u32[]{:S(2)}) collective-permute-start(f32[16,1152]{1,0:T(8,128)S(1)} %get-tuple-element.16), channel_id=1, source_target_pairs={{0,16},{128,144},{16,0},{144,128},{1,17},{129,145},{17,1},{145,129... | collective-permute-start | bytes 221192 | tf_op jit(solution)/shard_map/ppermute | solution.py:33
  130.5 3.6 %collective-permute-start.18 = (f32[16,1152]{1,0:T(8,128)S(1)}, f32[16,1152]{1,0:T(8,128)S(1)}, u32[]{:S(2)}, u32[]{:S(2)}) collective-permute-start(f32[16,1152]{1,0:T(8,128)S(1)} %get-tuple-element.16), channel_id=1, source_target_pairs={{0,144},{128,0},{16,128},{144,16},{1,145},{129,1},{17,129},{145,17... | collective-permute-start | bytes 221192 | tf_op jit(solution)/shard_map/ppermute | solution.py:33
  134.1 9.3 %collective-permute-start.19 = (f32[64,1152]{1,0:T(8,128)S(1)}, f32[64,1152]{1,0:T(8,128)S(1)}, u32[]{:S(2)}, u32[]{:S(2)}) collective-permute-start(f32[64,1152]{1,0:T(8,128)S(1)} %constant_dynamic-update-slice_fusion.4), channel_id=1, source_target_pairs={{0,32},{32,64},{64,96},{96,0},{1,33},{33,65},{65,97},{97,1},{2,34}... | collective-permute-start | bytes 884744 | tf_op jit(solution)/shard_map/ppermute | solution.py:23
  139.0 8.5 %collective-permute-start.20 = (f32[64,1152]{1,0:T(8,128)S(1)}, f32[64,1152]{1,0:T(8,128)S(1)}, u32[]{:S(2)}, u32[]{:S(2)}) collective-permute-start(f32[64,1152]{1,0:T(8,128)S(1)} %constant_dynamic-update-slice_fusion.4), channel_id=1, source_target_pairs={{0,64},{32,96},{64,0},{96,32},{1,65},{33,97},{65,1},{97,33},{2,66}... | collective-permute-start | bytes 884744 | tf_op jit(solution)/shard_map/ppermute | solution.py:23
  140.1 8.0 %collective-permute-start.21 = (f32[64,1152]{1,0:T(8,128)S(1)}, f32[64,1152]{1,0:T(8,128)S(1)}, u32[]{:S(2)}, u32[]{:S(2)}) collective-permute-start(f32[64,1152]{1,0:T(8,128)S(1)} %constant_dynamic-update-slice_fusion.4), channel_id=1, source_target_pairs={{0,96},{32,0},{64,32},{96,64},{1,97},{33,1},{65,33},{97,65},{2,98}... | collective-permute-start | bytes 884744 | tf_op jit(solution)/shard_map/ppermute | solution.py:23
  148.9 17.0 %collective-permute-start.22 = (f32[64,4608]{1,0:T(8,128)}, f32[64,4608]{1,0:T(8,128)}, u32[]{:S(2)}, u32[]{:S(2)}) collective-permute-start(f32[64,4608]{1,0:T(8,128)} %constant_dynamic-update-slice_fusion), channel_id=1, source_target_pairs={{0,1},{1,0},{2,3},{3,2},{4,5},{5,4},{6,7},{7,6},{8,9},{9,8},{10,11... | collective-permute-start | bytes 3538952 | tf_op jit(solution)/shard_map/ppermute | solution.py:28
  157.0 3.2 %collective-permute-start = (bf16[256,1024]{1,0:T(8,128)(2,1)S(1)}, bf16[256,1024]{1,0:T(8,128)(2,1)}, u32[]{:S(2)}, u32[]{:S(2)}) collective-permute-start(bf16[256,1024]{1,0:T(8,128)(2,1)S(1)} %copy-done.1), channel_id=1, source_target_pairs={{0,1},{1,0},{2,3},{3,2},{4,5},{5,4},{6,7},{7,6},{8,9},{9,8},{10,11... | collective-permute-start | bytes 1572872 | tf_op jit(solution)/shard_map/ppermute | solution.py:28
  169.4 1.5 copy-start.3
  170.8 1.9 copy-start.5
  178.0 9.3 %collective-permute-start.5 = (bf16[256,1536]{1,0:T(8,128)(2,1)}, bf16[256,1536]{1,0:T(8,128)(2,1)}, u32[]{:S(2)}, u32[]{:S(2)}) collective-permute-start(bf16[256,1536]{1,0:T(8,128)(2,1)} %get-tuple-element.12), channel_id=1, source_target_pairs={{0,1},{1,0},{2,3},{3,2},{4,5},{5,4},{6,7},{7,6},{8,9},{9,8},{10,11... | collective-permute-start | bytes 2359304 | tf_op jit(solution)/shard_map/ppermute | solution.py:28
  178.2 2.5 %copy-start.4 = (bf16[1024,2560]{1,0:T(8,128)(2,1)S(1)}, bf16[1024,2560]{1,0:T(8,128)(2,1)}, u32[]{:S(2)}) copy-start(bf16[1024,2560]{1,0:T(8,128)(2,1)} %all-gather.3.cloned.1.call-done.w_ref) | copy-start | bytes 15728644
  180.7 5.2 %copy-start.9 = (f32[64,4096]{1,0:T(8,128)S(1)}, f32[64,4096]{1,0:T(8,128)}, u32[]{:S(2)}) copy-start(f32[64,4096]{1,0:T(8,128)} %get-tuple-element.21) | copy-start | bytes 3145732
  180.7 5.2 %copy-start.10 = (f32[64,4096]{1,0:T(8,128)S(1)}, f32[64,4096]{1,0:T(8,128)}, u32[]{:S(2)}) copy-start(f32[64,4096]{1,0:T(8,128)} %get-tuple-element.22) | copy-start | bytes 3145732
  185.5 3.1 %collective-permute-start.3 = (bf16[256,2560]{1,0:T(8,128)(2,1)S(1)}, bf16[256,2560]{1,0:T(8,128)(2,1)S(1)}, u32[]{:S(2)}, u32[]{:S(2)}) collective-permute-start(bf16[256,2560]{1,0:T(8,128)(2,1)S(1)} %get-tuple-element.10), channel_id=1, source_target_pairs={{0,1},{1,0},{2,3},{3,2},{4,5},{5,4},{6,7},{7,6},{8,9},{9,8},{10,11... | collective-permute-start | bytes 3932168 | tf_op jit(solution)/shard_map/ppermute | solution.py:28
Sparse Core Ops, SparseCore 0:
  42.9 60.7 all-gather.4
  105.5 67.9 all-gather.2

commit v2 on v0

v2 whole, which is shorter than its diff:
```python
import functools
import math

import jax
import jax.numpy as jnp
from jax import lax
from jax.experimental import pallas as pl
from jax.experimental.pallas import tpu as pltpu
from jax.sharding import Mesh
from jax.sharding import PartitionSpec as P

adapter_scale = 2.0
AXES = ("x_lo", "y", "x_hi", "z", "core")
SIZES = (2, 4, 2, 8, 2)
D = 8192
HALF = D // 2
UCOLS = 2048
ZCOLS = HALF - UCOLS
STEP = 512
f32, bf16 = jnp.float32, jnp.bfloat16
ANY = pl.BlockSpec(memory_space=pl.ANY)


def shift(x, axis, k):
    n = SIZES[AXES.index(axis)]
    return lax.ppermute(x, axis, [(i, (i + k) % n) for i in range(n)])


def flip(x, axis, k):
    n = SIZES[AXES.index(axis)]
    return lax.ppermute(x, axis, [(i, i ^ k) for i in range(n)])


def cross_x(x):
    return lax.ppermute(x, ("x_lo", "x_hi"), [(0, 3), (3, 0), (1, 2), (2, 1)])


def after(x, *others):
    return lax.optimization_barrier((x, *others))[0]


def params(mib=32):
    return pltpu.CompilerParams(vmem_limit_bytes=mib * 2**20)


def product_kernel(at_ref, grads, pulled, down, *refs, paired):
    own_ref, other_ref = refs[-2:]
    half, step = grads.shape[1] // 2, own_ref.shape[1]
    total = jnp.dot(pulled[...], down[...], preferred_element_type=f32)
    for far in (0, 1):
        at = pl.ds(pl.multiple_of((at_ref[1] + far) % 2 * half, 128), half)
        rows = refs[0][:, far].reshape(half, step) if paired else refs[far][...]
        total += jnp.dot(grads[:, at], rows, preferred_element_type=f32)
    total = total.astype(bf16)
    rows = own_ref.shape[0]
    own_ref[...] = total[:rows]
    other_ref[...] = total[rows:]


def product(at, x_hi, grads, pulled, down_t, weights, result=None):
    tokens, n = grads.shape[0], weights[0].shape[-1]
    whole = lambda a: pl.BlockSpec(a.shape, lambda i, at: (0,) * a.ndim)
    args = [grads, pulled, down_t, *weights] + ([] if result is None else [result])
    weight_spec = lambda w: pl.BlockSpec((*w.shape[:-1], STEP), lambda i, at: (0,) * (w.ndim - 1) + (i,))
    size = sum(w.size for w in weights)
    return pl.pallas_call(
        functools.partial(product_kernel, paired=len(weights) == 1),
        grid_spec=pltpu.PrefetchScalarGridSpec(
            num_scalar_prefetch=1,
            grid=(n // STEP,),
            in_specs=[
                whole(grads),
                whole(pulled),
                pl.BlockSpec((pulled.shape[1], STEP), lambda i, at: (0, at[0] + i)),
            ]
            + [weight_spec(w) for w in weights]
            + ([] if result is None else [ANY]),
            out_specs=[
                pl.BlockSpec((tokens // 2, STEP), lambda i, at: (0, at[0] + i)),
                pl.BlockSpec((tokens // 2, STEP), lambda i, at: (0, i)),
            ],
        ),
        out_shape=[
            jax.ShapeDtypeStruct((tokens // 2, D), bf16),
            jax.ShapeDtypeStruct((tokens // 2, n), bf16),
        ],
        input_output_aliases={} if result is None else {len(args): 0},
        compiler_params=params(56),
        cost_estimate=pl.CostEstimate(
            flops=2 * tokens * size, bytes_accessed=2 * size + 2 * tokens * n, transcendentals=0
        ),
    )(jnp.stack([at // STEP, x_hi]), *args)


def place_kernel(at_ref, piece, _, out, sems, *, parts):
    step = piece.shape[1] // parts
    copies = []
    for k in range(parts):
        there = pl.ds(pl.multiple_of(at_ref[k], 128), step)
        source = piece.at[:, k * step : (k + 1) * step]
        copies.append(pltpu.make_async_copy(source, out.at[:, there], sems.at[k]))
    for copy in copies:
        copy.start()
    for copy in copies:
        copy.wait()


def place(at, piece, result):
    parts = at.shape[0]
    return pl.pallas_call(
        functools.partial(place_kernel, parts=parts),
        grid_spec=pltpu.PrefetchScalarGridSpec(
            num_scalar_prefetch=1,
            grid=(1,),
            in_specs=[pl.BlockSpec(piece.shape, lambda i, at: (0, 0)), ANY],
            out_specs=ANY,
            scratch_shapes=[pltpu.SemaphoreType.DMA((parts,))],
        ),
        out_shape=jax.ShapeDtypeStruct(result.shape, result.dtype),
        input_output_aliases={2: 0},
        compiler_params=params(),
        cost_estimate=pl.CostEstimate(flops=0, bytes_accessed=4 * piece.size, transcendentals=0),
    )(at, piece, result)


def adapter_kernel(core_ref, li_ref, down_ref, vg_ref, up_ref, keep_ref, give_ref, proj, pulled, *, factor):
    i = pl.program_id(0)
    step = li_ref.shape[1]
    rows = keep_ref.shape[1]
    blocks = pulled.shape[1] // rows
    per = keep_ref.shape[0] // blocks

    @pl.when(i == 0)
    def _():
        proj[...] = jnp.zeros_like(proj)
        pulled[...] = lax.dot_general(
            vg_ref[...], up_ref[...], (((1,), (1,)), ((), ())), preferred_element_type=f32
        ).astype(bf16)

    li = li_ref[...]
    proj[...] += lax.dot_general(
        li, down_ref[...], (((1,), (1,)), ((), ())), preferred_element_type=f32
    )
    part = factor * lax.dot_general(
        pulled[...], li, (((0,), (0,)), ((), ())), preferred_element_type=f32
    )
    mine = i // per == core_ref[0]

    def put(ref):
        for b in range(blocks):
            ref[b * per + i % per, :, :step] = part[b * rows : (b + 1) * rows]

    pl.when(mine)(lambda: put(keep_ref))
    pl.when(jnp.logical_not(mine))(lambda: put(give_ref))

    @pl.when(i == pl.num_programs(0) - 1)
    def _():
        up = factor * lax.dot_general(
            proj[...].astype(bf16), vg_ref[...], (((0,), (0,)), ((), ())), preferred_element_type=f32
        )
        h = up.shape[1] // 2
        w = h // per
        first = core_ref[0] == 0
        mine = jnp.where(first, up[:, :h], up[:, h:])
        other = jnp.where(first, up[:, h:], up[:, :h])
        for b in range(blocks):
            for c in range(per):
                part = slice(b * rows, (b + 1) * rows), slice(c * w, (c + 1) * w)
                keep_ref[b * per + c, :, step:] = mine[part]
                give_ref[b * per + c, :, step:] = other[part]


def adapter_parts(core, li, down_t, vg, up, factor, blocks=4, step=1024):
    tokens, width = li.shape
    rank, features = up.shape
    per = width // step // 2
    out = jax.ShapeDtypeStruct((blocks * per, rank // blocks, step + features // 2 // per), f32)
    whole = lambda a: pl.BlockSpec(a.shape, lambda i, c: (0,) * len(a.shape))
    return pl.pallas_call(
        functools.partial(adapter_kernel, factor=factor),
        grid_spec=pltpu.PrefetchScalarGridSpec(
            num_scalar_prefetch=1,
            grid=(width // step,),
            in_specs=[
                pl.BlockSpec((tokens, step), lambda i, c: (0, i)),
                pl.BlockSpec((rank, step), lambda i, c: (0, i)),
                whole(vg),
                whole(up),
            ],
            out_specs=[whole(out), whole(out)],
            scratch_shapes=[pltpu.VMEM((tokens, rank), f32), pltpu.VMEM((tokens, rank), bf16)],
        ),
        out_shape=[out, out],
        compiler_params=params(),
        cost_estimate=pl.CostEstimate(
            flops=4 * tokens * width * rank, bytes_accessed=2 * tokens * width + 4 * rank * width, transcendentals=0
        ),
    )(core, li, down_t, vg, up)


def finish_kernel(core_ref, mine, other, down_ref, up_ref, *, blocks):
    i = pl.program_id(0)
    step = down_ref.shape[1]
    per = mine.shape[0] // blocks

    def put(ref):
        for b in range(blocks):
            block = ref[b * per + i % per]
            rows = block.shape[0]
            down_ref[b * rows : (b + 1) * rows, :] = block[:, :step]
            up_ref[b * rows : (b + 1) * rows, :] = block[:, step:]

    pl.when(i < per)(lambda: put(mine))
    pl.when(i >= per)(lambda: put(other))


def finish(core, mine, other, rank, features, blocks=4, step=1024):
    per = mine.shape[0] // blocks
    whole = lambda a: pl.BlockSpec(a.shape, lambda i, c: (0,) * len(a.shape))
    at = lambda i, c: jnp.where(i < per, c[0], 1 - c[0]) * per + i % per
    return pl.pallas_call(
        functools.partial(finish_kernel, blocks=blocks),
        grid_spec=pltpu.PrefetchScalarGridSpec(
            num_scalar_prefetch=1,
            grid=(2 * per,),
            in_specs=[whole(mine), whole(other)],
            out_specs=[
                pl.BlockSpec((rank, step), lambda i, c: (0, at(i, c))),
                pl.BlockSpec((rank, features // 2 // per), lambda i, c: (0, at(i, c))),
            ],
        ),
        out_shape=[
            jax.ShapeDtypeStruct((rank, 2 * per * step), f32),
            jax.ShapeDtypeStruct((rank, features), f32),
        ],
        compiler_params=params(),
        cost_estimate=pl.CostEstimate(flops=0, bytes_accessed=8 * mine.size, transcendentals=0),
    )(core, mine, other)


def local(layer_input, value_grad, base_weight_t, adapter_down, adapter_up):
    core, x_hi = lax.axis_index("core"), lax.axis_index("x_hi")
    plane = ("x_lo", "y", "x_hi")
    tokens, features = value_grad.shape
    rank = adapter_up.shape[0]
    factor = adapter_scale / math.sqrt(tokens * math.prod(SIZES))
    down_t = adapter_down.T

    mine = lax.dynamic_slice_in_dim(base_weight_t, core * HALF, HALF, 1)
    give = lax.dynamic_slice_in_dim(base_weight_t, (1 - core) * HALF, HALF, 1)
    got = flip(give, "core", 1)
    chip_rows = jnp.where(core == 0, jnp.concatenate([mine, got]), jnp.concatenate([got, mine]))

    keep, give = adapter_parts(
        core.reshape(1), after(layer_input, chip_rows), down_t, value_grad, adapter_up, factor
    )
    total = keep + flip(give, "core", 1)
    total = lax.all_to_all(total, plane, 0, 0, tiled=True).sum(0)
    near = lax.all_gather(chip_rows[:, ZCOLS:], "z", axis=0, tiled=True)
    far = cross_x(after(near, total))
    strip = chip_rows[:, :ZCOLS]
    strips = after(jnp.stack([strip, cross_x(strip)]), near, total)
    weight_z = lax.all_gather(strips, "z", axis=0, tiled=False)

    for k in (1, 2, 4):
        total = total + flip(total, "z", k)
    half = lax.all_to_all(
        jnp.broadcast_to(total, (16, *total.shape)), plane, 0, 0, tiled=True
    )
    down_grad_t, up_grad = finish(core.reshape(1), half, flip(half, "core", 1), rank, features)

    grads = jnp.concatenate([value_grad, flip(value_grad, "core", 1)], 0)
    pulled = lax.dot_general(
        grads, adapter_up, (((1,), (1,)), ((), ())), preferred_element_type=f32
    ).astype(bf16)
    pulled = (adapter_scale * pulled).astype(bf16)
    result, send_u = product(core * HALF + ZCOLS, x_hi, grads, pulled, down_t, [near, far])
    result, send_z = product(core * HALF, x_hi, grads, pulled, down_t, [weight_z], result)
    base = (1 - core) * HALF
    result = place((base + ZCOLS).reshape(1), flip(send_u, "core", 1), result)
    result = place(base.reshape(1), flip(send_z, "core", 1), result)
    return (result, down_grad_t.T, up_grad)


def solution(mesh):
    fine = Mesh(mesh.devices.reshape(SIZES), AXES)
    return jax.shard_map(
        local,
        mesh=fine,
        in_specs=(P(AXES, None), P(AXES, None), P(("x_hi", "z", "core"), None), P(), P()),
        out_specs=(P(AXES, None), P(), P()),
        check_vma=False,
    )
```

time: 346 us -> 143 us (0.41)
  waiting for transfers between devices: 304 us -> 51.2 us
  starting transfers between devices: 0.08 us -> 43.3 us
  Pallas kernels: 0 us -> 24.3 us
  matrix products: 21.6 us -> 1.08 us
  other arithmetic: 0 us -> 3.53 us
    psum x1 -> x0, waiting for transfers between devices: 168 us -> none  [local(): down_grad, up_grad = lax.psum((part_down, part_up), ('dp', 'fsdp'))]
    all_gather x1 -> x2, waiting for transfers between devices: 135 us -> 1.11 us  [the longest x1 1.09 us: local(): near = lax.all_gather(chip_rows[:, ZCOLS:], 'z', axis=0, tiled=True)]
    ppermute x0 -> x11, starting transfers between devices: none -> 33.9 us  [the longest x9 28.7 us: flip(): return lax.ppermute(x, axis, [(i, i ^ k) for i in range(n)])]
    ppermute x0 -> x11, waiting for transfers between devices: none -> 32.8 us  [the longest x2 18.4 us: cross_x(): return lax.ppermute(x, ('x_lo', 'x_hi'), [(0, 3), (3, 0), (1, 2), (2, 1)])]
    pallas_call x0 -> x6, Pallas kernels: none -> 24.3 us  [the longest x2 14.2 us: product(): pl.pallas_call(functools.partial(product_kernel, paired=len(weights) == 1...]
    dot_general x5 -> x1, matrix products: 21.6 us -> 1.08 us  [local(): lax.dot_general(grads, adapter_up, (((1,), (1,)), ((), ())), preferred_el...]
    all_to_all x0 -> x2, waiting for transfers between devices: none -> 17.2 us  [the longest x1 17.2 us: local(): lax.all_to_all(jnp.broadcast_to(total, (16, *total.shape)), plane, 0, 0,...]
    all_to_all x0 -> x2, starting transfers between devices: none -> 9.4 us  [the longest x1 5.02 us: local(): total = lax.all_to_all(total, plane, 0, 0, tiled=True).sum(0)]
  transfers between devices with their start and end apart: 2 -> 15, of which waited for: 2 -> 9; matrix products, arithmetic and copies ran while one was open for 6% -> 4% of each run, Pallas kernels for 0% -> 15%
where the time goes in v2:
time: 143 us
  waiting for transfers between devices  51.2 us (36%)
  starting transfers between devices  43.3 us (30%)
  Pallas kernels  24.3 us (17%)
  between operations  14.2 us (10%)
  local copies, waits for them, and re-layouts  5.33 us (4%)
  other arithmetic  3.53 us (2%)
    ppermute x9, starting transfers between devices, flip(): return lax.ppermute(x, axis, [(i, i ^ k) for i in range(n)])  28.7 us
    ppermute x2, waiting for transfers between devices, cross_x(): return lax.ppermute(x, ('x_lo', 'x_hi'), [(0, 3), (3, 0), (1, 2), (2, 1)])  18.4 us
    all_to_all x1, waiting for transfers between devices, local(): lax.all_to_all(jnp.broadcast_to(total, (16, *total.shape)), plane, 0, 0,...  17.2 us
    ppermute x9, waiting for transfers between devices, flip(): return lax.ppermute(x, axis, [(i, i ^ k) for i in range(n)])  14.3 us
    pallas_call x2, Pallas kernels, product(): pl.pallas_call(functools.partial(product_kernel, paired=len(weights) == 1...  14.2 us
    ppermute x2, starting transfers between devices, cross_x(): return lax.ppermute(x, ('x_lo', 'x_hi'), [(0, 3), (3, 0), (1, 2), (2, 1)])  5.16 us
    all_to_all x1, starting transfers between devices, local(): total = lax.all_to_all(total, plane, 0, 0, tiled=True).sum(0)  5.02 us
    all_to_all x1, starting transfers between devices, local(): lax.all_to_all(jnp.broadcast_to(total, (16, *total.shape)), plane, 0, 0,...  4.38 us
  transfers between devices with their start and end apart: 15, of which 9 were waited for; matrix products, arithmetic and copies ran while one was open for 4% of the time, Pallas kernels for 15%

profile of v2, /device:TPU:1, one launch (start us, length us, event | category | flops | bytes accessed | tf_op | source)
XLA Modules:
  0.0 143.0 jit_solution(12025355432514186347)
XLA Ops:
  7.2 0.0 copy-start.2
  7.2 0.0 copy-start.3
  7.2 0.0 copy-start.1
  7.2 0.0 all-gather.4.cloned.1.call-start
  7.3 1.2 constant_dynamic-slice_fusion.1
  8.4 3.3 %collective-permute-start.1 = (bf16[32,4096]{1,0:T(8,128)(2,1)S(1)}, bf16[32,4096]{1,0:T(8,128)(2,1)S(1)}, u32[]{:S(2)}, u32[]{:S(2)}) collective-permute-start(bf16[32,4096]{1,0:T(8,128)(2,1)S(1)} %get-tuple-element.29), channel_id=1, source_target_pairs={{0,1},{1,0},{2,3},{3,2},{4,5},{5,4},{6,7},{7,6},{8,9},{9,8},{10,11... | collective-permute-start | bytes 786440 | tf_op jit(solution)/shard_map/ppermute | solution.py:31
  11.8 1.2 collective-permute-done.1
  12.9 0.1 maximum_select_fusion
  13.0 0.8 fusion.1
  13.8 0.0 all-gather.4.cloned.1.call-update
  13.8 0.0 copy-done.2
  13.8 0.0 copy-done.3
  13.8 0.0 copy-done.1
  13.9 0.0 copy-start
  13.9 2.2 %copy-done = bf16[256,8192]{1,0:T(8,128)(2,1)S(1)} copy-done((bf16[256,8192]{1,0:T(8,128)(2,1)S(1)}, bf16[256,8192]{1,0:T(8,128)(2,1)}, u32[]{:S(2)}) %copy-start) | copy-done | bytes 4194328
  16.0 3.9 %shard_map.76 = (f32[16,16,1152]{2,1,0:T(8,128)S(1)}, f32[16,16,1152]{2,1,0:T(8,128)S(1)}) custom-call(s32[1]{0:T(128)} %bitcast.6.core_ref, bf16[256,8192]{1,0:T(8,128)(2,1)S(1)} %copy-done, bf16[64,8192]{1,0:T(8,128)(2,1)S(1)} %bitcast.16, bf16[256,1024]{1,0:T(8,128)(2,1)S(1)} %copy-done.2, bf16[64,1024]{1,0:T(8,128)(2,1)S(1)} %copy-done.3), custom_call_target="tpu_custom_call" | custom-call | flops 536870912 | bytes 6291456 | tf_op jit(solution)/shard_map/pallas_call | solution.py:179
  19.9 0.5 collective-permute-start.3
  20.4 2.5 %collective-permute-done.3 = f32[16,16,1152]{2,1,0:T(8,128)S(1)} collective-permute-done((f32[16,16,1152]{2,1,0:T(8,128)S(1)}, f32[16,16,1152]{2,1,0:T(8,128)S(1)}, u32[]{:S(2)}, u32[]{:S(2)}) %collective-permute-start.3) | collective-permute-done | bytes 1179680 | tf_op jit(solution)/shard_map/ppermute | solution.py:31
  22.9 1.2 add.28
  24.1 5.0 %all-to-all-start = ((f32[16,16,1152]{2,1,0:T(8,128)}), f32[16,16,1152]{2,1,0:T(8,128)S(1)}, u32[]{:S(2)}, u32[]{:S(2)}) async-start(f32[16,16,1152]{2,1,0:T(8,128)} %add.28), calls=%async_computation | async-start | bytes 2359296 | tf_op jit(solution)/shard_map/all_to_all | solution.py:258
  29.1 0.0 all-gather.6.cloned.1.call-start
  29.2 2.7 %collective-permute-start.2 = (bf16[64,2048]{1,0:T(8,128)(2,1)S(1)}, bf16[64,2048]{1,0:T(8,128)(2,1)S(1)}, u32[]{:S(2)}, u32[]{:S(2)}) collective-permute-start(bf16[64,2048]{1,0:T(8,128)(2,1)S(1)} %get-tuple-element.27), channel_id=1, source_target_pairs={{0,144},{144,0},{16,128},{128,16},{1,145},{145,1},{17,129},{129,17... | collective-permute-start | bytes 786440 | tf_op jit(solution)/shard_map/ppermute | solution.py:35
  31.9 18.4 %collective-permute-done.2 = bf16[64,2048]{1,0:T(8,128)(2,1)S(1)} collective-permute-done((bf16[64,2048]{1,0:T(8,128)(2,1)S(1)}, bf16[64,2048]{1,0:T(8,128)(2,1)S(1)}, u32[]{:S(2)}, u32[]{:S(2)}) %collective-permute-start.2) | collective-permute-done | bytes 262176 | tf_op jit(solution)/shard_map/ppermute | solution.py:35
  50.3 0.9 pad_maximum_fusion
  51.2 0.0 all-to-all-done
  51.2 0.1 reduce_sum.9
  51.2 1.1 all-gather.4.cloned.1.call-done.refs_0_
  52.3 0.0 all-gather.6.cloned.1.call-update
  52.3 2.5 %collective-permute-start.4 = (bf16[512,2048]{1,0:T(8,128)(2,1)}, bf16[512,2048]{1,0:T(8,128)(2,1)}, u32[]{:S(2)}, u32[]{:S(2)}) collective-permute-start(bf16[512,2048]{1,0:T(8,128)(2,1)} %all-gather.4.cloned.1.call-done.refs_0_), channel_id=1, source_target_pairs={{0,144},{144,0},{16,128},{128,16},{1,145},{145,1},{17,129},{129,17... | collective-permute-start | bytes 6291464 | tf_op jit(solution)/shard_map/ppermute | solution.py:35
  54.8 0.5 collective-permute-start.7
  55.3 2.7 %collective-permute-done.7 = f32[16,1152]{1,0:T(8,128)S(1)} collective-permute-done((f32[16,1152]{1,0:T(8,128)S(1)}, f32[16,1152]{1,0:T(8,128)S(1)}, u32[]{:S(2)}, u32[]{:S(2)}) %collective-permute-start.7) | collective-permute-done | bytes 73760 | tf_op jit(solution)/shard_map/ppermute | solution.py:31
  58.1 1.8 %collective-permute-start.8 = (f32[16,1152]{1,0:T(8,128)S(1)}, f32[16,1152]{1,0:T(8,128)S(1)}, u32[]{:S(2)}, u32[]{:S(2)}) collective-permute-start(f32[16,1152]{1,0:T(8,128)S(1)} %add.31), channel_id=1, source_target_pairs={{0,4},{2,6},{4,0},{6,2},{8,12},{10,14},{12,8},{14,10},{1,5},{3,7},... | collective-permute-start | bytes 221192 | tf_op jit(solution)/shard_map/ppermute | solution.py:31
  59.9 3.6 %collective-permute-done.8 = f32[16,1152]{1,0:T(8,128)S(1)} collective-permute-done((f32[16,1152]{1,0:T(8,128)S(1)}, f32[16,1152]{1,0:T(8,128)S(1)}, u32[]{:S(2)}, u32[]{:S(2)}) %collective-permute-start.8) | collective-permute-done | bytes 73760 | tf_op jit(solution)/shard_map/ppermute | solution.py:31
  63.5 3.9 %collective-permute-start.9 = (f32[16,1152]{1,0:T(8,128)S(1)}, f32[16,1152]{1,0:T(8,128)S(1)}, u32[]{:S(2)}, u32[]{:S(2)}) collective-permute-start(f32[16,1152]{1,0:T(8,128)S(1)} %add.32), channel_id=1, source_target_pairs={{0,8},{2,10},{4,12},{6,14},{8,0},{10,2},{12,4},{14,6},{1,9},{3,11}... | collective-permute-start | bytes 221192 | tf_op jit(solution)/shard_map/ppermute | solution.py:31
  67.3 4.1 %collective-permute-done.9 = f32[16,1152]{1,0:T(8,128)S(1)} collective-permute-done((f32[16,1152]{1,0:T(8,128)S(1)}, f32[16,1152]{1,0:T(8,128)S(1)}, u32[]{:S(2)}, u32[]{:S(2)}) %collective-permute-start.9) | collective-permute-done | bytes 73760 | tf_op jit(solution)/shard_map/ppermute | solution.py:31
  71.5 1.1 broadcast_in_dim.3
  72.6 4.4 %all-to-all-start.1 = ((f32[16,16,1152]{2,1,0:T(8,128)}), f32[16,16,1152]{2,1,0:T(8,128)S(1)}, u32[]{:S(2)}, u32[]{:S(2)}) async-start(f32[16,16,1152]{2,1,0:T(8,128)} %broadcast_in_dim.3), calls=%async_computation.1 | async-start | bytes 2359296 | tf_op jit(solution)/shard_map/all_to_all | solution.py:267
  77.0 11.5 %collective-permute-start = (bf16[256,1024]{1,0:T(8,128)(2,1)S(1)}, bf16[256,1024]{1,0:T(8,128)(2,1)S(1)}, u32[]{:S(2)}, u32[]{:S(2)}) collective-permute-start(bf16[256,1024]{1,0:T(8,128)(2,1)S(1)} %copy-done.2), channel_id=1, source_target_pairs={{0,1},{1,0},{2,3},{3,2},{4,5},{5,4},{6,7},{7,6},{8,9},{9,8},{10,11... | collective-permute-start | bytes 1572872 | tf_op jit(solution)/shard_map/ppermute | solution.py:31
  88.4 0.6 pad_add_fusion.at_ref
  89.0 0.6 pad_add_fusion.1.at_ref
  89.7 0.2 collective-permute-done
  90.0 0.0 copy-start.4
  90.0 1.1 fusion.pulled
  91.1 0.0 copy-done.4
  91.1 17.2 %all-to-all-done.1.mine = f32[16,16,1152]{2,1,0:T(8,128)S(1)} async-done(((f32[16,16,1152]{2,1,0:T(8,128)}), f32[16,16,1152]{2,1,0:T(8,128)S(1)}, u32[]{:S(2)}, u32[]{:S(2)}) %all-to-all-start.1) | async-done | bytes 1179680 | tf_op jit(solution)/shard_map/all_to_all | solution.py:267
  108.3 6.8 %collective-permute-start.10 = (f32[16,16,1152]{2,1,0:T(8,128)S(1)}, f32[16,16,1152]{2,1,0:T(8,128)S(1)}, u32[]{:S(2)}, u32[]{:S(2)}) collective-permute-start(f32[16,16,1152]{2,1,0:T(8,128)S(1)} %all-to-all-done.1.mine), channel_id=1, source_target_pairs={{0,1},{1,0},{2,3},{3,2},{4,5},{5,4},{6,7},{7,6},{8,9},{9,8},{10,11... | collective-permute-start | bytes 3538952 | tf_op jit(solution)/shard_map/ppermute | solution.py:31
  115.1 0.0 collective-permute-done.4.refs_1_
  115.1 7.2 %shard_map.77 = (bf16[256,8192]{1,0:T(8,128)(2,1)}, bf16[256,2048]{1,0:T(8,128)(2,1)}) custom-call(s32[2]{0:T(128)} %pad_add_fusion.1.at_ref, bf16[512,1024]{1,0:T(8,128)(2,1)} %copy-done.4, bf16[512,64]{1,0:T(8,128)(2,1)} %fusion.pulled, bf16[64,8192]{1,0:T(8,128)(2,1)} %bitcast.14, bf16[512,2048]{1,0:T(8,128)(2,1)} %all-gather.4.cloned.1.call-done.refs_0_, ...), custom_call_target="tpu_custom_call" | custom-call | flops 2147483648 | bytes 6291456 | tf_op jit(solution)/shard_map/pallas_call | solution.py:66
  122.3 0.0 collective-permute-start.6
  122.3 0.0 all-gather.6.cloned.1.call-done
  122.4 7.1 %shard_map.78 = (bf16[256,8192]{1,0:T(8,128)(2,1)}, bf16[256,2048]{1,0:T(8,128)(2,1)}) custom-call(s32[2]{0:T(128)} %pad_add_fusion.at_ref, bf16[512,1024]{1,0:T(8,128)(2,1)} %copy-done.4, bf16[512,64]{1,0:T(8,128)(2,1)} %fusion.pulled, bf16[64,8192]{1,0:T(8,128)(2,1)} %bitcast.15, ...), custom_call_target="tpu_custom_call", output_to_operand_aliasing={{0}: (5, {})} | custom-call | flops 2147483648 | bytes 6291456 | tf_op jit(solution)/shard_map/pallas_call | solution.py:66
  129.4 0.5 collective-permute-start.5
  129.9 0.0 collective-permute-done.10.other
  129.9 3.0 %shard_map.81 = (f32[64,8192]{1,0:T(8,128)}, f32[64,1024]{1,0:T(8,128)}) custom-call(s32[1]{0:T(128)} %bitcast.6.core_ref, f32[16,16,1152]{2,1,0:T(8,128)S(1)} %all-to-all-done.1.mine, f32[16,16,1152]{2,1,0:T(8,128)S(1)} %collective-permute-done.10.other), custom_call_target="tpu_custom_call" | custom-call | bytes 2359296 | tf_op jit(solution)/shard_map/pallas_call | solution.py:221
  132.9 0.0 collective-permute-done.6.piece
  132.9 1.0 shard_map.79._
  133.9 0.0 collective-permute-done.5.piece
  133.9 2.2 %shard_map.80 = bf16[256,8192]{1,0:T(8,128)(2,1)} custom-call(s32[1]{0:T(128)} %bitcast.at_ref, bf16[256,2048]{1,0:T(8,128)(2,1)} %collective-permute-done.5.piece, bf16[256,8192]{1,0:T(8,128)(2,1)} %shard_map.79._), custom_call_target="tpu_custom_call", output_to_operand_aliasing={{}: (2, {})} | custom-call | bytes 2097152 | tf_op jit(solution)/shard_map/pallas_call | solution.py:110
  (5 shorter events, 0.1 us)
Async XLA Ops:
  7.2 6.7 %copy-start.2 = (bf16[256,1024]{1,0:T(8,128)(2,1)S(1)}, bf16[256,1024]{1,0:T(8,128)(2,1)}, u32[]{:S(2)}) copy-start(bf16[256,1024]{1,0:T(8,128)(2,1)} %vg_ref.1) | copy-start | bytes 1572868
  7.2 6.7 %copy-start.3 = (bf16[64,1024]{1,0:T(8,128)(2,1)S(1)}, bf16[64,1024]{1,0:T(8,128)(2,1)}, u32[]{:S(2)}) copy-start(bf16[64,1024]{1,0:T(8,128)(2,1)} %up_ref.1) | copy-start | bytes 393220
  7.2 6.7 %copy-start.1 = (bf16[8192,64]{0,1:T(8,128)(2,1)S(1)}, bf16[8192,64]{0,1:T(8,128)(2,1)}, u32[]{:S(2)}) copy-start(bf16[8192,64]{0,1:T(8,128)(2,1)} %param.8) | copy-start | bytes 3145732
  7.2 45.1 %all-gather.4.cloned.1.call-start = ((), (), s32[]{:S(2)}) async-start(), calls=%async_computation.2 | async-start | bytes 2359296 | tf_op jit(solution)/shard_map/all_gather | solution.py:259
  8.4 4.5 %collective-permute-start.1 = (bf16[32,4096]{1,0:T(8,128)(2,1)S(1)}, bf16[32,4096]{1,0:T(8,128)(2,1)S(1)}, u32[]{:S(2)}, u32[]{:S(2)}) collective-permute-start(bf16[32,4096]{1,0:T(8,128)(2,1)S(1)} %get-tuple-element.29), channel_id=1, source_target_pairs={{0,1},{1,0},{2,3},{3,2},{4,5},{5,4},{6,7},{7,6},{8,9},{9,8},{10,11... | collective-permute-start | bytes 786440 | tf_op jit(solution)/shard_map/ppermute | solution.py:31
  13.9 2.2 %copy-start = (bf16[256,8192]{1,0:T(8,128)(2,1)S(1)}, bf16[256,8192]{1,0:T(8,128)(2,1)}, u32[]{:S(2)}) copy-start(bf16[256,8192]{1,0:T(8,128)(2,1)} %li_ref) | copy-start | bytes 12582916
  19.9 3.0 %collective-permute-start.3 = (f32[16,16,1152]{2,1,0:T(8,128)S(1)}, f32[16,16,1152]{2,1,0:T(8,128)S(1)}, u32[]{:S(2)}, u32[]{:S(2)}) collective-permute-start(f32[16,16,1152]{2,1,0:T(8,128)S(1)} %get-tuple-element.16), channel_id=1, source_target_pairs={{0,1},{1,0},{2,3},{3,2},{4,5},{5,4},{6,7},{7,6},{8,9},{9,8},{10,11... | collective-permute-start | bytes 3538952 | tf_op jit(solution)/shard_map/ppermute | solution.py:31
  24.1 27.0 %all-to-all-start = ((f32[16,16,1152]{2,1,0:T(8,128)}), f32[16,16,1152]{2,1,0:T(8,128)S(1)}, u32[]{:S(2)}, u32[]{:S(2)}) async-start(f32[16,16,1152]{2,1,0:T(8,128)} %add.28), calls=%async_computation | async-start | bytes 2359296 | tf_op jit(solution)/shard_map/all_to_all | solution.py:258
  29.1 93.2 %all-gather.6.cloned.1.call-start = ((), (), s32[]{:S(2)}) async-start(), calls=%async_computation.3 | async-start | bytes 4718592 | tf_op jit(solution)/shard_map/all_gather | solution.py:263
  29.2 21.1 %collective-permute-start.2 = (bf16[64,2048]{1,0:T(8,128)(2,1)S(1)}, bf16[64,2048]{1,0:T(8,128)(2,1)S(1)}, u32[]{:S(2)}, u32[]{:S(2)}) collective-permute-start(bf16[64,2048]{1,0:T(8,128)(2,1)S(1)} %get-tuple-element.27), channel_id=1, source_target_pairs={{0,144},{144,0},{16,128},{128,16},{1,145},{145,1},{17,129},{129,17... | collective-permute-start | bytes 786440 | tf_op jit(solution)/shard_map/ppermute | solution.py:35
  52.3 62.8 %collective-permute-start.4 = (bf16[512,2048]{1,0:T(8,128)(2,1)}, bf16[512,2048]{1,0:T(8,128)(2,1)}, u32[]{:S(2)}, u32[]{:S(2)}) collective-permute-start(bf16[512,2048]{1,0:T(8,128)(2,1)} %all-gather.4.cloned.1.call-done.refs_0_), channel_id=1, source_target_pairs={{0,144},{144,0},{16,128},{128,16},{1,145},{145,1},{17,129},{129,17... | collective-permute-start | bytes 6291464 | tf_op jit(solution)/shard_map/ppermute | solution.py:35
  54.8 3.2 %collective-permute-start.7 = (f32[16,1152]{1,0:T(8,128)S(1)}, f32[16,1152]{1,0:T(8,128)S(1)}, u32[]{:S(2)}, u32[]{:S(2)}) collective-permute-start(f32[16,1152]{1,0:T(8,128)S(1)} %reduce_sum.9), channel_id=1, source_target_pairs={{0,2},{2,0},{4,6},{6,4},{8,10},{10,8},{12,14},{14,12},{1,3},{3,1},... | collective-permute-start | bytes 221192 | tf_op jit(solution)/shard_map/ppermute | solution.py:31
  58.1 5.4 %collective-permute-start.8 = (f32[16,1152]{1,0:T(8,128)S(1)}, f32[16,1152]{1,0:T(8,128)S(1)}, u32[]{:S(2)}, u32[]{:S(2)}) collective-permute-start(f32[16,1152]{1,0:T(8,128)S(1)} %add.31), channel_id=1, source_target_pairs={{0,4},{2,6},{4,0},{6,2},{8,12},{10,14},{12,8},{14,10},{1,5},{3,7},... | collective-permute-start | bytes 221192 | tf_op jit(solution)/shard_map/ppermute | solution.py:31
  63.5 8.0 %collective-permute-start.9 = (f32[16,1152]{1,0:T(8,128)S(1)}, f32[16,1152]{1,0:T(8,128)S(1)}, u32[]{:S(2)}, u32[]{:S(2)}) collective-permute-start(f32[16,1152]{1,0:T(8,128)S(1)} %add.32), channel_id=1, source_target_pairs={{0,8},{2,10},{4,12},{6,14},{8,0},{10,2},{12,4},{14,6},{1,9},{3,11}... | collective-permute-start | bytes 221192 | tf_op jit(solution)/shard_map/ppermute | solution.py:31
  72.6 35.8 %all-to-all-start.1 = ((f32[16,16,1152]{2,1,0:T(8,128)}), f32[16,16,1152]{2,1,0:T(8,128)S(1)}, u32[]{:S(2)}, u32[]{:S(2)}) async-start(f32[16,16,1152]{2,1,0:T(8,128)} %broadcast_in_dim.3), calls=%async_computation.1 | async-start | bytes 2359296 | tf_op jit(solution)/shard_map/all_to_all | solution.py:267
  77.0 13.0 %collective-permute-start = (bf16[256,1024]{1,0:T(8,128)(2,1)S(1)}, bf16[256,1024]{1,0:T(8,128)(2,1)S(1)}, u32[]{:S(2)}, u32[]{:S(2)}) collective-permute-start(bf16[256,1024]{1,0:T(8,128)(2,1)S(1)} %copy-done.2), channel_id=1, source_target_pairs={{0,1},{1,0},{2,3},{3,2},{4,5},{5,4},{6,7},{7,6},{8,9},{9,8},{10,11... | collective-permute-start | bytes 1572872 | tf_op jit(solution)/shard_map/ppermute | solution.py:31
  90.0 1.1 copy-start.4
  108.3 21.6 %collective-permute-start.10 = (f32[16,16,1152]{2,1,0:T(8,128)S(1)}, f32[16,16,1152]{2,1,0:T(8,128)S(1)}, u32[]{:S(2)}, u32[]{:S(2)}) collective-permute-start(f32[16,16,1152]{2,1,0:T(8,128)S(1)} %all-to-all-done.1.mine), channel_id=1, source_target_pairs={{0,1},{1,0},{2,3},{3,2},{4,5},{5,4},{6,7},{7,6},{8,9},{9,8},{10,11... | collective-permute-start | bytes 3538952 | tf_op jit(solution)/shard_map/ppermute | solution.py:31
  122.3 10.6 %collective-permute-start.6 = (bf16[256,2048]{1,0:T(8,128)(2,1)}, bf16[256,2048]{1,0:T(8,128)(2,1)S(1)}, u32[]{:S(2)}, u32[]{:S(2)}) collective-permute-start(bf16[256,2048]{1,0:T(8,128)(2,1)} %get-tuple-element.21), channel_id=1, source_target_pairs={{0,1},{1,0},{2,3},{3,2},{4,5},{5,4},{6,7},{7,6},{8,9},{9,8},{10,11... | collective-permute-start | bytes 3145736 | tf_op jit(solution)/shard_map/ppermute | solution.py:31
  129.4 4.5 %collective-permute-start.5 = (bf16[256,2048]{1,0:T(8,128)(2,1)}, bf16[256,2048]{1,0:T(8,128)(2,1)}, u32[]{:S(2)}, u32[]{:S(2)}) collective-permute-start(bf16[256,2048]{1,0:T(8,128)(2,1)} %get-tuple-element.20), channel_id=1, source_target_pairs={{0,1},{1,0},{2,3},{3,2},{4,5},{5,4},{6,7},{7,6},{8,9},{9,8},{10,11... | collective-permute-start | bytes 3145736 | tf_op jit(solution)/shard_map/ppermute | solution.py:31
Sparse Core Ops, SparseCore 0:
  13.9 38.3 all-gather.3
  54.1 58.9 all-gather.5

commit v3 on v2

--- a/solution.py
+++ b/solution.py
@@ -16,7 +16,6 @@
 HALF = D // 2
 UCOLS = 2048
 ZCOLS = HALF - UCOLS
-STEP = 512
 f32, bf16 = jnp.float32, jnp.bfloat16
 ANY = pl.BlockSpec(memory_space=pl.ANY)
 
@@ -57,27 +56,29 @@
     other_ref[...] = total[rows:]
 
 
-def product(at, x_hi, grads, pulled, down_t, weights, result=None):
-    tokens, n = grads.shape[0], weights[0].shape[-1]
+def product(ids, off, grads, pulled, down_t, weights, result=None, first=0, step=512):
+    tokens, n = grads.shape[0], weights[-1].shape[-1]
     whole = lambda a: pl.BlockSpec(a.shape, lambda i, at: (0,) * a.ndim)
     args = [grads, pulled, down_t, *weights] + ([] if result is None else [result])
-    weight_spec = lambda w: pl.BlockSpec((*w.shape[:-1], STEP), lambda i, at: (0,) * (w.ndim - 1) + (i,))
-    size = sum(w.size for w in weights)
+    block = lambda i, ids: (0, ids[0] * (HALF // step) + off // step + i)
+    weight_spec = lambda w: pl.BlockSpec(
+        (*w.shape[:-1], step), lambda i, at: (0,) * (w.ndim - 1) + (i + (first // step if w.shape[-1] > n else 0),)
+    )
     return pl.pallas_call(
         functools.partial(product_kernel, paired=len(weights) == 1),
         grid_spec=pltpu.PrefetchScalarGridSpec(
             num_scalar_prefetch=1,
-            grid=(n // STEP,),
+            grid=(n // step,),
             in_specs=[
                 whole(grads),
                 whole(pulled),
-                pl.BlockSpec((pulled.shape[1], STEP), lambda i, at: (0, at[0] + i)),
+                pl.BlockSpec((pulled.shape[1], step), block),
             ]
             + [weight_spec(w) for w in weights]
             + ([] if result is None else [ANY]),
             out_specs=[
-                pl.BlockSpec((tokens // 2, STEP), lambda i, at: (0, at[0] + i)),
-                pl.BlockSpec((tokens // 2, STEP), lambda i, at: (0, i)),
+                pl.BlockSpec((tokens // 2, step), block),
+                pl.BlockSpec((tokens // 2, step), lambda i, at: (0, i)),
             ],
         ),
         out_shape=[
@@ -86,41 +87,32 @@
         ],
         input_output_aliases={} if result is None else {len(args): 0},
         compiler_params=params(56),
-        cost_estimate=pl.CostEstimate(
-            flops=2 * tokens * size, bytes_accessed=2 * size + 2 * tokens * n, transcendentals=0
-        ),
-    )(jnp.stack([at // STEP, x_hi]), *args)
-
-
-def place_kernel(at_ref, piece, _, out, sems, *, parts):
-    step = piece.shape[1] // parts
-    copies = []
-    for k in range(parts):
-        there = pl.ds(pl.multiple_of(at_ref[k], 128), step)
-        source = piece.at[:, k * step : (k + 1) * step]
-        copies.append(pltpu.make_async_copy(source, out.at[:, there], sems.at[k]))
-    for copy in copies:
-        copy.start()
-    for copy in copies:
-        copy.wait()
-
-
-def place(at, piece, result):
-    parts = at.shape[0]
-    return pl.pallas_call(
-        functools.partial(place_kernel, parts=parts),
+        cost_estimate=pl.CostEstimate(flops=0, bytes_accessed=0, transcendentals=0),
+    )(ids, *args)
+
+
+def place_kernel(ids_ref, piece, _, out, sem, *, off):
+    there = pl.multiple_of((1 - ids_ref[0]) * HALF + off, 128)
+    copy = pltpu.make_async_copy(piece, out.at[:, pl.ds(there, piece.shape[1])], sem)
+    copy.start()
+    copy.wait()
+
+
+def place(ids, off, piece, result):
+    return pl.pallas_call(
+        functools.partial(place_kernel, off=off),
         grid_spec=pltpu.PrefetchScalarGridSpec(
             num_scalar_prefetch=1,
             grid=(1,),
-            in_specs=[pl.BlockSpec(piece.shape, lambda i, at: (0, 0)), ANY],
+            in_specs=[pl.BlockSpec(piece.shape, lambda i, ids: (0, 0)), ANY],
             out_specs=ANY,
-            scratch_shapes=[pltpu.SemaphoreType.DMA((parts,))],
+            scratch_shapes=[pltpu.SemaphoreType.DMA],
         ),
         out_shape=jax.ShapeDtypeStruct(result.shape, result.dtype),
         input_output_aliases={2: 0},
         compiler_params=params(),
-        cost_estimate=pl.CostEstimate(flops=0, bytes_accessed=4 * piece.size, transcendentals=0),
-    )(at, piece, result)
+        cost_estimate=pl.CostEstimate(flops=0, bytes_accessed=0, transcendentals=0),
+    )(ids, piece, result)
 
 
 def adapter_kernel(core_ref, li_ref, down_ref, vg_ref, up_ref, keep_ref, give_ref, proj, pulled, *, factor):
@@ -239,46 +231,53 @@
 
 
 def local(layer_input, value_grad, base_weight_t, adapter_down, adapter_up):
-    core, x_hi = lax.axis_index("core"), lax.axis_index("x_hi")
-    plane = ("x_lo", "y", "x_hi")
+    core, x_hi, z = (lax.axis_index(a) for a in ("core", "x_hi", "z"))
+    plane = ("x_lo", "y")
     tokens, features = value_grad.shape
     rank = adapter_up.shape[0]
     factor = adapter_scale / math.sqrt(tokens * math.prod(SIZES))
     down_t = adapter_down.T
+    ids = jnp.stack([core, x_hi])
 
     mine = lax.dynamic_slice_in_dim(base_weight_t, core * HALF, HALF, 1)
     give = lax.dynamic_slice_in_dim(base_weight_t, (1 - core) * HALF, HALF, 1)
     got = flip(give, "core", 1)
-    chip_rows = jnp.where(core == 0, jnp.concatenate([mine, got]), jnp.concatenate([got, mine]))
+    rows = lambda a, b: jnp.where(core == 0, jnp.concatenate([a, b]), jnp.concatenate([b, a]))
+    chip_rows = rows(mine[:, ZCOLS:], got[:, ZCOLS:])
 
     keep, give = adapter_parts(
-        core.reshape(1), after(layer_input, chip_rows), down_t, value_grad, adapter_up, factor
+        ids, after(layer_input, chip_rows), down_t, value_grad, adapter_up, factor
     )
     total = keep + flip(give, "core", 1)
-    total = lax.all_to_all(total, plane, 0, 0, tiled=True).sum(0)
-    near = lax.all_gather(chip_rows[:, ZCOLS:], "z", axis=0, tiled=True)
-    far = cross_x(after(near, total))
-    strip = chip_rows[:, :ZCOLS]
+    total = lax.all_to_all(total, plane, 0, 0, tiled=True).reshape(8, 2, *total.shape[1:]).sum(0)
+    total = total + flip(total, "x_hi", 1)
+    pick = lambda at: lax.dynamic_index_in_dim(total, at % 2, 0, False)
+    total = pick(z) + flip(pick(z + 1), "z", 1)
+    near = lax.all_gather(chip_rows, "z", axis=0, tiled=True)
+    near = after(near, total)
+    far = cross_x(near)
+    strip = rows(mine[:, :ZCOLS], got[:, :ZCOLS])
     strips = after(jnp.stack([strip, cross_x(strip)]), near, total)
     weight_z = lax.all_gather(strips, "z", axis=0, tiled=False)
 
-    for k in (1, 2, 4):
-        total = total + flip(total, "z", k)
-    half = lax.all_to_all(
-        jnp.broadcast_to(total, (16, *total.shape)), plane, 0, 0, tiled=True
-    )
-    down_grad_t, up_grad = finish(core.reshape(1), half, flip(half, "core", 1), rank, features)
-
+    total = total + flip(total, "z", 2)
+    total = total + flip(total, "z", 4)
+    both = flip(total, "z", 1)
+    total = jnp.where(z % 2 == 0, jnp.stack([total, both]), jnp.stack([both, total]))
     grads = jnp.concatenate([value_grad, flip(value_grad, "core", 1)], 0)
     pulled = lax.dot_general(
         grads, adapter_up, (((1,), (1,)), ((), ())), preferred_element_type=f32
     ).astype(bf16)
     pulled = (adapter_scale * pulled).astype(bf16)
-    result, send_u = product(core * HALF + ZCOLS, x_hi, grads, pulled, down_t, [near, far])
-    result, send_z = product(core * HALF, x_hi, grads, pulled, down_t, [weight_z], result)
-    base = (1 - core) * HALF
-    result = place((base + ZCOLS).reshape(1), flip(send_u, "core", 1), result)
-    result = place(base.reshape(1), flip(send_z, "core", 1), result)
+    half = lax.all_to_all(
+        jnp.broadcast_to(total, (8, *total.shape)).reshape(16, *total.shape[1:]), plane, 0, 0, tiled=True
+    )
+    result, send_u = product(ids, ZCOLS, grads, pulled, down_t, [near, far], step=1024)
+    half = after(half, send_u)
+    result, send_z = product(ids, 0, grads, pulled, down_t, [weight_z], result, step=1024)
+    result = place(ids, ZCOLS, flip(send_u, "core", 1), result)
+    result = place(ids, 0, flip(send_z, "core", 1), result)
+    down_grad_t, up_grad = finish(ids, half, flip(half, "core", 1), rank, features)
     return (result, down_grad_t.T, up_grad)
 
 

time: 143 us -> 136 us (0.951)
  starting transfers between devices: 43.3 us -> 37.5 us
  waiting for transfers between devices: 51.2 us -> 49.1 us
    ppermute x9 -> x11, waiting for transfers between devices: 14.3 us -> 21.1 us  [flip(): return lax.ppermute(x, axis, [(i, i ^ k) for i in range(n)])]
    ppermute x2, waiting for transfers between devices: 18.4 us -> 11.9 us  [cross_x(): return lax.ppermute(x, ('x_lo', 'x_hi'), [(0, 3), (3, 0), (1, 2), (2, 1)])]
    ppermute x9 -> x11, starting transfers between devices: 28.7 us -> 25.1 us  [flip(): return lax.ppermute(x, axis, [(i, i ^ k) for i in range(n)])]
    all_to_all x2, waiting for transfers between devices: 17.2 us -> 13.7 us  [the longest x1 13.7 us: local(): lax.all_to_all(total, plane, 0, 0, tiled=True)]
    all_gather x1, waiting for transfers between devices: 0.01 us -> 2.32 us  [local(): weight_z = lax.all_gather(strips, 'z', axis=0, tiled=False)]
    all_to_all x2, starting transfers between devices: 9.4 us -> 7.34 us  [the longest x1 3.78 us: local(): lax.all_to_all(jnp.broadcast_to(total, (8, *total.shape)).reshape(16, *to...]
  transfers between devices with their start and end apart: 15 -> 17, of which waited for: 9 -> 11; matrix products, arithmetic and copies ran while one was open for 4% -> 4% of each run, Pallas kernels for 15% -> 17%
where the time goes in v3:
time: 136 us; the launch traced here: 135 us
  waiting for transfers between devices  49.1 us (36%)
  starting transfers between devices  37.5 us (28%)
  Pallas kernels  24.9 us (18%)
  between operations  14.3 us (11%)
  local copies, waits for them, and re-layouts  5.5 us (4%)
  other arithmetic  3.11 us (2%)
    ppermute x11, starting transfers between devices, flip(): return lax.ppermute(x, axis, [(i, i ^ k) for i in range(n)])  25.1 us
    ppermute x11, waiting for transfers between devices, flip(): return lax.ppermute(x, axis, [(i, i ^ k) for i in range(n)])  21.1 us
    pallas_call x2, Pallas kernels, product(): pl.pallas_call(functools.partial(product_kernel, paired=len(weights) == 1...  13.8 us
    all_to_all x1, waiting for transfers between devices, local(): lax.all_to_all(total, plane, 0, 0, tiled=True)  13.7 us
    ppermute x2, waiting for transfers between devices, cross_x(): return lax.ppermute(x, ('x_lo', 'x_hi'), [(0, 3), (3, 0), (1, 2), (2, 1)])  11.9 us
    ppermute x2, starting transfers between devices, cross_x(): return lax.ppermute(x, ('x_lo', 'x_hi'), [(0, 3), (3, 0), (1, 2), (2, 1)])  4.94 us
    pallas_call x1, Pallas kernels, adapter_parts(): pl.pallas_call(functools.partial(adapter_kernel, factor=factor), grid_spe...  4.44 us
    all_to_all x1, starting transfers between devices, local(): lax.all_to_all(jnp.broadcast_to(total, (8, *total.shape)).reshape(16, *to...  3.78 us
  transfers between devices with their start and end apart: 17, of which 11 were waited for; matrix products, arithmetic and copies ran while one was open for 4% of the time, Pallas kernels for 17%

profile of v3, /device:TPU:1, one launch (start us, length us, event | category | flops | bytes accessed | tf_op | source)
XLA Modules:
  0.0 135.5 jit_solution(9506334390243644187)
XLA Ops:
  7.2 0.0 copy-start.2
  7.2 0.0 copy-start.3
  7.2 0.0 copy-start
  7.2 0.0 all-gather.4.cloned.1.call-start
  7.2 1.1 constant_dynamic-slice_fusion.1
  8.3 3.3 %collective-permute-start.1 = (bf16[32,4096]{1,0:T(8,128)(2,1)S(1)}, bf16[32,4096]{1,0:T(8,128)(2,1)S(1)}, u32[]{:S(2)}, u32[]{:S(2)}) collective-permute-start(bf16[32,4096]{1,0:T(8,128)(2,1)S(1)} %constant_dynamic-slice_fusion.1), channel_id=1, source_target_pairs={{0,1},{1,0},{2,3},{3,2},{4,5},{5,4},{6,7},{7,6},{8,9},{9,8},{10,11... | collective-permute-start | bytes 786440 | tf_op jit(solution)/shard_map/ppermute | solution.py:30
  11.7 1.0 constant_dynamic-slice_fusion.2
  12.7 0.2 collective-permute-done.1
  12.9 0.8 maximum_select_fusion.2
  13.6 0.0 all-gather.4.cloned.1.call-update
  13.6 0.1 pad_add_fusion.core_ref.at_ref.ids_ref
  13.7 0.0 copy-start.4
  13.7 0.0 copy-done.2
  13.7 0.0 copy-done.3
  13.7 0.0 copy-done
  13.7 0.0 copy-start.1
  13.7 2.2 %copy-done.1 = bf16[256,8192]{1,0:T(8,128)(2,1)S(1)} copy-done((bf16[256,8192]{1,0:T(8,128)(2,1)S(1)}, bf16[256,8192]{1,0:T(8,128)(2,1)}, u32[]{:S(2)}) %copy-start.1) | copy-done | bytes 4194328
  15.9 4.4 %shard_map.76 = (f32[16,16,1152]{2,1,0:T(8,128)S(1)}, f32[16,16,1152]{2,1,0:T(8,128)S(1)}) custom-call(s32[2]{0:T(128)S(1)} %pad_add_fusion.core_ref.at_ref.ids_ref, bf16[256,8192]{1,0:T(8,128)(2,1)S(1)} %copy-done.1, bf16[64,8192]{1,0:T(8,128)(2,1)S(1)} %bitcast.21, bf16[256,1024]{1,0:T(8,128)(2,1)S(1)} %copy-done.2, bf16[64,1024]{1,0:T(8,128)(2,1)S(1)} %copy-done.3), custom_call_target="tpu_custom_call" | custom-call | flops 536870912 | bytes 6291456 | tf_op jit(solution)/shard_map/pallas_call | solution.py:171
  20.4 0.0 copy-done.4
  20.4 0.5 collective-permute-start.3
  20.8 2.5 %collective-permute-done.3 = f32[16,16,1152]{2,1,0:T(8,128)S(1)} collective-permute-done((f32[16,16,1152]{2,1,0:T(8,128)S(1)}, f32[16,16,1152]{2,1,0:T(8,128)S(1)}, u32[]{:S(2)}, u32[]{:S(2)}) %collective-permute-start.3) | collective-permute-done | bytes 1179680 | tf_op jit(solution)/shard_map/ppermute | solution.py:30
  23.3 1.2 add.41
  24.5 3.6 %all-to-all-start = ((f32[16,16,1152]{2,1,0:T(8,128)}), f32[16,16,1152]{2,1,0:T(8,128)S(1)}, u32[]{:S(2)}, u32[]{:S(2)}) async-start(f32[16,16,1152]{2,1,0:T(8,128)} %add.41), calls=%async_computation | async-start | bytes 2359296 | tf_op jit(solution)/shard_map/all_to_all | solution.py:252
  28.1 0.0 all-gather.6.cloned.1.call-start
  28.2 2.6 %collective-permute-start.2 = (bf16[64,2048]{1,0:T(8,128)(2,1)S(1)}, bf16[64,2048]{1,0:T(8,128)(2,1)S(1)}, u32[]{:S(2)}, u32[]{:S(2)}) collective-permute-start(bf16[64,2048]{1,0:T(8,128)(2,1)S(1)} %maximum_select_fusion.1), channel_id=1, source_target_pairs={{0,144},{144,0},{16,128},{128,16},{1,145},{145,1},{17,129},{129,17... | collective-permute-start | bytes 786440 | tf_op jit(solution)/shard_map/ppermute | solution.py:34
  30.8 13.7 %all-to-all-done = f32[16,16,1152]{2,1,0:T(8,128)S(1)} async-done(((f32[16,16,1152]{2,1,0:T(8,128)}), f32[16,16,1152]{2,1,0:T(8,128)S(1)}, u32[]{:S(2)}, u32[]{:S(2)}) %all-to-all-start) | async-done | bytes 1179680 | tf_op jit(solution)/shard_map/all_to_all | solution.py:252
  44.5 0.1 reduce_sum.9
  44.6 2.3 %collective-permute-start.4 = (f32[2,16,1152]{2,1,0:T(8,128)S(1)}, f32[2,16,1152]{2,1,0:T(8,128)S(1)}, u32[]{:S(2)}, u32[]{:S(2)}) collective-permute-start(f32[2,16,1152]{2,1,0:T(8,128)S(1)} %reduce_sum.9), channel_id=1, source_target_pairs={{0,16},{16,0},{1,17},{17,1},{2,18},{18,2},{3,19},{19,3},{4,20},{20... | collective-permute-start | bytes 442376 | tf_op jit(solution)/shard_map/ppermute | solution.py:30
  46.9 3.9 %collective-permute-done.4 = f32[2,16,1152]{2,1,0:T(8,128)S(1)} collective-permute-done((f32[2,16,1152]{2,1,0:T(8,128)S(1)}, f32[2,16,1152]{2,1,0:T(8,128)S(1)}, u32[]{:S(2)}, u32[]{:S(2)}) %collective-permute-start.4) | collective-permute-done | bytes 147488 | tf_op jit(solution)/shard_map/ppermute | solution.py:30
  50.9 1.4 %collective-permute-start.5 = (f32[16,1152]{1,0:T(8,128)S(1)}, f32[16,1152]{1,0:T(8,128)S(1)}, u32[]{:S(2)}, u32[]{:S(2)}) collective-permute-start(f32[16,1152]{1,0:T(8,128)S(1)} %dynamic-slice_bitcast_fusion), channel_id=1, source_target_pairs={{0,2},{2,0},{4,6},{6,4},{8,10},{10,8},{12,14},{14,12},{1,3},{3,1},... | collective-permute-start | bytes 221192 | tf_op jit(solution)/shard_map/ppermute | solution.py:30
  52.3 0.0 collective-permute-done.2
  52.3 0.8 pad_maximum_fusion
  53.1 2.1 %collective-permute-done.5 = f32[16,1152]{1,0:T(8,128)S(1)} collective-permute-done((f32[16,1152]{1,0:T(8,128)S(1)}, f32[16,1152]{1,0:T(8,128)S(1)}, u32[]{:S(2)}, u32[]{:S(2)}) %collective-permute-start.5) | collective-permute-done | bytes 73760 | tf_op jit(solution)/shard_map/ppermute | solution.py:30
  55.2 0.0 all-gather.4.cloned.1.call-done.refs_0_
  55.2 0.0 all-gather.6.cloned.1.call-update
  55.3 2.4 %collective-permute-start.6 = (bf16[512,2048]{1,0:T(8,128)(2,1)}, bf16[512,2048]{1,0:T(8,128)(2,1)}, u32[]{:S(2)}, u32[]{:S(2)}) collective-permute-start(bf16[512,2048]{1,0:T(8,128)(2,1)} %all-gather.4.cloned.1.call-done.refs_0_), channel_id=1, source_target_pairs={{0,144},{144,0},{16,128},{128,16},{1,145},{145,1},{17,129},{129,17... | collective-permute-start | bytes 6291464 | tf_op jit(solution)/shard_map/ppermute | solution.py:34
  57.7 2.2 %collective-permute-start.9 = (f32[16,1152]{1,0:T(8,128)S(1)}, f32[16,1152]{1,0:T(8,128)S(1)}, u32[]{:S(2)}, u32[]{:S(2)}) collective-permute-start(f32[16,1152]{1,0:T(8,128)S(1)} %bitcast_add_fusion), channel_id=1, source_target_pairs={{0,4},{2,6},{4,0},{6,2},{8,12},{10,14},{12,8},{14,10},{1,5},{3,7},... | collective-permute-start | bytes 221192 | tf_op jit(solution)/shard_map/ppermute | solution.py:30
  59.9 2.3 %collective-permute-done.9 = f32[16,1152]{1,0:T(8,128)S(1)} collective-permute-done((f32[16,1152]{1,0:T(8,128)S(1)}, f32[16,1152]{1,0:T(8,128)S(1)}, u32[]{:S(2)}, u32[]{:S(2)}) %collective-permute-start.9) | collective-permute-done | bytes 73760 | tf_op jit(solution)/shard_map/ppermute | solution.py:30
  62.2 6.6 %collective-permute-start.10 = (f32[16,1152]{1,0:T(8,128)S(1)}, f32[16,1152]{1,0:T(8,128)S(1)}, u32[]{:S(2)}, u32[]{:S(2)}) collective-permute-start(f32[16,1152]{1,0:T(8,128)S(1)} %add.49), channel_id=1, source_target_pairs={{0,8},{2,10},{4,12},{6,14},{8,0},{10,2},{12,4},{14,6},{1,9},{3,11}... | collective-permute-start | bytes 221192 | tf_op jit(solution)/shard_map/ppermute | solution.py:30
  68.8 2.6 %collective-permute-done.10 = f32[16,1152]{1,0:T(8,128)S(1)} collective-permute-done((f32[16,1152]{1,0:T(8,128)S(1)}, f32[16,1152]{1,0:T(8,128)S(1)}, u32[]{:S(2)}, u32[]{:S(2)}) %collective-permute-start.10) | collective-permute-done | bytes 73760 | tf_op jit(solution)/shard_map/ppermute | solution.py:30
  71.4 0.2 collective-permute-start.11
  71.6 6.0 %collective-permute-done.11 = f32[16,1152]{1,0:T(8,128)S(1)} collective-permute-done((f32[16,1152]{1,0:T(8,128)S(1)}, f32[16,1152]{1,0:T(8,128)S(1)}, u32[]{:S(2)}, u32[]{:S(2)}) %collective-permute-start.11) | collective-permute-done | bytes 73760 | tf_op jit(solution)/shard_map/ppermute | solution.py:30
  77.6 1.1 broadcast_in_dim.3
  78.7 3.8 %all-to-all-start.1 = ((f32[16,16,1152]{2,1,0:T(8,128)}), f32[16,16,1152]{2,1,0:T(8,128)S(1)}, u32[]{:S(2)}, u32[]{:S(2)}) async-start(f32[16,16,1152]{2,1,0:T(8,128)} %bitcast.12), calls=%async_computation.1 | async-start | bytes 2359296 | tf_op jit(solution)/shard_map/all_to_all | solution.py:272
  82.5 5.2 %collective-permute-start = (bf16[256,1024]{1,0:T(8,128)(2,1)S(1)}, bf16[256,1024]{1,0:T(8,128)(2,1)S(1)}, u32[]{:S(2)}, u32[]{:S(2)}) collective-permute-start(bf16[256,1024]{1,0:T(8,128)(2,1)S(1)} %copy-done.2), channel_id=1, source_target_pairs={{0,1},{1,0},{2,3},{3,2},{4,5},{5,4},{6,7},{7,6},{8,9},{9,8},{10,11... | collective-permute-start | bytes 1572872 | tf_op jit(solution)/shard_map/ppermute | solution.py:30
  87.7 1.5 %collective-permute-done = bf16[256,1024]{1,0:T(8,128)(2,1)S(1)} collective-permute-done((bf16[256,1024]{1,0:T(8,128)(2,1)S(1)}, bf16[256,1024]{1,0:T(8,128)(2,1)S(1)}, u32[]{:S(2)}, u32[]{:S(2)}) %collective-permute-start) | collective-permute-done | bytes 524320 | tf_op jit(solution)/shard_map/ppermute | solution.py:30
  89.3 0.0 copy-start.6
  89.3 1.1 fusion.pulled
  90.4 11.9 %collective-permute-done.6.refs_1_ = bf16[512,2048]{1,0:T(8,128)(2,1)} collective-permute-done((bf16[512,2048]{1,0:T(8,128)(2,1)}, bf16[512,2048]{1,0:T(8,128)(2,1)}, u32[]{:S(2)}, u32[]{:S(2)}) %collective-permute-start.6) | collective-permute-done | bytes 2097184 | tf_op jit(solution)/shard_map/ppermute | solution.py:34
  102.3 0.0 copy-done.6
  102.3 7.0 %shard_map.77 = (bf16[256,8192]{1,0:T(8,128)(2,1)}, bf16[256,2048]{1,0:T(8,128)(2,1)}) custom-call(s32[2]{0:T(128)} %copy-done.4, bf16[512,1024]{1,0:T(8,128)(2,1)} %copy-done.6, bf16[512,64]{1,0:T(8,128)(2,1)} %fusion.pulled, bf16[64,8192]{1,0:T(8,128)(2,1)} %bitcast.19, bf16[512,2048]{1,0:T(8,128)(2,1)} %all-gather.4.cloned.1.call-done.refs_0_, ...), custom_call_target="tpu_custom_call" | custom-call | tf_op jit(solution)/shard_map/pallas_call | solution.py:67
  109.3 0.0 all-to-all-done.1.mine
  109.3 2.7 %collective-permute-start.12 = (f32[16,16,1152]{2,1,0:T(8,128)S(1)}, f32[16,16,1152]{2,1,0:T(8,128)S(1)}, u32[]{:S(2)}, u32[]{:S(2)}) collective-permute-start(f32[16,16,1152]{2,1,0:T(8,128)S(1)} %all-to-all-done.1.mine), channel_id=1, source_target_pairs={{0,1},{1,0},{2,3},{3,2},{4,5},{5,4},{6,7},{7,6},{8,9},{9,8},{10,11... | collective-permute-start | bytes 3538952 | tf_op jit(solution)/shard_map/ppermute | solution.py:30
  112.0 0.1 collective-permute-start.8
  112.1 2.3 %all-gather.6.cloned.1.call-done = bf16[16,64,2048]{2,1,0:T(8,128)(2,1)} async-done(((bf16[2,64,2048]{2,1,0:T(8,128)(2,1)}), bf16[16,64,2048]{2,1,0:T(8,128)(2,1)}) %all-gather.6.cloned.1.call-update) | async-done | bytes 4194320 | tf_op jit(solution)/shard_map/all_gather | solution.py:261
  114.5 6.8 %shard_map.78 = (bf16[256,8192]{1,0:T(8,128)(2,1)}, bf16[256,2048]{1,0:T(8,128)(2,1)}) custom-call(s32[2]{0:T(128)} %copy-done.4, bf16[512,1024]{1,0:T(8,128)(2,1)} %copy-done.6, bf16[512,64]{1,0:T(8,128)(2,1)} %fusion.pulled, bf16[64,8192]{1,0:T(8,128)(2,1)} %bitcast.20, bf16[8,2,64,2048]{3,2,1,0:T(8,128)(2,1)} %bitcast.23, ...), custom_call_target="tpu_custom_call", output_to_operand_aliasing={{0}: (5, {})} | custom-call | tf_op jit(solution)/shard_map/pallas_call | solution.py:67
  121.3 0.7 collective-permute-start.7
  121.9 0.0 collective-permute-done.12.other
  121.9 0.0 copy-done.5
  121.9 3.6 %shard_map.81 = (f32[64,8192]{1,0:T(8,128)}, f32[64,1024]{1,0:T(8,128)}) custom-call(s32[2]{0:T(128)S(1)} %copy-done.5, f32[16,16,1152]{2,1,0:T(8,128)S(1)} %all-to-all-done.1.mine, f32[16,16,1152]{2,1,0:T(8,128)S(1)} %collective-permute-done.12.other), custom_call_target="tpu_custom_call" | custom-call | bytes 2359296 | tf_op jit(solution)/shard_map/pallas_call | solution.py:213
  125.5 0.0 collective-permute-done.8.piece
  125.5 1.5 %shard_map.79._ = bf16[256,8192]{1,0:T(8,128)(2,1)} custom-call(s32[2]{0:T(128)S(1)} %copy-done.5, bf16[256,2048]{1,0:T(8,128)(2,1)S(1)} %collective-permute-done.8.piece, bf16[256,8192]{1,0:T(8,128)(2,1)} %get-tuple-element.23._), custom_call_target="tpu_custom_call", output_to_operand_aliasing={{}: (2, {})} | custom-call | tf_op jit(solution)/shard_map/pallas_call | solution.py:102
  127.1 0.0 collective-permute-done.7.piece
  127.1 1.5 %shard_map.80 = bf16[256,8192]{1,0:T(8,128)(2,1)} custom-call(s32[2]{0:T(128)S(1)} %copy-done.5, bf16[256,2048]{1,0:T(8,128)(2,1)S(1)} %collective-permute-done.7.piece, bf16[256,8192]{1,0:T(8,128)(2,1)} %shard_map.79._), custom_call_target="tpu_custom_call", output_to_operand_aliasing={{}: (2, {})} | custom-call | tf_op jit(solution)/shard_map/pallas_call | solution.py:102
  (12 shorter events, 0.3 us)
Async XLA Ops:
  7.2 6.6 %copy-start.2 = (bf16[256,1024]{1,0:T(8,128)(2,1)S(1)}, bf16[256,1024]{1,0:T(8,128)(2,1)}, u32[]{:S(2)}) copy-start(bf16[256,1024]{1,0:T(8,128)(2,1)} %vg_ref.1) | copy-start | bytes 1572868
  7.2 6.5 %copy-start.3 = (bf16[64,1024]{1,0:T(8,128)(2,1)S(1)}, bf16[64,1024]{1,0:T(8,128)(2,1)}, u32[]{:S(2)}) copy-start(bf16[64,1024]{1,0:T(8,128)(2,1)} %up_ref.1) | copy-start | bytes 393220
  7.2 6.5 %copy-start = (bf16[8192,64]{0,1:T(8,128)(2,1)S(1)}, bf16[8192,64]{0,1:T(8,128)(2,1)}, u32[]{:S(2)}) copy-start(bf16[8192,64]{0,1:T(8,128)(2,1)} %param.8) | copy-start | bytes 3145732
  7.2 48.0 %all-gather.4.cloned.1.call-start = ((), (), s32[]{:S(2)}) async-start(), calls=%async_computation.2 | async-start | bytes 2359296 | tf_op jit(solution)/shard_map/all_gather | solution.py:256
  8.3 4.5 %collective-permute-start.1 = (bf16[32,4096]{1,0:T(8,128)(2,1)S(1)}, bf16[32,4096]{1,0:T(8,128)(2,1)S(1)}, u32[]{:S(2)}, u32[]{:S(2)}) collective-permute-start(bf16[32,4096]{1,0:T(8,128)(2,1)S(1)} %constant_dynamic-slice_fusion.1), channel_id=1, source_target_pairs={{0,1},{1,0},{2,3},{3,2},{4,5},{5,4},{6,7},{7,6},{8,9},{9,8},{10,11... | collective-permute-start | bytes 786440 | tf_op jit(solution)/shard_map/ppermute | solution.py:30
  13.7 6.7 %copy-start.4 = (s32[2]{0:T(128)}, s32[2]{0:T(128)S(1)}, u32[]{:S(2)}) copy-start(s32[2]{0:T(128)S(1)} %pad_add_fusion.core_ref.at_ref.ids_ref) | copy-start | bytes 28
  13.7 2.2 %copy-start.1 = (bf16[256,8192]{1,0:T(8,128)(2,1)S(1)}, bf16[256,8192]{1,0:T(8,128)(2,1)}, u32[]{:S(2)}) copy-start(bf16[256,8192]{1,0:T(8,128)(2,1)} %li_ref) | copy-start | bytes 12582916
  20.4 2.9 %collective-permute-start.3 = (f32[16,16,1152]{2,1,0:T(8,128)S(1)}, f32[16,16,1152]{2,1,0:T(8,128)S(1)}, u32[]{:S(2)}, u32[]{:S(2)}) collective-permute-start(f32[16,16,1152]{2,1,0:T(8,128)S(1)} %get-tuple-element.17), channel_id=1, source_target_pairs={{0,1},{1,0},{2,3},{3,2},{4,5},{5,4},{6,7},{7,6},{8,9},{9,8},{10,11... | collective-permute-start | bytes 3538952 | tf_op jit(solution)/shard_map/ppermute | solution.py:30
  24.5 20.0 %all-to-all-start = ((f32[16,16,1152]{2,1,0:T(8,128)}), f32[16,16,1152]{2,1,0:T(8,128)S(1)}, u32[]{:S(2)}, u32[]{:S(2)}) async-start(f32[16,16,1152]{2,1,0:T(8,128)} %add.41), calls=%async_computation | async-start | bytes 2359296 | tf_op jit(solution)/shard_map/all_to_all | solution.py:252
  28.1 86.3 %all-gather.6.cloned.1.call-start = ((), (), s32[]{:S(2)}) async-start(), calls=%async_computation.3 | async-start | bytes 4718592 | tf_op jit(solution)/shard_map/all_gather | solution.py:261
  28.2 24.0 %collective-permute-start.2 = (bf16[64,2048]{1,0:T(8,128)(2,1)S(1)}, bf16[64,2048]{1,0:T(8,128)(2,1)S(1)}, u32[]{:S(2)}, u32[]{:S(2)}) collective-permute-start(bf16[64,2048]{1,0:T(8,128)(2,1)S(1)} %maximum_select_fusion.1), channel_id=1, source_target_pairs={{0,144},{144,0},{16,128},{128,16},{1,145},{145,1},{17,129},{129,17... | collective-permute-start | bytes 786440 | tf_op jit(solution)/shard_map/ppermute | solution.py:34
  44.6 6.3 %collective-permute-start.4 = (f32[2,16,1152]{2,1,0:T(8,128)S(1)}, f32[2,16,1152]{2,1,0:T(8,128)S(1)}, u32[]{:S(2)}, u32[]{:S(2)}) collective-permute-start(f32[2,16,1152]{2,1,0:T(8,128)S(1)} %reduce_sum.9), channel_id=1, source_target_pairs={{0,16},{16,0},{1,17},{17,1},{2,18},{18,2},{3,19},{19,3},{4,20},{20... | collective-permute-start | bytes 442376 | tf_op jit(solution)/shard_map/ppermute | solution.py:30
  50.9 4.3 %collective-permute-start.5 = (f32[16,1152]{1,0:T(8,128)S(1)}, f32[16,1152]{1,0:T(8,128)S(1)}, u32[]{:S(2)}, u32[]{:S(2)}) collective-permute-start(f32[16,1152]{1,0:T(8,128)S(1)} %dynamic-slice_bitcast_fusion), channel_id=1, source_target_pairs={{0,2},{2,0},{4,6},{6,4},{8,10},{10,8},{12,14},{14,12},{1,3},{3,1},... | collective-permute-start | bytes 221192 | tf_op jit(solution)/shard_map/ppermute | solution.py:30
  55.3 47.0 %collective-permute-start.6 = (bf16[512,2048]{1,0:T(8,128)(2,1)}, bf16[512,2048]{1,0:T(8,128)(2,1)}, u32[]{:S(2)}, u32[]{:S(2)}) collective-permute-start(bf16[512,2048]{1,0:T(8,128)(2,1)} %all-gather.4.cloned.1.call-done.refs_0_), channel_id=1, source_target_pairs={{0,144},{144,0},{16,128},{128,16},{1,145},{145,1},{17,129},{129,17... | collective-permute-start | bytes 6291464 | tf_op jit(solution)/shard_map/ppermute | solution.py:34
  57.7 4.5 %collective-permute-start.9 = (f32[16,1152]{1,0:T(8,128)S(1)}, f32[16,1152]{1,0:T(8,128)S(1)}, u32[]{:S(2)}, u32[]{:S(2)}) collective-permute-start(f32[16,1152]{1,0:T(8,128)S(1)} %bitcast_add_fusion), channel_id=1, source_target_pairs={{0,4},{2,6},{4,0},{6,2},{8,12},{10,14},{12,8},{14,10},{1,5},{3,7},... | collective-permute-start | bytes 221192 | tf_op jit(solution)/shard_map/ppermute | solution.py:30
  62.2 9.2 %collective-permute-start.10 = (f32[16,1152]{1,0:T(8,128)S(1)}, f32[16,1152]{1,0:T(8,128)S(1)}, u32[]{:S(2)}, u32[]{:S(2)}) collective-permute-start(f32[16,1152]{1,0:T(8,128)S(1)} %add.49), channel_id=1, source_target_pairs={{0,8},{2,10},{4,12},{6,14},{8,0},{10,2},{12,4},{14,6},{1,9},{3,11}... | collective-permute-start | bytes 221192 | tf_op jit(solution)/shard_map/ppermute | solution.py:30
  71.4 6.2 %collective-permute-start.11 = (f32[16,1152]{1,0:T(8,128)S(1)}, f32[16,1152]{1,0:T(8,128)S(1)}, u32[]{:S(2)}, u32[]{:S(2)}) collective-permute-start(f32[16,1152]{1,0:T(8,128)S(1)} %add.50), channel_id=1, source_target_pairs={{0,2},{2,0},{4,6},{6,4},{8,10},{10,8},{12,14},{14,12},{1,3},{3,1},... | collective-permute-start | bytes 221192 | tf_op jit(solution)/shard_map/ppermute | solution.py:30
  78.7 30.6 %all-to-all-start.1 = ((f32[16,16,1152]{2,1,0:T(8,128)}), f32[16,16,1152]{2,1,0:T(8,128)S(1)}, u32[]{:S(2)}, u32[]{:S(2)}) async-start(f32[16,16,1152]{2,1,0:T(8,128)} %bitcast.12), calls=%async_computation.1 | async-start | bytes 2359296 | tf_op jit(solution)/shard_map/all_to_all | solution.py:272
  82.5 6.8 %collective-permute-start = (bf16[256,1024]{1,0:T(8,128)(2,1)S(1)}, bf16[256,1024]{1,0:T(8,128)(2,1)S(1)}, u32[]{:S(2)}, u32[]{:S(2)}) collective-permute-start(bf16[256,1024]{1,0:T(8,128)(2,1)S(1)} %copy-done.2), channel_id=1, source_target_pairs={{0,1},{1,0},{2,3},{3,2},{4,5},{5,4},{6,7},{7,6},{8,9},{9,8},{10,11... | collective-permute-start | bytes 1572872 | tf_op jit(solution)/shard_map/ppermute | solution.py:30
  89.3 13.0 %copy-start.6 = (bf16[512,1024]{1,0:T(8,128)(2,1)}, bf16[512,1024]{1,0:T(8,128)(2,1)S(1)}, u32[]{:S(2)}) copy-start(bf16[512,1024]{1,0:T(8,128)(2,1)S(1)} %constant_dynamic-update-slice_fusion.grads) | copy-start | bytes 3145732
  109.3 12.6 %collective-permute-start.12 = (f32[16,16,1152]{2,1,0:T(8,128)S(1)}, f32[16,16,1152]{2,1,0:T(8,128)S(1)}, u32[]{:S(2)}, u32[]{:S(2)}) collective-permute-start(f32[16,16,1152]{2,1,0:T(8,128)S(1)} %all-to-all-done.1.mine), channel_id=1, source_target_pairs={{0,1},{1,0},{2,3},{3,2},{4,5},{5,4},{6,7},{7,6},{8,9},{9,8},{10,11... | collective-permute-start | bytes 3538952 | tf_op jit(solution)/shard_map/ppermute | solution.py:30
  112.0 13.5 %collective-permute-start.8 = (bf16[256,2048]{1,0:T(8,128)(2,1)}, bf16[256,2048]{1,0:T(8,128)(2,1)S(1)}, u32[]{:S(2)}, u32[]{:S(2)}) collective-permute-start(bf16[256,2048]{1,0:T(8,128)(2,1)} %get-tuple-element.22), channel_id=1, source_target_pairs={{0,1},{1,0},{2,3},{3,2},{4,5},{5,4},{6,7},{7,6},{8,9},{9,8},{10,11... | collective-permute-start | bytes 3145736 | tf_op jit(solution)/shard_map/ppermute | solution.py:30
  114.5 7.5 %copy-start.5 = (s32[2]{0:T(128)S(1)}, s32[2]{0:T(128)}, u32[]{:S(2)}) copy-start(s32[2]{0:T(128)} %copy-done.4) | copy-start | bytes 28
  121.3 5.8 %collective-permute-start.7 = (bf16[256,2048]{1,0:T(8,128)(2,1)}, bf16[256,2048]{1,0:T(8,128)(2,1)S(1)}, u32[]{:S(2)}, u32[]{:S(2)}) collective-permute-start(bf16[256,2048]{1,0:T(8,128)(2,1)} %get-tuple-element.21), channel_id=1, source_target_pairs={{0,1},{1,0},{2,3},{3,2},{4,5},{5,4},{6,7},{7,6},{8,9},{9,8},{10,11... | collective-permute-start | bytes 3145736 | tf_op jit(solution)/shard_map/ppermute | solution.py:30
Sparse Core Ops, SparseCore 0:
  13.8 38.3 all-gather.3
  55.4 59.0 all-gather.5

commit v4 on v3

--- a/solution.py
+++ b/solution.py
@@ -91,28 +91,24 @@
     )(ids, *args)
 
 
-def place_kernel(ids_ref, piece, _, out, sem, *, off):
-    there = pl.multiple_of((1 - ids_ref[0]) * HALF + off, 128)
+def place_kernel(piece, _, out, sem, *, off):
+    there = pl.multiple_of((1 - lax.axis_index("core")) * HALF + off, 128)
     copy = pltpu.make_async_copy(piece, out.at[:, pl.ds(there, piece.shape[1])], sem)
     copy.start()
     copy.wait()
 
 
-def place(ids, off, piece, result):
+def place(off, piece, result):
     return pl.pallas_call(
         functools.partial(place_kernel, off=off),
-        grid_spec=pltpu.PrefetchScalarGridSpec(
-            num_scalar_prefetch=1,
-            grid=(1,),
-            in_specs=[pl.BlockSpec(piece.shape, lambda i, ids: (0, 0)), ANY],
-            out_specs=ANY,
-            scratch_shapes=[pltpu.SemaphoreType.DMA],
-        ),
+        in_specs=[pl.BlockSpec(memory_space=pltpu.VMEM), ANY],
+        out_specs=ANY,
+        scratch_shapes=[pltpu.SemaphoreType.DMA],
         out_shape=jax.ShapeDtypeStruct(result.shape, result.dtype),
-        input_output_aliases={2: 0},
+        input_output_aliases={1: 0},
         compiler_params=params(),
         cost_estimate=pl.CostEstimate(flops=0, bytes_accessed=0, transcendentals=0),
-    )(ids, piece, result)
+    )(piece, result)
 
 
 def adapter_kernel(core_ref, li_ref, down_ref, vg_ref, up_ref, keep_ref, give_ref, proj, pulled, *, factor):
@@ -190,44 +186,37 @@
     )(core, li, down_t, vg, up)
 
 
-def finish_kernel(core_ref, mine, other, down_ref, up_ref, *, blocks):
-    i = pl.program_id(0)
-    step = down_ref.shape[1]
-    per = mine.shape[0] // blocks
-
-    def put(ref):
-        for b in range(blocks):
-            block = ref[b * per + i % per]
-            rows = block.shape[0]
-            down_ref[b * rows : (b + 1) * rows, :] = block[:, :step]
-            up_ref[b * rows : (b + 1) * rows, :] = block[:, step:]
-
-    pl.when(i < per)(lambda: put(mine))
-    pl.when(i >= per)(lambda: put(other))
-
-
-def finish(core, mine, other, rank, features, blocks=4, step=1024):
-    per = mine.shape[0] // blocks
-    whole = lambda a: pl.BlockSpec(a.shape, lambda i, c: (0,) * len(a.shape))
-    at = lambda i, c: jnp.where(i < per, c[0], 1 - c[0]) * per + i % per
-    return pl.pallas_call(
-        functools.partial(finish_kernel, blocks=blocks),
-        grid_spec=pltpu.PrefetchScalarGridSpec(
-            num_scalar_prefetch=1,
-            grid=(2 * per,),
-            in_specs=[whole(mine), whole(other)],
-            out_specs=[
-                pl.BlockSpec((rank, step), lambda i, c: (0, at(i, c))),
-                pl.BlockSpec((rank, features // 2 // per), lambda i, c: (0, at(i, c))),
-            ],
-        ),
-        out_shape=[
-            jax.ShapeDtypeStruct((rank, 2 * per * step), f32),
-            jax.ShapeDtypeStruct((rank, features), f32),
-        ],
+def finish_kernel(piece, *refs, other, blocks):
+    down, up, sems = refs[-3:]
+    half = lax.axis_index("core")
+    half = 1 - half if other else half
+    per, rows = piece.shape[0] // blocks, piece.shape[1]
+    step = down.shape[1] // 2 // per
+    width = piece.shape[2] - step
+    copies = []
+    for part in range(piece.shape[0]):
+        to = pl.ds(part // per * rows, rows)
+        for at, (out, n, first) in enumerate(((down, step, 0), (up, width, step))):
+            there = pl.ds(pl.multiple_of(half * (per * n) + part % per * n, 128), n)
+            source = piece.at[part, :, pl.ds(first, n)]
+            copies.append(pltpu.make_async_copy(source, out.at[to, there], sems.at[part, at]))
+    for copy in copies:
+        copy.start()
+    for copy in copies:
+        copy.wait()
+
+
+def finish(piece, rank, features, before=(), blocks=4):
+    return pl.pallas_call(
+        functools.partial(finish_kernel, other=bool(before), blocks=blocks),
+        in_specs=[pl.BlockSpec(memory_space=pltpu.VMEM)] + [ANY] * len(before),
+        out_specs=[ANY, ANY],
+        scratch_shapes=[pltpu.SemaphoreType.DMA((piece.shape[0], 2))],
+        out_shape=[jax.ShapeDtypeStruct((rank, D), f32), jax.ShapeDtypeStruct((rank, features), f32)],
+        input_output_aliases={1: 0, 2: 1} if before else {},
         compiler_params=params(),
-        cost_estimate=pl.CostEstimate(flops=0, bytes_accessed=8 * mine.size, transcendentals=0),
-    )(core, mine, other)
+        cost_estimate=pl.CostEstimate(flops=0, bytes_accessed=0, transcendentals=0),
+    )(piece, *before)
 
 
 def local(layer_input, value_grad, base_weight_t, adapter_down, adapter_up):
@@ -274,10 +263,11 @@
     )
     result, send_u = product(ids, ZCOLS, grads, pulled, down_t, [near, far], step=1024)
     half = after(half, send_u)
-    result, send_z = product(ids, 0, grads, pulled, down_t, [weight_z], result, step=1024)
-    result = place(ids, ZCOLS, flip(send_u, "core", 1), result)
-    result = place(ids, 0, flip(send_z, "core", 1), result)
-    down_grad_t, up_grad = finish(ids, half, flip(half, "core", 1), rank, features)
+    sums = finish(half, rank, features)
+    result, send_z = product(ids, 0, after(grads, *sums), pulled, down_t, [weight_z], result, step=1024)
+    result = place(ZCOLS, flip(send_u, "core", 1), result)
+    down_grad_t, up_grad = finish(flip(half, "core", 1), rank, features, sums)
+    result = place(0, flip(send_z, "core", 1), result)
     return (result, down_grad_t.T, up_grad)
 
 

time: 136 us -> 132 us (0.971)
  Pallas kernels: 24.9 us -> 22.6 us
    pallas_call x3 -> x4, Pallas kernels: 6.66 us -> 4.54 us  [the longest x2 2.57 us: finish(): pl.pallas_call(functools.partial(finish_kernel, other=bool(before), block...]
  transfers between devices with their start and end apart: 17 -> 17, of which waited for: 11 -> 12; matrix products, arithmetic and copies ran while one was open for 4% -> 4% of each run, Pallas kernels for 17% -> 16%
where the time goes in v4:
time: 132 us
  waiting for transfers between devices  48.1 us (36%)
  starting transfers between devices  37.5 us (28%)
  Pallas kernels  22.6 us (17%)
  between operations  14.3 us (11%)
  local copies, waits for them, and re-layouts  5.49 us (4%)
  other arithmetic  3.11 us (2%)
    ppermute x11, starting transfers between devices, flip(): return lax.ppermute(x, axis, [(i, i ^ k) for i in range(n)])  25.2 us
    ppermute x11, waiting for transfers between devices, flip(): return lax.ppermute(x, axis, [(i, i ^ k) for i in range(n)])  21.3 us
    all_to_all x1, waiting for transfers between devices, local(): lax.all_to_all(total, plane, 0, 0, tiled=True)  13.7 us
    pallas_call x2, Pallas kernels, product(): pl.pallas_call(functools.partial(product_kernel, paired=len(weights) == 1...  13.7 us
    ppermute x2, waiting for transfers between devices, cross_x(): return lax.ppermute(x, ('x_lo', 'x_hi'), [(0, 3), (3, 0), (1, 2), (2, 1)])  12 us
    ppermute x2, starting transfers between devices, cross_x(): return lax.ppermute(x, ('x_lo', 'x_hi'), [(0, 3), (3, 0), (1, 2), (2, 1)])  4.94 us
    pallas_call x1, Pallas kernels, adapter_parts(): pl.pallas_call(functools.partial(adapter_kernel, factor=factor), grid_spe...  4.44 us
    all_to_all x1, starting transfers between devices, local(): lax.all_to_all(jnp.broadcast_to(total, (8, *total.shape)).reshape(16, *to...  3.71 us
  transfers between devices with their start and end apart: 17, of which 12 were waited for; matrix products, arithmetic and copies ran while one was open for 4% of the time, Pallas kernels for 16%

profile of v4, /device:TPU:1, one launch (start us, length us, event | category | flops | bytes accessed | tf_op | source)
XLA Modules:
  0.0 132.1 jit_solution(17273486086963722580)
XLA Ops:
  7.2 0.0 copy-start
  7.2 0.0 copy-start.2
  7.2 0.0 copy-start.3
  7.2 0.0 all-gather.4.cloned.1.call-start
  7.2 1.1 constant_dynamic-slice_fusion.1
  8.3 3.3 %collective-permute-start.1 = (bf16[32,4096]{1,0:T(8,128)(2,1)S(1)}, bf16[32,4096]{1,0:T(8,128)(2,1)S(1)}, u32[]{:S(2)}, u32[]{:S(2)}) collective-permute-start(bf16[32,4096]{1,0:T(8,128)(2,1)S(1)} %constant_dynamic-slice_fusion.1), channel_id=1, source_target_pairs={{0,1},{1,0},{2,3},{3,2},{4,5},{5,4},{6,7},{7,6},{8,9},{9,8},{10,11... | collective-permute-start | bytes 786440 | tf_op jit(solution)/shard_map/ppermute | solution.py:30
  11.7 1.0 constant_dynamic-slice_fusion.2
  12.7 0.2 collective-permute-done.1
  12.9 0.8 maximum_select_fusion
  13.6 0.0 all-gather.4.cloned.1.call-update
  13.6 0.1 pad_add_fusion.core_ref.at_ref
  13.7 0.0 copy-start.4
  13.7 0.0 copy-done
  13.7 0.0 copy-done.2
  13.7 0.0 copy-done.3
  13.7 0.0 copy-start.1
  13.7 2.2 %copy-done.1 = bf16[256,8192]{1,0:T(8,128)(2,1)S(1)} copy-done((bf16[256,8192]{1,0:T(8,128)(2,1)S(1)}, bf16[256,8192]{1,0:T(8,128)(2,1)}, u32[]{:S(2)}) %copy-start.1) | copy-done | bytes 4194328
  15.9 4.4 %shard_map.76 = (f32[16,16,1152]{2,1,0:T(8,128)S(1)}, f32[16,16,1152]{2,1,0:T(8,128)S(1)}) custom-call(s32[2]{0:T(128)S(1)} %pad_add_fusion.core_ref.at_ref, bf16[256,8192]{1,0:T(8,128)(2,1)S(1)} %copy-done.1, bf16[64,8192]{1,0:T(8,128)(2,1)S(1)} %bitcast.21, bf16[256,1024]{1,0:T(8,128)(2,1)S(1)} %copy-done.2, bf16[64,1024]{1,0:T(8,128)(2,1)S(1)} %copy-done.3), custom_call_target="tpu_custom_call" | custom-call | flops 536870912 | bytes 6291456 | tf_op jit(solution)/shard_map/pallas_call | solution.py:167
  20.4 0.0 copy-done.4
  20.4 0.5 collective-permute-start.2
  20.8 2.5 %collective-permute-done.2 = f32[16,16,1152]{2,1,0:T(8,128)S(1)} collective-permute-done((f32[16,16,1152]{2,1,0:T(8,128)S(1)}, f32[16,16,1152]{2,1,0:T(8,128)S(1)}, u32[]{:S(2)}, u32[]{:S(2)}) %collective-permute-start.2) | collective-permute-done | bytes 1179680 | tf_op jit(solution)/shard_map/ppermute | solution.py:30
  23.3 1.2 add.42
  24.5 3.6 %all-to-all-start = ((f32[16,16,1152]{2,1,0:T(8,128)}), f32[16,16,1152]{2,1,0:T(8,128)S(1)}, u32[]{:S(2)}, u32[]{:S(2)}) async-start(f32[16,16,1152]{2,1,0:T(8,128)} %add.42), calls=%async_computation | async-start | bytes 2359296 | tf_op jit(solution)/shard_map/all_to_all | solution.py:241
  28.1 0.0 all-gather.6.cloned.1.call-start
  28.2 2.6 %collective-permute-start.9 = (bf16[64,2048]{1,0:T(8,128)(2,1)S(1)}, bf16[64,2048]{1,0:T(8,128)(2,1)S(1)}, u32[]{:S(2)}, u32[]{:S(2)}) collective-permute-start(bf16[64,2048]{1,0:T(8,128)(2,1)S(1)} %maximum_select_fusion.2), channel_id=1, source_target_pairs={{0,144},{144,0},{16,128},{128,16},{1,145},{145,1},{17,129},{129,17... | collective-permute-start | bytes 786440 | tf_op jit(solution)/shard_map/ppermute | solution.py:34
  30.8 13.7 %all-to-all-done = f32[16,16,1152]{2,1,0:T(8,128)S(1)} async-done(((f32[16,16,1152]{2,1,0:T(8,128)}), f32[16,16,1152]{2,1,0:T(8,128)S(1)}, u32[]{:S(2)}, u32[]{:S(2)}) %all-to-all-start) | async-done | bytes 1179680 | tf_op jit(solution)/shard_map/all_to_all | solution.py:241
  44.5 0.1 reduce_sum.9
  44.6 2.3 %collective-permute-start.3 = (f32[2,16,1152]{2,1,0:T(8,128)S(1)}, f32[2,16,1152]{2,1,0:T(8,128)S(1)}, u32[]{:S(2)}, u32[]{:S(2)}) collective-permute-start(f32[2,16,1152]{2,1,0:T(8,128)S(1)} %reduce_sum.9), channel_id=1, source_target_pairs={{0,16},{16,0},{1,17},{17,1},{2,18},{18,2},{3,19},{19,3},{4,20},{20... | collective-permute-start | bytes 442376 | tf_op jit(solution)/shard_map/ppermute | solution.py:30
  46.9 3.9 %collective-permute-done.3 = f32[2,16,1152]{2,1,0:T(8,128)S(1)} collective-permute-done((f32[2,16,1152]{2,1,0:T(8,128)S(1)}, f32[2,16,1152]{2,1,0:T(8,128)S(1)}, u32[]{:S(2)}, u32[]{:S(2)}) %collective-permute-start.3) | collective-permute-done | bytes 147488 | tf_op jit(solution)/shard_map/ppermute | solution.py:30
  50.9 1.4 %collective-permute-start.4 = (f32[16,1152]{1,0:T(8,128)S(1)}, f32[16,1152]{1,0:T(8,128)S(1)}, u32[]{:S(2)}, u32[]{:S(2)}) collective-permute-start(f32[16,1152]{1,0:T(8,128)S(1)} %dynamic-slice_bitcast_fusion), channel_id=1, source_target_pairs={{0,2},{2,0},{4,6},{6,4},{8,10},{10,8},{12,14},{14,12},{1,3},{3,1},... | collective-permute-start | bytes 221192 | tf_op jit(solution)/shard_map/ppermute | solution.py:30
  52.3 0.0 collective-permute-done.9
  52.3 0.8 pad_maximum_fusion
  53.1 2.1 %collective-permute-done.4 = f32[16,1152]{1,0:T(8,128)S(1)} collective-permute-done((f32[16,1152]{1,0:T(8,128)S(1)}, f32[16,1152]{1,0:T(8,128)S(1)}, u32[]{:S(2)}, u32[]{:S(2)}) %collective-permute-start.4) | collective-permute-done | bytes 73760 | tf_op jit(solution)/shard_map/ppermute | solution.py:30
  55.2 0.0 all-gather.4.cloned.1.call-done.refs_0_
  55.3 0.0 all-gather.6.cloned.1.call-update
  55.3 2.4 %collective-permute-start.8 = (bf16[512,2048]{1,0:T(8,128)(2,1)}, bf16[512,2048]{1,0:T(8,128)(2,1)}, u32[]{:S(2)}, u32[]{:S(2)}) collective-permute-start(bf16[512,2048]{1,0:T(8,128)(2,1)} %all-gather.4.cloned.1.call-done.refs_0_), channel_id=1, source_target_pairs={{0,144},{144,0},{16,128},{128,16},{1,145},{145,1},{17,129},{129,17... | collective-permute-start | bytes 6291464 | tf_op jit(solution)/shard_map/ppermute | solution.py:34
  57.7 2.2 %collective-permute-start.5 = (f32[16,1152]{1,0:T(8,128)S(1)}, f32[16,1152]{1,0:T(8,128)S(1)}, u32[]{:S(2)}, u32[]{:S(2)}) collective-permute-start(f32[16,1152]{1,0:T(8,128)S(1)} %bitcast_add_fusion), channel_id=1, source_target_pairs={{0,4},{2,6},{4,0},{6,2},{8,12},{10,14},{12,8},{14,10},{1,5},{3,7},... | collective-permute-start | bytes 221192 | tf_op jit(solution)/shard_map/ppermute | solution.py:30
  59.9 2.3 %collective-permute-done.5 = f32[16,1152]{1,0:T(8,128)S(1)} collective-permute-done((f32[16,1152]{1,0:T(8,128)S(1)}, f32[16,1152]{1,0:T(8,128)S(1)}, u32[]{:S(2)}, u32[]{:S(2)}) %collective-permute-start.5) | collective-permute-done | bytes 73760 | tf_op jit(solution)/shard_map/ppermute | solution.py:30
  62.2 6.6 %collective-permute-start.6 = (f32[16,1152]{1,0:T(8,128)S(1)}, f32[16,1152]{1,0:T(8,128)S(1)}, u32[]{:S(2)}, u32[]{:S(2)}) collective-permute-start(f32[16,1152]{1,0:T(8,128)S(1)} %add.49), channel_id=1, source_target_pairs={{0,8},{2,10},{4,12},{6,14},{8,0},{10,2},{12,4},{14,6},{1,9},{3,11}... | collective-permute-start | bytes 221192 | tf_op jit(solution)/shard_map/ppermute | solution.py:30
  68.8 2.6 %collective-permute-done.6 = f32[16,1152]{1,0:T(8,128)S(1)} collective-permute-done((f32[16,1152]{1,0:T(8,128)S(1)}, f32[16,1152]{1,0:T(8,128)S(1)}, u32[]{:S(2)}, u32[]{:S(2)}) %collective-permute-start.6) | collective-permute-done | bytes 73760 | tf_op jit(solution)/shard_map/ppermute | solution.py:30
  71.4 0.1 collective-permute-start.7
  71.6 6.0 %collective-permute-done.7 = f32[16,1152]{1,0:T(8,128)S(1)} collective-permute-done((f32[16,1152]{1,0:T(8,128)S(1)}, f32[16,1152]{1,0:T(8,128)S(1)}, u32[]{:S(2)}, u32[]{:S(2)}) %collective-permute-start.7) | collective-permute-done | bytes 73760 | tf_op jit(solution)/shard_map/ppermute | solution.py:30
  77.6 1.1 broadcast_in_dim.3
  78.7 3.7 %all-to-all-start.1 = ((f32[16,16,1152]{2,1,0:T(8,128)}), f32[16,16,1152]{2,1,0:T(8,128)S(1)}, u32[]{:S(2)}, u32[]{:S(2)}) async-start(f32[16,16,1152]{2,1,0:T(8,128)} %bitcast.8), calls=%async_computation.1 | async-start | bytes 2359296 | tf_op jit(solution)/shard_map/all_to_all | solution.py:261
  82.4 5.3 %collective-permute-start = (bf16[256,1024]{1,0:T(8,128)(2,1)S(1)}, bf16[256,1024]{1,0:T(8,128)(2,1)S(1)}, u32[]{:S(2)}, u32[]{:S(2)}) collective-permute-start(bf16[256,1024]{1,0:T(8,128)(2,1)S(1)} %copy-done.2), channel_id=1, source_target_pairs={{0,1},{1,0},{2,3},{3,2},{4,5},{5,4},{6,7},{7,6},{8,9},{9,8},{10,11... | collective-permute-start | bytes 1572872 | tf_op jit(solution)/shard_map/ppermute | solution.py:30
  87.7 1.5 %collective-permute-done = bf16[256,1024]{1,0:T(8,128)(2,1)S(1)} collective-permute-done((bf16[256,1024]{1,0:T(8,128)(2,1)S(1)}, bf16[256,1024]{1,0:T(8,128)(2,1)S(1)}, u32[]{:S(2)}, u32[]{:S(2)}) %collective-permute-start) | collective-permute-done | bytes 524320 | tf_op jit(solution)/shard_map/ppermute | solution.py:30
  89.3 0.0 copy-start.5
  89.3 1.1 fusion.pulled
  90.4 11.9 %collective-permute-done.8.refs_1_ = bf16[512,2048]{1,0:T(8,128)(2,1)} collective-permute-done((bf16[512,2048]{1,0:T(8,128)(2,1)}, bf16[512,2048]{1,0:T(8,128)(2,1)}, u32[]{:S(2)}, u32[]{:S(2)}) %collective-permute-start.8) | collective-permute-done | bytes 2097184 | tf_op jit(solution)/shard_map/ppermute | solution.py:34
  102.3 0.0 copy-done.5
  102.3 7.0 %shard_map.77 = (bf16[256,8192]{1,0:T(8,128)(2,1)}, bf16[256,2048]{1,0:T(8,128)(2,1)}) custom-call(s32[2]{0:T(128)} %copy-done.4, bf16[512,1024]{1,0:T(8,128)(2,1)} %copy-done.5, bf16[512,64]{1,0:T(8,128)(2,1)} %fusion.pulled, bf16[64,8192]{1,0:T(8,128)(2,1)} %bitcast.19, bf16[512,2048]{1,0:T(8,128)(2,1)} %all-gather.4.cloned.1.call-done.refs_0_, ...), custom_call_target="tpu_custom_call" | custom-call | tf_op jit(solution)/shard_map/pallas_call | solution.py:67
  109.3 0.0 all-to-all-done.1.piece
  109.3 2.7 %collective-permute-start.12 = (f32[16,16,1152]{2,1,0:T(8,128)S(1)}, f32[16,16,1152]{2,1,0:T(8,128)S(1)}, u32[]{:S(2)}, u32[]{:S(2)}) collective-permute-start(f32[16,16,1152]{2,1,0:T(8,128)S(1)} %all-to-all-done.1.piece), channel_id=1, source_target_pairs={{0,1},{1,0},{2,3},{3,2},{4,5},{5,4},{6,7},{7,6},{8,9},{9,8},{10,11... | collective-permute-start | bytes 3538952 | tf_op jit(solution)/shard_map/ppermute | solution.py:30
  112.0 1.3 shard_map.78
  113.3 0.1 collective-permute-start.11
  113.4 1.0 all-gather.6.cloned.1.call-done
  114.5 6.7 %shard_map.79 = (bf16[256,8192]{1,0:T(8,128)(2,1)}, bf16[256,2048]{1,0:T(8,128)(2,1)}) custom-call(s32[2]{0:T(128)} %copy-done.4, bf16[512,1024]{1,0:T(8,128)(2,1)} %copy-done.5, bf16[512,64]{1,0:T(8,128)(2,1)} %fusion.pulled, bf16[64,8192]{1,0:T(8,128)(2,1)} %bitcast.20, bf16[8,2,64,2048]{3,2,1,0:T(8,128)(2,1)} %bitcast.23, ...), custom_call_target="tpu_custom_call", output_to_operand_aliasing={{0}: (5, {})} | custom-call | tf_op jit(solution)/shard_map/pallas_call | solution.py:67
  121.1 0.7 collective-permute-start.10
  121.8 0.0 collective-permute-done.12.piece
  121.8 1.3 shard_map.82
  123.1 0.0 collective-permute-done.11.piece
  123.1 1.0 shard_map.80._
  124.1 0.2 collective-permute-done.10.piece
  124.3 1.0 shard_map.81
  (11 shorter events, 0.3 us)
Async XLA Ops:
  7.2 6.6 %copy-start = (bf16[8192,64]{0,1:T(8,128)(2,1)S(1)}, bf16[8192,64]{0,1:T(8,128)(2,1)}, u32[]{:S(2)}) copy-start(bf16[8192,64]{0,1:T(8,128)(2,1)} %param.8) | copy-start | bytes 3145732
  7.2 6.5 %copy-start.2 = (bf16[256,1024]{1,0:T(8,128)(2,1)S(1)}, bf16[256,1024]{1,0:T(8,128)(2,1)}, u32[]{:S(2)}) copy-start(bf16[256,1024]{1,0:T(8,128)(2,1)} %vg_ref.1) | copy-start | bytes 1572868
  7.2 6.5 %copy-start.3 = (bf16[64,1024]{1,0:T(8,128)(2,1)S(1)}, bf16[64,1024]{1,0:T(8,128)(2,1)}, u32[]{:S(2)}) copy-start(bf16[64,1024]{1,0:T(8,128)(2,1)} %up_ref.1) | copy-start | bytes 393220
  7.2 48.0 %all-gather.4.cloned.1.call-start = ((), (), s32[]{:S(2)}) async-start(), calls=%async_computation.2 | async-start | bytes 2359296 | tf_op jit(solution)/shard_map/all_gather | solution.py:245
  8.3 4.5 %collective-permute-start.1 = (bf16[32,4096]{1,0:T(8,128)(2,1)S(1)}, bf16[32,4096]{1,0:T(8,128)(2,1)S(1)}, u32[]{:S(2)}, u32[]{:S(2)}) collective-permute-start(bf16[32,4096]{1,0:T(8,128)(2,1)S(1)} %constant_dynamic-slice_fusion.1), channel_id=1, source_target_pairs={{0,1},{1,0},{2,3},{3,2},{4,5},{5,4},{6,7},{7,6},{8,9},{9,8},{10,11... | collective-permute-start | bytes 786440 | tf_op jit(solution)/shard_map/ppermute | solution.py:30
  13.7 6.7 %copy-start.4 = (s32[2]{0:T(128)}, s32[2]{0:T(128)S(1)}, u32[]{:S(2)}) copy-start(s32[2]{0:T(128)S(1)} %pad_add_fusion.core_ref.at_ref) | copy-start | bytes 28
  13.7 2.2 %copy-start.1 = (bf16[256,8192]{1,0:T(8,128)(2,1)S(1)}, bf16[256,8192]{1,0:T(8,128)(2,1)}, u32[]{:S(2)}) copy-start(bf16[256,8192]{1,0:T(8,128)(2,1)} %li_ref) | copy-start | bytes 12582916
  20.4 2.9 %collective-permute-start.2 = (f32[16,16,1152]{2,1,0:T(8,128)S(1)}, f32[16,16,1152]{2,1,0:T(8,128)S(1)}, u32[]{:S(2)}, u32[]{:S(2)}) collective-permute-start(f32[16,16,1152]{2,1,0:T(8,128)S(1)} %get-tuple-element.20), channel_id=1, source_target_pairs={{0,1},{1,0},{2,3},{3,2},{4,5},{5,4},{6,7},{7,6},{8,9},{9,8},{10,11... | collective-permute-start | bytes 3538952 | tf_op jit(solution)/shard_map/ppermute | solution.py:30
  24.5 20.0 %all-to-all-start = ((f32[16,16,1152]{2,1,0:T(8,128)}), f32[16,16,1152]{2,1,0:T(8,128)S(1)}, u32[]{:S(2)}, u32[]{:S(2)}) async-start(f32[16,16,1152]{2,1,0:T(8,128)} %add.42), calls=%async_computation | async-start | bytes 2359296 | tf_op jit(solution)/shard_map/all_to_all | solution.py:241
  28.1 86.4 %all-gather.6.cloned.1.call-start = ((), (), s32[]{:S(2)}) async-start(), calls=%async_computation.3 | async-start | bytes 4718592 | tf_op jit(solution)/shard_map/all_gather | solution.py:250
  28.2 24.0 %collective-permute-start.9 = (bf16[64,2048]{1,0:T(8,128)(2,1)S(1)}, bf16[64,2048]{1,0:T(8,128)(2,1)S(1)}, u32[]{:S(2)}, u32[]{:S(2)}) collective-permute-start(bf16[64,2048]{1,0:T(8,128)(2,1)S(1)} %maximum_select_fusion.2), channel_id=1, source_target_pairs={{0,144},{144,0},{16,128},{128,16},{1,145},{145,1},{17,129},{129,17... | collective-permute-start | bytes 786440 | tf_op jit(solution)/shard_map/ppermute | solution.py:34
  44.6 6.3 %collective-permute-start.3 = (f32[2,16,1152]{2,1,0:T(8,128)S(1)}, f32[2,16,1152]{2,1,0:T(8,128)S(1)}, u32[]{:S(2)}, u32[]{:S(2)}) collective-permute-start(f32[2,16,1152]{2,1,0:T(8,128)S(1)} %reduce_sum.9), channel_id=1, source_target_pairs={{0,16},{16,0},{1,17},{17,1},{2,18},{18,2},{3,19},{19,3},{4,20},{20... | collective-permute-start | bytes 442376 | tf_op jit(solution)/shard_map/ppermute | solution.py:30
  50.9 4.3 %collective-permute-start.4 = (f32[16,1152]{1,0:T(8,128)S(1)}, f32[16,1152]{1,0:T(8,128)S(1)}, u32[]{:S(2)}, u32[]{:S(2)}) collective-permute-start(f32[16,1152]{1,0:T(8,128)S(1)} %dynamic-slice_bitcast_fusion), channel_id=1, source_target_pairs={{0,2},{2,0},{4,6},{6,4},{8,10},{10,8},{12,14},{14,12},{1,3},{3,1},... | collective-permute-start | bytes 221192 | tf_op jit(solution)/shard_map/ppermute | solution.py:30
  55.3 47.0 %collective-permute-start.8 = (bf16[512,2048]{1,0:T(8,128)(2,1)}, bf16[512,2048]{1,0:T(8,128)(2,1)}, u32[]{:S(2)}, u32[]{:S(2)}) collective-permute-start(bf16[512,2048]{1,0:T(8,128)(2,1)} %all-gather.4.cloned.1.call-done.refs_0_), channel_id=1, source_target_pairs={{0,144},{144,0},{16,128},{128,16},{1,145},{145,1},{17,129},{129,17... | collective-permute-start | bytes 6291464 | tf_op jit(solution)/shard_map/ppermute | solution.py:34
  57.7 4.5 %collective-permute-start.5 = (f32[16,1152]{1,0:T(8,128)S(1)}, f32[16,1152]{1,0:T(8,128)S(1)}, u32[]{:S(2)}, u32[]{:S(2)}) collective-permute-start(f32[16,1152]{1,0:T(8,128)S(1)} %bitcast_add_fusion), channel_id=1, source_target_pairs={{0,4},{2,6},{4,0},{6,2},{8,12},{10,14},{12,8},{14,10},{1,5},{3,7},... | collective-permute-start | bytes 221192 | tf_op jit(solution)/shard_map/ppermute | solution.py:30
  62.2 9.2 %collective-permute-start.6 = (f32[16,1152]{1,0:T(8,128)S(1)}, f32[16,1152]{1,0:T(8,128)S(1)}, u32[]{:S(2)}, u32[]{:S(2)}) collective-permute-start(f32[16,1152]{1,0:T(8,128)S(1)} %add.49), channel_id=1, source_target_pairs={{0,8},{2,10},{4,12},{6,14},{8,0},{10,2},{12,4},{14,6},{1,9},{3,11}... | collective-permute-start | bytes 221192 | tf_op jit(solution)/shard_map/ppermute | solution.py:30
  71.4 6.2 %collective-permute-start.7 = (f32[16,1152]{1,0:T(8,128)S(1)}, f32[16,1152]{1,0:T(8,128)S(1)}, u32[]{:S(2)}, u32[]{:S(2)}) collective-permute-start(f32[16,1152]{1,0:T(8,128)S(1)} %add.50), channel_id=1, source_target_pairs={{0,2},{2,0},{4,6},{6,4},{8,10},{10,8},{12,14},{14,12},{1,3},{3,1},... | collective-permute-start | bytes 221192 | tf_op jit(solution)/shard_map/ppermute | solution.py:30
  78.7 30.6 %all-to-all-start.1 = ((f32[16,16,1152]{2,1,0:T(8,128)}), f32[16,16,1152]{2,1,0:T(8,128)S(1)}, u32[]{:S(2)}, u32[]{:S(2)}) async-start(f32[16,16,1152]{2,1,0:T(8,128)} %bitcast.8), calls=%async_computation.1 | async-start | bytes 2359296 | tf_op jit(solution)/shard_map/all_to_all | solution.py:261
  82.4 6.8 %collective-permute-start = (bf16[256,1024]{1,0:T(8,128)(2,1)S(1)}, bf16[256,1024]{1,0:T(8,128)(2,1)S(1)}, u32[]{:S(2)}, u32[]{:S(2)}) collective-permute-start(bf16[256,1024]{1,0:T(8,128)(2,1)S(1)} %copy-done.2), channel_id=1, source_target_pairs={{0,1},{1,0},{2,3},{3,2},{4,5},{5,4},{6,7},{7,6},{8,9},{9,8},{10,11... | collective-permute-start | bytes 1572872 | tf_op jit(solution)/shard_map/ppermute | solution.py:30
  89.3 13.0 %copy-start.5 = (bf16[512,1024]{1,0:T(8,128)(2,1)}, bf16[512,1024]{1,0:T(8,128)(2,1)S(1)}, u32[]{:S(2)}) copy-start(bf16[512,1024]{1,0:T(8,128)(2,1)S(1)} %constant_dynamic-update-slice_fusion.grads) | copy-start | bytes 3145732
  109.3 12.5 %collective-permute-start.12 = (f32[16,16,1152]{2,1,0:T(8,128)S(1)}, f32[16,16,1152]{2,1,0:T(8,128)S(1)}, u32[]{:S(2)}, u32[]{:S(2)}) collective-permute-start(f32[16,16,1152]{2,1,0:T(8,128)S(1)} %all-to-all-done.1.piece), channel_id=1, source_target_pairs={{0,1},{1,0},{2,3},{3,2},{4,5},{5,4},{6,7},{7,6},{8,9},{9,8},{10,11... | collective-permute-start | bytes 3538952 | tf_op jit(solution)/shard_map/ppermute | solution.py:30
  113.3 9.8 %collective-permute-start.11 = (bf16[256,2048]{1,0:T(8,128)(2,1)}, bf16[256,2048]{1,0:T(8,128)(2,1)S(1)}, u32[]{:S(2)}, u32[]{:S(2)}) collective-permute-start(bf16[256,2048]{1,0:T(8,128)(2,1)} %get-tuple-element.22), channel_id=1, source_target_pairs={{0,1},{1,0},{2,3},{3,2},{4,5},{5,4},{6,7},{7,6},{8,9},{9,8},{10,11... | collective-permute-start | bytes 3145736 | tf_op jit(solution)/shard_map/ppermute | solution.py:30
  121.1 3.2 %collective-permute-start.10 = (bf16[256,2048]{1,0:T(8,128)(2,1)}, bf16[256,2048]{1,0:T(8,128)(2,1)S(1)}, u32[]{:S(2)}, u32[]{:S(2)}) collective-permute-start(bf16[256,2048]{1,0:T(8,128)(2,1)} %get-tuple-element.29), channel_id=1, source_target_pairs={{0,1},{1,0},{2,3},{3,2},{4,5},{5,4},{6,7},{7,6},{8,9},{9,8},{10,11... | collective-permute-start | bytes 3145736 | tf_op jit(solution)/shard_map/ppermute | solution.py:30
Sparse Core Ops, SparseCore 0:
  13.8 38.3 all-gather.3
  55.4 59.0 all-gather.5

commit v5 on v4

--- a/solution.py
+++ b/solution.py
@@ -239,9 +239,9 @@
     )
     total = keep + flip(give, "core", 1)
     total = lax.all_to_all(total, plane, 0, 0, tiled=True).reshape(8, 2, *total.shape[1:]).sum(0)
-    total = total + flip(total, "x_hi", 1)
     pick = lambda at: lax.dynamic_index_in_dim(total, at % 2, 0, False)
     total = pick(z) + flip(pick(z + 1), "z", 1)
+    total = total + flip(total, "x_hi", 1)
     near = lax.all_gather(chip_rows, "z", axis=0, tiled=True)
     near = after(near, total)
     far = cross_x(near)

time: 132 us -> 132 us (level)
  waiting for transfers between devices: 48.1 us -> 45.5 us
  starting transfers between devices: 37.5 us -> 39.5 us
    ppermute x2, waiting for transfers between devices: 12 us -> 9.61 us  [cross_x(): return lax.ppermute(x, ('x_lo', 'x_hi'), [(0, 3), (3, 0), (1, 2), (2, 1)])]
    ppermute x11, starting transfers between devices: 25.2 us -> 27.3 us  [flip(): return lax.ppermute(x, axis, [(i, i ^ k) for i in range(n)])]
where the time goes in v5:
time: 132 us
  waiting for transfers between devices  45.5 us (34%)
  starting transfers between devices  39.5 us (30%)
  Pallas kernels  22.6 us (17%)
  between operations  14.3 us (11%)
  local copies, waits for them, and re-layouts  5.49 us (4%)
  other arithmetic  3.11 us (2%)
    ppermute x11, starting transfers between devices, flip(): return lax.ppermute(x, axis, [(i, i ^ k) for i in range(n)])  27.3 us
    ppermute x11, waiting for transfers between devices, flip(): return lax.ppermute(x, axis, [(i, i ^ k) for i in range(n)])  20.5 us
    all_to_all x1, waiting for transfers between devices, local(): lax.all_to_all(total, plane, 0, 0, tiled=True)  13.7 us
    pallas_call x2, Pallas kernels, product(): pl.pallas_call(functools.partial(product_kernel, paired=len(weights) == 1...  13.7 us
    ppermute x2, waiting for transfers between devices, cross_x(): return lax.ppermute(x, ('x_lo', 'x_hi'), [(0, 3), (3, 0), (1, 2), (2, 1)])  9.61 us
    ppermute x2, starting transfers between devices, cross_x(): return lax.ppermute(x, ('x_lo', 'x_hi'), [(0, 3), (3, 0), (1, 2), (2, 1)])  5.07 us
    pallas_call x1, Pallas kernels, adapter_parts(): pl.pallas_call(functools.partial(adapter_kernel, factor=factor), grid_spe...  4.44 us
    all_to_all x1, starting transfers between devices, local(): lax.all_to_all(total, plane, 0, 0, tiled=True)  3.56 us
  transfers between devices with their start and end apart: 17, of which 12 were waited for; matrix products, arithmetic and copies ran while one was open for 4% of the time, Pallas kernels for 16%

profile of v5, /device:TPU:1, one launch (start us, length us, event | category | flops | bytes accessed | tf_op | source)
XLA Modules:
  0.0 131.7 jit_solution(2492391897795697408)
XLA Ops:
  7.2 0.0 copy-start
  7.2 0.0 copy-start.2
  7.2 0.0 copy-start.3
  7.2 0.0 all-gather.4.cloned.1.call-start
  7.2 1.1 constant_dynamic-slice_fusion.1
  8.3 3.3 %collective-permute-start.1 = (bf16[32,4096]{1,0:T(8,128)(2,1)S(1)}, bf16[32,4096]{1,0:T(8,128)(2,1)S(1)}, u32[]{:S(2)}, u32[]{:S(2)}) collective-permute-start(bf16[32,4096]{1,0:T(8,128)(2,1)S(1)} %constant_dynamic-slice_fusion.1), channel_id=1, source_target_pairs={{0,1},{1,0},{2,3},{3,2},{4,5},{5,4},{6,7},{7,6},{8,9},{9,8},{10,11... | collective-permute-start | bytes 786440 | tf_op jit(solution)/shard_map/ppermute | solution.py:30
  11.7 1.0 constant_dynamic-slice_fusion.2
  12.7 0.2 collective-permute-done.1
  12.9 0.8 maximum_select_fusion
  13.6 0.0 all-gather.4.cloned.1.call-update
  13.6 0.1 pad_add_fusion.core_ref.at_ref
  13.7 0.0 copy-start.4
  13.7 0.0 copy-done
  13.7 0.0 copy-done.2
  13.7 0.0 copy-done.3
  13.7 0.0 copy-start.1
  13.7 2.2 %copy-done.1 = bf16[256,8192]{1,0:T(8,128)(2,1)S(1)} copy-done((bf16[256,8192]{1,0:T(8,128)(2,1)S(1)}, bf16[256,8192]{1,0:T(8,128)(2,1)}, u32[]{:S(2)}) %copy-start.1) | copy-done | bytes 4194328
  15.9 4.4 %shard_map.76 = (f32[16,16,1152]{2,1,0:T(8,128)S(1)}, f32[16,16,1152]{2,1,0:T(8,128)S(1)}) custom-call(s32[2]{0:T(128)S(1)} %pad_add_fusion.core_ref.at_ref, bf16[256,8192]{1,0:T(8,128)(2,1)S(1)} %copy-done.1, bf16[64,8192]{1,0:T(8,128)(2,1)S(1)} %bitcast.21, bf16[256,1024]{1,0:T(8,128)(2,1)S(1)} %copy-done.2, bf16[64,1024]{1,0:T(8,128)(2,1)S(1)} %copy-done.3), custom_call_target="tpu_custom_call" | custom-call | flops 536870912 | bytes 6291456 | tf_op jit(solution)/shard_map/pallas_call | solution.py:167
  20.4 0.0 copy-done.4
  20.4 0.5 collective-permute-start.2
  20.8 2.5 %collective-permute-done.2 = f32[16,16,1152]{2,1,0:T(8,128)S(1)} collective-permute-done((f32[16,16,1152]{2,1,0:T(8,128)S(1)}, f32[16,16,1152]{2,1,0:T(8,128)S(1)}, u32[]{:S(2)}, u32[]{:S(2)}) %collective-permute-start.2) | collective-permute-done | bytes 1179680 | tf_op jit(solution)/shard_map/ppermute | solution.py:30
  23.3 1.2 add.42
  24.5 3.6 %all-to-all-start = ((f32[16,16,1152]{2,1,0:T(8,128)}), f32[16,16,1152]{2,1,0:T(8,128)S(1)}, u32[]{:S(2)}, u32[]{:S(2)}) async-start(f32[16,16,1152]{2,1,0:T(8,128)} %add.42), calls=%async_computation | async-start | bytes 2359296 | tf_op jit(solution)/shard_map/all_to_all | solution.py:241
  28.1 0.0 all-gather.6.cloned.1.call-start
  28.2 2.6 %collective-permute-start.9 = (bf16[64,2048]{1,0:T(8,128)(2,1)S(1)}, bf16[64,2048]{1,0:T(8,128)(2,1)S(1)}, u32[]{:S(2)}, u32[]{:S(2)}) collective-permute-start(bf16[64,2048]{1,0:T(8,128)(2,1)S(1)} %maximum_select_fusion.2), channel_id=1, source_target_pairs={{0,144},{144,0},{16,128},{128,16},{1,145},{145,1},{17,129},{129,17... | collective-permute-start | bytes 786440 | tf_op jit(solution)/shard_map/ppermute | solution.py:34
  30.8 13.7 %all-to-all-done = f32[16,16,1152]{2,1,0:T(8,128)S(1)} async-done(((f32[16,16,1152]{2,1,0:T(8,128)}), f32[16,16,1152]{2,1,0:T(8,128)S(1)}, u32[]{:S(2)}, u32[]{:S(2)}) %all-to-all-start) | async-done | bytes 1179680 | tf_op jit(solution)/shard_map/all_to_all | solution.py:241
  44.5 0.1 reduce_sum.9
  44.6 1.5 %collective-permute-start.3 = (f32[16,1152]{1,0:T(8,128)S(1)}, f32[16,1152]{1,0:T(8,128)S(1)}, u32[]{:S(2)}, u32[]{:S(2)}) collective-permute-start(f32[16,1152]{1,0:T(8,128)S(1)} %dynamic-slice_bitcast_fusion), channel_id=1, source_target_pairs={{0,2},{2,0},{4,6},{6,4},{8,10},{10,8},{12,14},{14,12},{1,3},{3,1},... | collective-permute-start | bytes 221192 | tf_op jit(solution)/shard_map/ppermute | solution.py:30
  46.2 3.3 %collective-permute-done.3 = f32[16,1152]{1,0:T(8,128)S(1)} collective-permute-done((f32[16,1152]{1,0:T(8,128)S(1)}, f32[16,1152]{1,0:T(8,128)S(1)}, u32[]{:S(2)}, u32[]{:S(2)}) %collective-permute-start.3) | collective-permute-done | bytes 73760 | tf_op jit(solution)/shard_map/ppermute | solution.py:30
  49.4 3.1 %collective-permute-start.4 = (f32[16,1152]{1,0:T(8,128)S(1)}, f32[16,1152]{1,0:T(8,128)S(1)}, u32[]{:S(2)}, u32[]{:S(2)}) collective-permute-start(f32[16,1152]{1,0:T(8,128)S(1)} %bitcast_add_fusion), channel_id=1, source_target_pairs={{0,16},{16,0},{1,17},{17,1},{2,18},{18,2},{3,19},{19,3},{4,20},{20... | collective-permute-start | bytes 221192 | tf_op jit(solution)/shard_map/ppermute | solution.py:30
  52.5 0.0 collective-permute-done.9
  52.5 0.8 pad_maximum_fusion
  53.4 0.9 collective-permute-done.4
  54.3 0.0 all-gather.4.cloned.1.call-done.refs_0_
  54.3 0.0 all-gather.6.cloned.1.call-update
  54.3 2.5 %collective-permute-start.8 = (bf16[512,2048]{1,0:T(8,128)(2,1)}, bf16[512,2048]{1,0:T(8,128)(2,1)}, u32[]{:S(2)}, u32[]{:S(2)}) collective-permute-start(bf16[512,2048]{1,0:T(8,128)(2,1)} %all-gather.4.cloned.1.call-done.refs_0_), channel_id=1, source_target_pairs={{0,144},{144,0},{16,128},{128,16},{1,145},{145,1},{17,129},{129,17... | collective-permute-start | bytes 6291464 | tf_op jit(solution)/shard_map/ppermute | solution.py:34
  56.8 3.7 %collective-permute-start.5 = (f32[16,1152]{1,0:T(8,128)S(1)}, f32[16,1152]{1,0:T(8,128)S(1)}, u32[]{:S(2)}, u32[]{:S(2)}) collective-permute-start(f32[16,1152]{1,0:T(8,128)S(1)} %add.48), channel_id=1, source_target_pairs={{0,4},{2,6},{4,0},{6,2},{8,12},{10,14},{12,8},{14,10},{1,5},{3,7},... | collective-permute-start | bytes 221192 | tf_op jit(solution)/shard_map/ppermute | solution.py:30
  60.5 2.1 %collective-permute-done.5 = f32[16,1152]{1,0:T(8,128)S(1)} collective-permute-done((f32[16,1152]{1,0:T(8,128)S(1)}, f32[16,1152]{1,0:T(8,128)S(1)}, u32[]{:S(2)}, u32[]{:S(2)}) %collective-permute-start.5) | collective-permute-done | bytes 73760 | tf_op jit(solution)/shard_map/ppermute | solution.py:30
  62.7 5.6 %collective-permute-start.6 = (f32[16,1152]{1,0:T(8,128)S(1)}, f32[16,1152]{1,0:T(8,128)S(1)}, u32[]{:S(2)}, u32[]{:S(2)}) collective-permute-start(f32[16,1152]{1,0:T(8,128)S(1)} %add.49), channel_id=1, source_target_pairs={{0,8},{2,10},{4,12},{6,14},{8,0},{10,2},{12,4},{14,6},{1,9},{3,11}... | collective-permute-start | bytes 221192 | tf_op jit(solution)/shard_map/ppermute | solution.py:30
  68.2 3.4 %collective-permute-done.6 = f32[16,1152]{1,0:T(8,128)S(1)} collective-permute-done((f32[16,1152]{1,0:T(8,128)S(1)}, f32[16,1152]{1,0:T(8,128)S(1)}, u32[]{:S(2)}, u32[]{:S(2)}) %collective-permute-start.6) | collective-permute-done | bytes 73760 | tf_op jit(solution)/shard_map/ppermute | solution.py:30
  71.7 0.1 collective-permute-start.7
  71.8 6.4 %collective-permute-done.7 = f32[16,1152]{1,0:T(8,128)S(1)} collective-permute-done((f32[16,1152]{1,0:T(8,128)S(1)}, f32[16,1152]{1,0:T(8,128)S(1)}, u32[]{:S(2)}, u32[]{:S(2)}) %collective-permute-start.7) | collective-permute-done | bytes 73760 | tf_op jit(solution)/shard_map/ppermute | solution.py:30
  78.2 1.1 broadcast_in_dim.3
  79.3 3.6 %all-to-all-start.1 = ((f32[16,16,1152]{2,1,0:T(8,128)}), f32[16,16,1152]{2,1,0:T(8,128)S(1)}, u32[]{:S(2)}, u32[]{:S(2)}) async-start(f32[16,16,1152]{2,1,0:T(8,128)} %bitcast.8), calls=%async_computation.1 | async-start | bytes 2359296 | tf_op jit(solution)/shard_map/all_to_all | solution.py:261
  82.9 4.9 %collective-permute-start = (bf16[256,1024]{1,0:T(8,128)(2,1)S(1)}, bf16[256,1024]{1,0:T(8,128)(2,1)S(1)}, u32[]{:S(2)}, u32[]{:S(2)}) collective-permute-start(bf16[256,1024]{1,0:T(8,128)(2,1)S(1)} %copy-done.2), channel_id=1, source_target_pairs={{0,1},{1,0},{2,3},{3,2},{4,5},{5,4},{6,7},{7,6},{8,9},{9,8},{10,11... | collective-permute-start | bytes 1572872 | tf_op jit(solution)/shard_map/ppermute | solution.py:30
  87.8 1.5 %collective-permute-done = bf16[256,1024]{1,0:T(8,128)(2,1)S(1)} collective-permute-done((bf16[256,1024]{1,0:T(8,128)(2,1)S(1)}, bf16[256,1024]{1,0:T(8,128)(2,1)S(1)}, u32[]{:S(2)}, u32[]{:S(2)}) %collective-permute-start) | collective-permute-done | bytes 524320 | tf_op jit(solution)/shard_map/ppermute | solution.py:30
  89.4 0.0 copy-start.5
  89.4 1.1 fusion.pulled
  90.5 9.6 %collective-permute-done.8.refs_1_ = bf16[512,2048]{1,0:T(8,128)(2,1)} collective-permute-done((bf16[512,2048]{1,0:T(8,128)(2,1)}, bf16[512,2048]{1,0:T(8,128)(2,1)}, u32[]{:S(2)}, u32[]{:S(2)}) %collective-permute-start.8) | collective-permute-done | bytes 2097184 | tf_op jit(solution)/shard_map/ppermute | solution.py:34
  100.1 0.0 copy-done.5
  100.1 7.0 %shard_map.77 = (bf16[256,8192]{1,0:T(8,128)(2,1)}, bf16[256,2048]{1,0:T(8,128)(2,1)}) custom-call(s32[2]{0:T(128)} %copy-done.4, bf16[512,1024]{1,0:T(8,128)(2,1)} %copy-done.5, bf16[512,64]{1,0:T(8,128)(2,1)} %fusion.pulled, bf16[64,8192]{1,0:T(8,128)(2,1)} %bitcast.19, bf16[512,2048]{1,0:T(8,128)(2,1)} %all-gather.4.cloned.1.call-done.refs_0_, ...), custom_call_target="tpu_custom_call" | custom-call | tf_op jit(solution)/shard_map/pallas_call | solution.py:67
  107.1 0.0 all-to-all-done.1.piece
  107.1 4.0 %collective-permute-start.12 = (f32[16,16,1152]{2,1,0:T(8,128)S(1)}, f32[16,16,1152]{2,1,0:T(8,128)S(1)}, u32[]{:S(2)}, u32[]{:S(2)}) collective-permute-start(f32[16,16,1152]{2,1,0:T(8,128)S(1)} %all-to-all-done.1.piece), channel_id=1, source_target_pairs={{0,1},{1,0},{2,3},{3,2},{4,5},{5,4},{6,7},{7,6},{8,9},{9,8},{10,11... | collective-permute-start | bytes 3538952 | tf_op jit(solution)/shard_map/ppermute | solution.py:30
  111.1 1.3 shard_map.78
  112.4 0.1 collective-permute-start.11
  112.5 1.7 %all-gather.6.cloned.1.call-done = bf16[16,64,2048]{2,1,0:T(8,128)(2,1)} async-done(((bf16[2,64,2048]{2,1,0:T(8,128)(2,1)}), bf16[16,64,2048]{2,1,0:T(8,128)(2,1)}) %all-gather.6.cloned.1.call-update) | async-done | bytes 4194320 | tf_op jit(solution)/shard_map/all_gather | solution.py:250
  114.2 6.7 %shard_map.79 = (bf16[256,8192]{1,0:T(8,128)(2,1)}, bf16[256,2048]{1,0:T(8,128)(2,1)}) custom-call(s32[2]{0:T(128)} %copy-done.4, bf16[512,1024]{1,0:T(8,128)(2,1)} %copy-done.5, bf16[512,64]{1,0:T(8,128)(2,1)} %fusion.pulled, bf16[64,8192]{1,0:T(8,128)(2,1)} %bitcast.20, bf16[8,2,64,2048]{3,2,1,0:T(8,128)(2,1)} %bitcast.23, ...), custom_call_target="tpu_custom_call", output_to_operand_aliasing={{0}: (5, {})} | custom-call | tf_op jit(solution)/shard_map/pallas_call | solution.py:67
  120.8 0.5 collective-permute-start.10
  121.3 0.0 collective-permute-done.12.piece
  121.3 1.3 shard_map.82
  122.6 0.0 collective-permute-done.11.piece
  122.7 1.0 shard_map.80._
  123.7 0.2 collective-permute-done.10.piece
  123.8 1.0 shard_map.81
  (11 shorter events, 0.3 us)
Async XLA Ops:
  7.2 6.6 %copy-start = (bf16[8192,64]{0,1:T(8,128)(2,1)S(1)}, bf16[8192,64]{0,1:T(8,128)(2,1)}, u32[]{:S(2)}) copy-start(bf16[8192,64]{0,1:T(8,128)(2,1)} %param.8) | copy-start | bytes 3145732
  7.2 6.5 %copy-start.2 = (bf16[256,1024]{1,0:T(8,128)(2,1)S(1)}, bf16[256,1024]{1,0:T(8,128)(2,1)}, u32[]{:S(2)}) copy-start(bf16[256,1024]{1,0:T(8,128)(2,1)} %vg_ref.1) | copy-start | bytes 1572868
  7.2 6.5 %copy-start.3 = (bf16[64,1024]{1,0:T(8,128)(2,1)S(1)}, bf16[64,1024]{1,0:T(8,128)(2,1)}, u32[]{:S(2)}) copy-start(bf16[64,1024]{1,0:T(8,128)(2,1)} %up_ref.1) | copy-start | bytes 393220
  7.2 47.1 %all-gather.4.cloned.1.call-start = ((), (), s32[]{:S(2)}) async-start(), calls=%async_computation.2 | async-start | bytes 2359296 | tf_op jit(solution)/shard_map/all_gather | solution.py:245
  8.3 4.5 %collective-permute-start.1 = (bf16[32,4096]{1,0:T(8,128)(2,1)S(1)}, bf16[32,4096]{1,0:T(8,128)(2,1)S(1)}, u32[]{:S(2)}, u32[]{:S(2)}) collective-permute-start(bf16[32,4096]{1,0:T(8,128)(2,1)S(1)} %constant_dynamic-slice_fusion.1), channel_id=1, source_target_pairs={{0,1},{1,0},{2,3},{3,2},{4,5},{5,4},{6,7},{7,6},{8,9},{9,8},{10,11... | collective-permute-start | bytes 786440 | tf_op jit(solution)/shard_map/ppermute | solution.py:30
  13.7 6.7 %copy-start.4 = (s32[2]{0:T(128)}, s32[2]{0:T(128)S(1)}, u32[]{:S(2)}) copy-start(s32[2]{0:T(128)S(1)} %pad_add_fusion.core_ref.at_ref) | copy-start | bytes 28
  13.7 2.2 %copy-start.1 = (bf16[256,8192]{1,0:T(8,128)(2,1)S(1)}, bf16[256,8192]{1,0:T(8,128)(2,1)}, u32[]{:S(2)}) copy-start(bf16[256,8192]{1,0:T(8,128)(2,1)} %li_ref) | copy-start | bytes 12582916
  20.4 2.9 %collective-permute-start.2 = (f32[16,16,1152]{2,1,0:T(8,128)S(1)}, f32[16,16,1152]{2,1,0:T(8,128)S(1)}, u32[]{:S(2)}, u32[]{:S(2)}) collective-permute-start(f32[16,16,1152]{2,1,0:T(8,128)S(1)} %get-tuple-element.20), channel_id=1, source_target_pairs={{0,1},{1,0},{2,3},{3,2},{4,5},{5,4},{6,7},{7,6},{8,9},{9,8},{10,11... | collective-permute-start | bytes 3538952 | tf_op jit(solution)/shard_map/ppermute | solution.py:30
  24.5 20.0 %all-to-all-start = ((f32[16,16,1152]{2,1,0:T(8,128)}), f32[16,16,1152]{2,1,0:T(8,128)S(1)}, u32[]{:S(2)}, u32[]{:S(2)}) async-start(f32[16,16,1152]{2,1,0:T(8,128)} %add.42), calls=%async_computation | async-start | bytes 2359296 | tf_op jit(solution)/shard_map/all_to_all | solution.py:241
  28.1 86.0 %all-gather.6.cloned.1.call-start = ((), (), s32[]{:S(2)}) async-start(), calls=%async_computation.3 | async-start | bytes 4718592 | tf_op jit(solution)/shard_map/all_gather | solution.py:250
  28.2 24.3 %collective-permute-start.9 = (bf16[64,2048]{1,0:T(8,128)(2,1)S(1)}, bf16[64,2048]{1,0:T(8,128)(2,1)S(1)}, u32[]{:S(2)}, u32[]{:S(2)}) collective-permute-start(bf16[64,2048]{1,0:T(8,128)(2,1)S(1)} %maximum_select_fusion.2), channel_id=1, source_target_pairs={{0,144},{144,0},{16,128},{128,16},{1,145},{145,1},{17,129},{129,17... | collective-permute-start | bytes 786440 | tf_op jit(solution)/shard_map/ppermute | solution.py:34
  44.6 4.8 %collective-permute-start.3 = (f32[16,1152]{1,0:T(8,128)S(1)}, f32[16,1152]{1,0:T(8,128)S(1)}, u32[]{:S(2)}, u32[]{:S(2)}) collective-permute-start(f32[16,1152]{1,0:T(8,128)S(1)} %dynamic-slice_bitcast_fusion), channel_id=1, source_target_pairs={{0,2},{2,0},{4,6},{6,4},{8,10},{10,8},{12,14},{14,12},{1,3},{3,1},... | collective-permute-start | bytes 221192 | tf_op jit(solution)/shard_map/ppermute | solution.py:30
  49.4 4.8 %collective-permute-start.4 = (f32[16,1152]{1,0:T(8,128)S(1)}, f32[16,1152]{1,0:T(8,128)S(1)}, u32[]{:S(2)}, u32[]{:S(2)}) collective-permute-start(f32[16,1152]{1,0:T(8,128)S(1)} %bitcast_add_fusion), channel_id=1, source_target_pairs={{0,16},{16,0},{1,17},{17,1},{2,18},{18,2},{3,19},{19,3},{4,20},{20... | collective-permute-start | bytes 221192 | tf_op jit(solution)/shard_map/ppermute | solution.py:30
  54.3 45.7 %collective-permute-start.8 = (bf16[512,2048]{1,0:T(8,128)(2,1)}, bf16[512,2048]{1,0:T(8,128)(2,1)}, u32[]{:S(2)}, u32[]{:S(2)}) collective-permute-start(bf16[512,2048]{1,0:T(8,128)(2,1)} %all-gather.4.cloned.1.call-done.refs_0_), channel_id=1, source_target_pairs={{0,144},{144,0},{16,128},{128,16},{1,145},{145,1},{17,129},{129,17... | collective-permute-start | bytes 6291464 | tf_op jit(solution)/shard_map/ppermute | solution.py:34
  56.8 5.8 %collective-permute-start.5 = (f32[16,1152]{1,0:T(8,128)S(1)}, f32[16,1152]{1,0:T(8,128)S(1)}, u32[]{:S(2)}, u32[]{:S(2)}) collective-permute-start(f32[16,1152]{1,0:T(8,128)S(1)} %add.48), channel_id=1, source_target_pairs={{0,4},{2,6},{4,0},{6,2},{8,12},{10,14},{12,8},{14,10},{1,5},{3,7},... | collective-permute-start | bytes 221192 | tf_op jit(solution)/shard_map/ppermute | solution.py:30
  62.7 9.0 %collective-permute-start.6 = (f32[16,1152]{1,0:T(8,128)S(1)}, f32[16,1152]{1,0:T(8,128)S(1)}, u32[]{:S(2)}, u32[]{:S(2)}) collective-permute-start(f32[16,1152]{1,0:T(8,128)S(1)} %add.49), channel_id=1, source_target_pairs={{0,8},{2,10},{4,12},{6,14},{8,0},{10,2},{12,4},{14,6},{1,9},{3,11}... | collective-permute-start | bytes 221192 | tf_op jit(solution)/shard_map/ppermute | solution.py:30
  71.7 6.5 %collective-permute-start.7 = (f32[16,1152]{1,0:T(8,128)S(1)}, f32[16,1152]{1,0:T(8,128)S(1)}, u32[]{:S(2)}, u32[]{:S(2)}) collective-permute-start(f32[16,1152]{1,0:T(8,128)S(1)} %add.50), channel_id=1, source_target_pairs={{0,2},{2,0},{4,6},{6,4},{8,10},{10,8},{12,14},{14,12},{1,3},{3,1},... | collective-permute-start | bytes 221192 | tf_op jit(solution)/shard_map/ppermute | solution.py:30
  79.3 27.8 %all-to-all-start.1 = ((f32[16,16,1152]{2,1,0:T(8,128)}), f32[16,16,1152]{2,1,0:T(8,128)S(1)}, u32[]{:S(2)}, u32[]{:S(2)}) async-start(f32[16,16,1152]{2,1,0:T(8,128)} %bitcast.8), calls=%async_computation.1 | async-start | bytes 2359296 | tf_op jit(solution)/shard_map/all_to_all | solution.py:261
  82.9 6.4 %collective-permute-start = (bf16[256,1024]{1,0:T(8,128)(2,1)S(1)}, bf16[256,1024]{1,0:T(8,128)(2,1)S(1)}, u32[]{:S(2)}, u32[]{:S(2)}) collective-permute-start(bf16[256,1024]{1,0:T(8,128)(2,1)S(1)} %copy-done.2), channel_id=1, source_target_pairs={{0,1},{1,0},{2,3},{3,2},{4,5},{5,4},{6,7},{7,6},{8,9},{9,8},{10,11... | collective-permute-start | bytes 1572872 | tf_op jit(solution)/shard_map/ppermute | solution.py:30
  89.4 10.7 %copy-start.5 = (bf16[512,1024]{1,0:T(8,128)(2,1)}, bf16[512,1024]{1,0:T(8,128)(2,1)S(1)}, u32[]{:S(2)}) copy-start(bf16[512,1024]{1,0:T(8,128)(2,1)S(1)} %constant_dynamic-update-slice_fusion.grads) | copy-start | bytes 3145732
  107.1 14.3 %collective-permute-start.12 = (f32[16,16,1152]{2,1,0:T(8,128)S(1)}, f32[16,16,1152]{2,1,0:T(8,128)S(1)}, u32[]{:S(2)}, u32[]{:S(2)}) collective-permute-start(f32[16,16,1152]{2,1,0:T(8,128)S(1)} %all-to-all-done.1.piece), channel_id=1, source_target_pairs={{0,1},{1,0},{2,3},{3,2},{4,5},{5,4},{6,7},{7,6},{8,9},{9,8},{10,11... | collective-permute-start | bytes 3538952 | tf_op jit(solution)/shard_map/ppermute | solution.py:30
  112.4 10.3 %collective-permute-start.11 = (bf16[256,2048]{1,0:T(8,128)(2,1)}, bf16[256,2048]{1,0:T(8,128)(2,1)S(1)}, u32[]{:S(2)}, u32[]{:S(2)}) collective-permute-start(bf16[256,2048]{1,0:T(8,128)(2,1)} %get-tuple-element.22), channel_id=1, source_target_pairs={{0,1},{1,0},{2,3},{3,2},{4,5},{5,4},{6,7},{7,6},{8,9},{9,8},{10,11... | collective-permute-start | bytes 3145736 | tf_op jit(solution)/shard_map/ppermute | solution.py:30
  120.8 3.0 %collective-permute-start.10 = (bf16[256,2048]{1,0:T(8,128)(2,1)}, bf16[256,2048]{1,0:T(8,128)(2,1)S(1)}, u32[]{:S(2)}, u32[]{:S(2)}) collective-permute-start(bf16[256,2048]{1,0:T(8,128)(2,1)} %get-tuple-element.29), channel_id=1, source_target_pairs={{0,1},{1,0},{2,3},{3,2},{4,5},{5,4},{6,7},{7,6},{8,9},{9,8},{10,11... | collective-permute-start | bytes 3145736 | tf_op jit(solution)/shard_map/ppermute | solution.py:30
Sparse Core Ops, SparseCore 0:
  13.8 39.1 all-gather.3
  54.8 59.3 all-gather.5
